TPU v7x, 32 devices: a whole 2x2x4 slice. The times are simulated.
32 devices in a mesh: dp: 16 (over z, x, core), mp: 2 (over y).
Axes of the slice: x: 2, y: 2, z: 4, core: 2. Of those that a mesh axis runs over, the one named last changes fastest.
Arguments:
- hidden_in: bfloat16 [32768, 1024], P(('dp', 'mp')), may hold values from -6 to 6
- query_weight: bfloat16 [1024, 1024], replicated, may hold values from -0.1875 to 0.1875
- key_weight: bfloat16 [1024, 1024], replicated, may hold values from -0.1875 to 0.1875
- value_weight: bfloat16 [1024, 1024], replicated, may hold values from -0.1875 to 0.1875
- select_weight: bfloat16 [1024, 1024], replicated, may hold values from -0.1875 to 0.1875
- out_weight: bfloat16 [1024, 1024], replicated, may hold values from -0.1875 to 0.1875
- first_weight: bfloat16 [1024, 2816], P(None, 'mp'), may hold values from -0.1875 to 0.1875
- second_weight: bfloat16 [1024, 2816], P(None, 'mp'), may hold values from -0.1875 to 0.1875
- down_weight: bfloat16 [2816, 1024], P('mp'), may hold values from -0.109375 to 0.109375
- decay_slope: float32 [8], replicated, may hold values from 0.00012207031 to 0.5
- doc_lengths: int32 [16, 3], P('dp'), may hold values from 384 to 1024, as said below
- cotangent: bfloat16 [32768, 1024], P(('dp', 'mp')), may hold values from -6 to 6
Outputs:
- output: bfloat16 [32768, 1024], P(('dp', 'mp'))
- grad_hidden: bfloat16 [32768, 1024], P(('dp', 'mp'))
- grad_query: float32 [1024, 1024], P('dp', 'mp')
- grad_key: float32 [1024, 1024], P('dp', 'mp')
- grad_value: float32 [1024, 1024], P('dp', 'mp')
- grad_select: float32 [1024, 1024], P('dp', 'mp')
- grad_out: float32 [1024, 1024], P('dp', 'mp')
- grad_first: float32 [1024, 2816], P('dp', 'mp')
- grad_second: float32 [1024, 2816], P('dp', 'mp')
- grad_down: float32 [2816, 1024], P('mp', 'dp')
Inputs may be any that keep to these rules, and one draw needn't show every extreme that they name: `doc_lengths`: row g gives the lengths of the 3 documents packed in order from the first of the group's 2048 rows; the rows after them are padding. Two of the documents have 2048 // 4 tokens and one has 1024, which one is drawn; the last document gives up 0 to 128 of its tokens to padding.
All inputs are finite; a program needn't handle non-finite values.
Results may differ from a plain program's by a relative error of at most 0.019.
Values may be sent and summed in bfloat16 or wider, within the bound.
A program may use at most 320 MiB of HBM per device.

v0:
```python
import functools

import jax
import jax.numpy as jnp
import numpy as np
from jax import lax
from jax.experimental import pallas as pl
from jax.experimental.pallas import tpu as pltpu
from jax.sharding import PartitionSpec as P

HEAD = 128
CHUNK = 256
EPSILON = 1e-06
BF16 = jnp.bfloat16
F32 = jnp.float32
VMEM_LIMIT = 58 * 1024 * 1024


def nn(left, right):
    return jnp.dot(left, right, preferred_element_type=F32)


def nt(left, right):
    return lax.dot_general(left, right, (((1,), (1,)), ((), ())), preferred_element_type=F32)


def scale_of(values):
    return lax.rsqrt(jnp.mean(values * values, axis=-1, keepdims=True) + EPSILON)


def norm_back(values, scale, upstream):
    return scale * upstream - values * (scale * scale * scale) * jnp.mean(
        values * upstream, axis=-1, keepdims=True
    )


def sigmoid(v):
    return 1.0 / (1.0 + jnp.exp(-v))


def featured(pre, cos, sin):
    act = pre * sigmoid(pre)
    return jnp.concatenate([act * cos, act * sin], axis=-1).astype(BF16)


def head_slice(h):
    return slice(h * HEAD, (h + 1) * HEAD)


def row_index(shape):
    return lax.broadcasted_iota(jnp.int32, shape, 0)


def fade_from_start(slope, width):
    return jnp.exp(-slope * (row_index((CHUNK, width)) + 1).astype(F32))


def fade_to_end(slope, width):
    return jnp.exp(-slope * (CHUNK - 1 - row_index((CHUNK, width))).astype(F32))


def decay_table(slope, transposed):
    rows = lax.broadcasted_iota(jnp.int32, (CHUNK, CHUNK), 0)
    cols = lax.broadcasted_iota(jnp.int32, (CHUNK, CHUNK), 1)
    gap = cols - rows if transposed else rows - cols
    return jnp.where(gap >= 0, jnp.exp(-slope * jnp.maximum(gap, 0).astype(F32)), 0.0)


def plus(*arrays):
    total = arrays[0].astype(F32)
    for a in arrays[1:]:
        total = total + a.astype(F32)
    return total


def smem():
    return pl.BlockSpec(memory_space=pltpu.SMEM)


def anywhere():
    return pl.BlockSpec(memory_space=pl.ANY)


def once(shape):
    zeros = (0,) * len(shape)
    return pl.BlockSpec(shape, lambda *_: zeros, pipeline_mode=pl.Buffered(1))


def whole_block(shape):
    zeros = (0,) * len(shape)
    return pl.BlockSpec(shape, lambda *_: zeros)


def cost(flops, arrays):
    moved = sum(int(np.prod(a.shape)) * jnp.dtype(a.dtype).itemsize for a in arrays)
    return pl.CostEstimate(flops=int(flops), bytes_accessed=moved, transcendentals=0)


def struct(shape, dtype=BF16):
    return jax.ShapeDtypeStruct(tuple(shape), dtype)


def flipped(index, mask):
    bit = 1
    while bit <= mask:
        if mask & bit:
            index = index + bit * (1 - 2 * lax.rem(lax.div(index, bit), 2))
        bit *= 2
    return index


def remote(src, dst, send, recv, axis, mask):
    return pltpu.make_async_remote_copy(
        src_ref=src,
        dst_ref=dst,
        send_sem=send,
        recv_sem=recv,
        device_id={axis: flipped(lax.axis_index(axis), mask)},
        device_id_type=pl.DeviceIdType.MESH,
    )


def greet(partners):
    barrier = pltpu.get_barrier_semaphore()
    for axis, mask in partners:
        pl.semaphore_signal(
            barrier,
            inc=1,
            device_id={axis: flipped(lax.axis_index(axis), mask)},
            device_id_type=pl.DeviceIdType.MESH,
        )
    pl.semaphore_wait(barrier, len(partners))


class Carry:
    def __init__(self, inputs, outs, phases):
        self.inputs, self.outs, self.phases = list(inputs), list(outs), phases
        count = sum(len(p[2]) for p in phases)
        self.scratch = [pltpu.SemaphoreType.DMA((count,)), pltpu.SemaphoreType.DMA((count,))]
        self.partners = [(c[2], c[3]) for p in phases for c in p[2]]

    def copies(self, which, ins, outs, scratch):
        at = sum(len(p[2]) for p in self.phases[:which])
        send, recv = scratch
        for k, (src, dst, axis, mask) in enumerate(self.phases[which][2]):
            yield remote(src(ins, outs), dst(ins, outs), send.at[at + k], recv.at[at + k], axis, mask)

    def before(self, step, ins, outs, scratch):
        for p, phase in enumerate(self.phases):

            @pl.when(step == phase[0])
            def _(p=p):
                for copy in self.copies(p, ins, outs, scratch):
                    copy.start()

    def after(self, step, ins, outs, scratch):
        for p, phase in enumerate(self.phases):

            @pl.when(step == phase[1])
            def _(p=p):
                for copy in self.copies(p, ins, outs, scratch):
                    copy.wait()


class Reducer:
    KINDS = 8

    def __init__(self, start, blocks, items, depth, rows, delays):
        self.start, self.blocks, self.items = start, blocks, items
        self.depth, self.rows, self.delays = depth, rows, delays
        half, n, wide = depth // 2, 2 * depth * rows, 2 * HEAD
        buf = lambda *shape: pltpu.VMEM(shape, BF16)
        pair = (half, items, rows, wide)
        flat = (2, half, items, rows, HEAD)
        one = (half, items, rows, HEAD)
        self.scratch = [
            buf(2, items, n, wide),
            buf(2, items, n, wide),
            buf(4, items, n, wide),
            buf(2, *pair),
            buf(2, *pair),
            buf(blocks, *pair),
            buf(2, *flat),
            buf(2, *flat),
            buf(blocks, *flat),
            buf(2, *one),
            buf(2, *one),
            buf(blocks, *one),
            buf(2, *one),
            buf(2, *one),
            buf(blocks, *one),
            buf(2, depth, items, rows, HEAD),
            buf(blocks, depth - 1, items, rows, HEAD),
            pltpu.SemaphoreType.DMA((self.KINDS, blocks)),
            pltpu.SemaphoreType.DMA((self.KINDS, blocks)),
        ]
        self.partners = [("dp", 1), ("dp", 2), ("mp", 1)] + [("dp", 4 * k) for k in range(1, depth)]
        self.last = start + blocks - 1 + delays[3]

    def bind(self, scratch):
        self.refs = scratch
        self.given, self.kept = scratch[:2]
        self.x = lax.rem(lax.div(lax.axis_index("dp"), 2), 2)
        self.z = lax.div(lax.axis_index("dp"), 4)

    def copies(self, stage, j):
        (given, kept, got, ps, pk, pr, qs, qk, qr, ps2, pk2, pr2, qs2, qk2, qr2, line, zr, send, recv) = self.refs
        slot = lax.rem(j, 2)
        if stage == 0:
            plan = [(0, given.at[slot], got.at[lax.rem(j, 4)], "dp", 1)]
        elif stage == 1:
            plan = [(1, ps.at[slot], pr.at[j], "dp", 2), (2, qs.at[slot], qr.at[j], "mp", 1)]
        elif stage == 2:
            plan = [(3, ps2.at[slot], pr2.at[j], "mp", 1), (4, qs2.at[slot], qr2.at[j], "dp", 2)]
        else:
            plan = [
                (4 + k, line.at[slot, flipped(self.z, k)], zr.at[j, k - 1], "dp", 4 * k)
                for k in range(1, self.depth)
            ]
        return [remote(src, dst, send.at[i, j], recv.at[i, j], axis, mask) for i, src, dst, axis, mask in plan]

    def begin(self, j):
        for copy in self.copies(0, j):
            copy.start()

    def run(self, step, out):
        for stage in (4, 3, 2, 1):
            j = step - self.start - self.delays[stage - 1]

            @pl.when(jnp.logical_and(j >= 0, j < self.blocks))
            def _(stage=stage, j=j):
                for copy in self.copies(stage - 1, j):
                    copy.wait()
                self.add(stage, j, out)
                if stage < 4:
                    for copy in self.copies(stage, j):
                        copy.start()

    def add(self, stage, j, out):
        (given, kept, got, ps, pk, pr, qs, qk, qr, ps2, pk2, pr2, qs2, qk2, qr2, line, zr, send, recv) = self.refs
        slot, x, rows = lax.rem(j, 2), self.x, self.rows
        half = self.depth // 2
        if stage == 1:
            four = lax.rem(j, 4)

            def total(t, z, at):
                here = pl.ds(pl.multiple_of((2 * z + at) * rows, rows), rows)
                return plus(kept[slot, t, here, :], got[four, t, here, :]).astype(BF16)

            for z in range(half):
                for t in range(self.items):
                    ps[slot, z, t] = total(t, z, 1 - x)
                    pk[slot, z, t] = total(t, z, x)
                    for at in range(2):
                        block = total(t, half + z, at)
                        qk[slot, at, z, t] = block[:, :HEAD]
                        qs[slot, at, z, t] = block[:, HEAD:]
        elif stage == 2:
            for z in range(half):
                block = plus(pk[slot, z], pr[j, z]).astype(BF16)
                pk2[slot, z] = block[:, :, :HEAD]
                ps2[slot, z] = block[:, :, HEAD:]
                qs2[slot, z] = plus(qk[slot, 1 - x, z], qr[j, 1 - x, z]).astype(BF16)
                qk2[slot, z] = plus(qk[slot, x, z], qr[j, x, z]).astype(BF16)
        elif stage == 3:
            for z in range(half):
                line[slot, z] = plus(pk2[slot, z], pr2[j, z]).astype(BF16)
                line[slot, half + z] = plus(qk2[slot, z], qr2[j, z]).astype(BF16)
        else:
            total = plus(line[slot, self.z], *[zr[j, k] for k in range(self.depth - 1)])
            out[:, :, pl.ds(pl.multiple_of(j * HEAD, HEAD), HEAD)] = total


def launch(kernel, name, steps, inputs, specs, outs, out_specs, scratch, flops, guests=(), ident=None, partners=()):
    guests = list(guests)
    partners = list(partners) + [p for g in guests for p in g.partners]
    partners = sorted(set(partners))
    all_inputs = list(inputs) + [a for g in guests for a in g.inputs]
    all_specs = list(specs) + [anywhere() for g in guests for _ in g.inputs]
    all_outs = list(outs) + [a for g in guests for a in g.outs]
    all_out_specs = list(out_specs) + [anywhere() for g in guests for _ in g.outs]
    all_scratch = list(scratch) + [a for g in guests for a in g.scratch]

    def body(*refs):
        refs = list(refs)
        take = lambda k: [refs.pop(0) for _ in range(k)]
        own = take(len(inputs))
        ins = [take(len(g.inputs)) for g in guests]
        own += take(len(outs))
        gone = [take(len(g.outs)) for g in guests]
        own += take(len(scratch))
        held = [take(len(g.scratch)) for g in guests]
        step = pl.program_id(0)
        if partners:

            @pl.when(step == 0)
            def _():
                greet(partners)

        for g, i, o, s in zip(guests, ins, gone, held):
            g.before(step, i, o, s)
        kernel(*own)
        for g, i, o, s in zip(guests, ins, gone, held):
            g.after(step, i, o, s)

    extra = dict(collective_id=ident, has_side_effects=True) if partners else {}
    return pl.pallas_call(
        body,
        grid=(steps,),
        in_specs=all_specs,
        out_specs=all_out_specs,
        out_shape=all_outs,
        scratch_shapes=all_scratch,
        compiler_params=pltpu.CompilerParams(
            vmem_limit_bytes=VMEM_LIMIT, dimension_semantics=("arbitrary",), **extra
        ),
        cost_estimate=cost(flops, all_inputs + all_outs),
        name=name,
    )(*all_inputs)


def chunk_info(lengths, me, peers, count):
    chunks = count // CHUNK
    offset = me * count
    first = offset + CHUNK * jnp.arange(chunks, dtype=jnp.int32)
    begin, start = jnp.zeros_like(first), jnp.int32(0)
    for i in range(lengths.shape[0]):
        begin = jnp.where(first >= start, start, begin)
        start = start + lengths[i]
    base = first - begin
    keep = (base > 0).astype(jnp.int32)
    before = (begin < offset).astype(jnp.int32)
    after = ((begin[-1] <= first) & (me < peers - 1)).astype(jnp.int32)
    live = jnp.clip(start - offset, 0, count)
    return jnp.concatenate([base, keep, before, after, live[None]]).astype(jnp.int32)


def turning(info, chunks, longest):
    freq = 10000.0 ** (-np.arange(HEAD, dtype=np.float64) / HEAD)
    phase = np.arange(longest, dtype=np.float64)[:, None] * freq[None, :]
    table = jnp.asarray(np.concatenate([np.cos(phase), np.sin(phase)], axis=1), F32)
    return jnp.concatenate(
        [lax.dynamic_slice(table, (info[c], 0), (CHUNK, 2 * HEAD)) for c in range(chunks)], axis=0
    )


def keys_kernel(chunks, heads, info, slopes, hid, wk, wv, rot, normed_o, turned_o, kpre_o, val_o, st_o, fin_o, state):
    c = pl.program_id(0)

    @pl.when(c == 0)
    def _():
        state[...] = jnp.zeros_like(state)

    x = hid[...].astype(F32)
    normed = (x * scale_of(x)).astype(BF16)
    normed_o[...] = normed
    turned_o[...] = normed.T.reshape(turned_o.shape)
    kpre = nn(normed, wk[...])
    kpre_o[...] = kpre.astype(BF16)
    values = nn(normed, wv[...])
    val_o[...] = values.astype(BF16)
    cs, sn = rot[:, :HEAD], rot[:, HEAD:]
    keep = info[chunks + c].astype(F32)
    for h in range(heads):
        slope = slopes[h]
        key = featured(kpre[:, head_slice(h)], cs, sn)
        faded = (values[:, head_slice(h)] * fade_to_end(slope, HEAD)).astype(BF16)
        old = state[h] * keep
        st_o[0, h] = old.astype(BF16)
        state[h] = jnp.exp(jnp.full((1, 2 * HEAD), -slope * CHUNK, F32)) * old + nn(faded.T, key)
    fin_o[...] = state[...].astype(BF16)


def run_keys(info, slopes, hidden, wk, wv, rot, parts, **ride):
    n, d = hidden.shape
    heads, chunks = d // HEAD, n // CHUNK
    turned = (parts // 2, 2, d // parts, n)
    tile = pl.BlockSpec((CHUNK, d), lambda c: (c, 0))
    outs = [
        struct((n, d)),
        struct(turned),
        struct((n, d)),
        struct((n, d)),
        struct((chunks, heads, HEAD, 2 * HEAD)),
        struct((heads, HEAD, 2 * HEAD)),
    ]
    return launch(
        functools.partial(keys_kernel, chunks, heads),
        "keys_values_states",
        chunks,
        [info, slopes, hidden, wk, wv, rot],
        [smem(), smem(), tile, whole_block(wk.shape), whole_block(wv.shape), pl.BlockSpec((CHUNK, 2 * HEAD), lambda c: (c, 0))],
        outs,
        [
            tile,
            pl.BlockSpec(turned[:3] + (CHUNK,), lambda c: (0, 0, 0, c)),
            tile,
            tile,
            pl.BlockSpec((1, heads, HEAD, 2 * HEAD), lambda c: (c, 0, 0, 0)),
            whole_block((heads, HEAD, 2 * HEAD)),
        ],
        [pltpu.VMEM((heads, HEAD, 2 * HEAD), F32)],
        4 * n * d * d,
        **ride,
    )


def inside_kernel(chunks, heads, info, slopes, normed, wq, ws, kpre, values, st, rot, qpre_o, sel_o, att_o):
    c = pl.program_id(0)
    x = normed[...]
    qpre = nn(x, wq[...])
    qpre_o[...] = qpre.astype(BF16)
    sel_o[...] = nn(x, ws[...]).astype(BF16)
    cs, sn = rot[:, :HEAD], rot[:, HEAD:]
    for h in range(heads):
        slope = slopes[h]
        query = featured(qpre[:, head_slice(h)], cs, sn)
        key = featured(kpre[:, head_slice(h)].astype(F32), cs, sn)
        weights = (nt(query, key) * decay_table(slope, False)).astype(BF16)
        att_o[:, head_slice(h)] = nn(weights, values[:, head_slice(h)]) + fade_from_start(
            slope, HEAD
        ) * nt(query, st[0, h])


def run_inside(info, slopes, normed, wq, ws, kpre, values, st, rot, **ride):
    n, d = normed.shape
    heads, chunks = d // HEAD, n // CHUNK
    tile = pl.BlockSpec((CHUNK, d), lambda c: (c, 0))
    outs = [struct((n, d)), struct((n, d)), struct((n, d), F32)]
    return launch(
        functools.partial(inside_kernel, chunks, heads),
        "queries_attention",
        chunks,
        [info, slopes, normed, wq, ws, kpre, values, st, rot],
        [
            smem(),
            smem(),
            tile,
            whole_block(wq.shape),
            whole_block(ws.shape),
            tile,
            tile,
            pl.BlockSpec((1, heads, HEAD, 2 * HEAD), lambda c: (c, 0, 0, 0)),
            pl.BlockSpec((CHUNK, 2 * HEAD), lambda c: (c, 0)),
        ],
        outs,
        [tile, tile, tile],
        [],
        6 * n * d * d,
        **ride,
    )


def mix_kernel(chunks, heads, info, slopes, att, qpre, came, sel, wo, hid, cot, rot, att_o, mixt_o, mid_o, sec_o, sect_o, cott_o, total):
    c = pl.program_id(0)
    cs, sn = rot[:, :HEAD], rot[:, HEAD:]
    reached = info[2 * chunks + c].astype(F32)
    lag = (c * CHUNK).astype(F32)
    alive = (row_index((CHUNK, HEAD)) + c * CHUNK < info[4 * chunks]).astype(F32)
    for h in range(heads):
        slope = slopes[h]
        query = featured(qpre[:, head_slice(h)].astype(F32), cs, sn)
        fade = jnp.exp(-slope * (row_index((CHUNK, HEAD)).astype(F32) + (lag + 1.0))) * reached
        total[:, head_slice(h)] = (att[:, head_slice(h)] + fade * nt(query, came[h])) * alive
    attended = total[...]
    att_o[...] = attended.astype(BF16)
    mixed = (attended * scale_of(attended) * sel[...].astype(F32)).astype(BF16)
    mixt_o[...] = mixed.T.reshape(mixt_o.shape)
    middle = hid[...].astype(F32) + nn(mixed, wo[...])
    mid_o[...] = middle
    second = (middle * scale_of(middle)).astype(BF16)
    sec_o[...] = second
    sect_o[...] = second.T.reshape(sect_o.shape)
    cott_o[...] = cot[...].T.reshape(cott_o.shape)


def run_mix(info, slopes, att, qpre, came, sel, wo, hidden, cot, rot, parts, **ride):
    n, d = hidden.shape
    heads, chunks = d // HEAD, n // CHUNK
    turned = (parts // 2, 2, d // parts, n)
    tile = pl.BlockSpec((CHUNK, d), lambda c: (c, 0))
    turned_tile = pl.BlockSpec(turned[:3] + (CHUNK,), lambda c: (0, 0, 0, c))
    outs = [
        struct((n, d)),
        struct(turned),
        struct((n, d), F32),
        struct((n, d)),
        struct(turned),
        struct(turned),
    ]
    return launch(
        functools.partial(mix_kernel, chunks, heads),
        "carried_mixed_middle",
        chunks,
        [info, slopes, att, qpre, came, sel, wo, hidden, cot, rot],
        [
            smem(),
            smem(),
            tile,
            tile,
            whole_block(came.shape),
            tile,
            whole_block(wo.shape),
            tile,
            tile,
            pl.BlockSpec((CHUNK, 2 * HEAD), lambda c: (c, 0)),
        ],
        outs,
        [tile, turned_tile, tile, tile, turned_tile, turned_tile],
        [pltpu.VMEM((CHUNK, d), F32)],
        3 * n * d * d,
        **ride,
    )


def sglu_kernel(chunks, peers, sec, cot, w1, w2, wd, units_o, term_o, part_o):
    step = pl.program_id(0)
    here = pl.ds(pl.multiple_of(lax.rem(step, chunks) * CHUNK, CHUNK), CHUNK)
    left = nn(sec[...], w1[...])
    right = nn(sec[...], w2[...])
    inner = (left * right).astype(BF16)
    upstream = nt(cot[...], wd[...])
    grad_left = (upstream * right).astype(BF16)
    grad_right = (upstream * left).astype(BF16)
    units_o[0] = grad_left
    units_o[1] = grad_right
    units_o[2] = inner
    term = nn(inner, wd[...])
    part = nt(grad_left, w1[...]) + nt(grad_right, w2[...])

    @pl.when(step < chunks)
    def _():
        term_o[here, :] = term
        part_o[here, :] = part

    @pl.when(step >= chunks)
    def _():
        term_o[here, :] += term
        part_o[here, :] += part


def run_sglu(second, cot, w1, w2, wd):
    n, d = second.shape
    peers, _, width = w1.shape
    chunks = n // CHUNK
    tile = pl.BlockSpec((CHUNK, d), lambda s: (lax.rem(s, chunks), 0))
    block = lambda shape: pl.BlockSpec((None,) + shape, lambda s: (lax.div(s, chunks), 0, 0))
    return launch(
        functools.partial(sglu_kernel, chunks, peers),
        "sglu",
        peers * chunks,
        [second, cot, w1, w2, wd],
        [tile, tile, block((d, width)), block((d, width)), block((width, d))],
        [struct((3, peers, n, width)), struct((n, d), F32), struct((n, d), F32)],
        [
            pl.BlockSpec((3, None, CHUNK, width), lambda s: (0, lax.div(s, chunks), lax.rem(s, chunks), 0)),
            whole_block((n, d)),
            whole_block((n, d)),
        ],
        [],
        12 * n * d * width * peers,
    )


def units_kernel(geo, reducer, ride, first_weight, second_weight, down_weight, x, *refs):
    blocks, cut, d, units = geo["blocks"], geo["cut"], geo["d"], geo["units"]
    refs = list(refs)
    take = lambda k: [refs.pop(0) for _ in range(k)]
    cot_h, xt_h, cott_h = take(3)
    pieces = take(12)
    had_b = take(3)
    term_o, part_o, out = take(3)
    pieces = pieces + had_b + take(9)
    term, part, cot, xt, cott, o1, o2, od, c1, c2, cd, sems, out_sems = take(13)
    reducer.bind(take(len(reducer.scratch)))
    step = pl.program_id(0)
    ride.before(step, had_b, pieces[15:], refs)
    core = lax.rem(lax.axis_index("dp"), 2)
    eighth = lax.rem(lax.axis_index("dp"), 8)

    def fetch(g):
        size = cut if g == 0 else units - cut
        masks = [(0, None, 0), (3, 0, 2), (3, 1, 4), (3, 2, 1), (6, 0, 6), (6, 1, 3), (6, 2, 5), (9, None, 7)]
        copies = []
        for w, region in enumerate((o1, o2, od)):
            rows = d // 8 if w < 2 else size // 8
            for k, (at, inner, mask) in enumerate(masks):
                src = pieces[12 * g + at + w]
                src = src if inner is None else src.at[inner]
                here = pl.ds(pl.multiple_of(flipped(eighth, mask) * rows, 16), rows)
                dst = region.at[here, pl.ds(0, size)] if w < 2 else region.at[here, :]
                copies.append(pltpu.make_async_copy(src, dst, sems.at[g, w, k]))
        return copies

    own = [
        pltpu.make_async_copy(cot_h, cot, out_sems.at[2]),
        pltpu.make_async_copy(xt_h.at[:, 1 - core], xt.at[0], out_sems.at[3]),
        pltpu.make_async_copy(xt_h.at[:, core], xt.at[1], out_sems.at[4]),
        pltpu.make_async_copy(cott_h.at[:, 1 - core], cott.at[0], out_sems.at[5]),
        pltpu.make_async_copy(cott_h.at[:, core], cott.at[1], out_sems.at[6]),
    ]
    done = [
        pltpu.make_async_copy(term, term_o, out_sems.at[0]),
        pltpu.make_async_copy(part, part_o, out_sems.at[1]),
    ]
    turn = cut // HEAD

    @pl.when(step == 0)
    def _():
        for copy in fetch(0) + own:
            copy.start()
        term[...] = jnp.zeros_like(term)
        part[...] = jnp.zeros_like(part)
        for copy in fetch(0):
            copy.wait()

    @pl.when(step == turn)
    def _():
        for copy in fetch(1):
            copy.wait()

    @pl.when(step < blocks)
    def _():
        local = step - jnp.where(step >= turn, turn, 0)
        here = pl.ds(pl.multiple_of(local * HEAD, HEAD), HEAD)
        c1[:, :HEAD] = first_weight[...]
        c1[:, HEAD:] = o1[:, here]
        c2[:, :HEAD] = second_weight[...]
        c2[:, HEAD:] = o2[:, here]
        cd[:HEAD, :] = down_weight[...]
        cd[HEAD:, :] = od[here, :]

    @pl.when(step == turn - 1)
    def _():
        for copy in fetch(1):
            copy.start()

    @pl.when(step == 0)
    def _():
        for copy in own:
            copy.wait()

    @pl.when(step < blocks)
    def _():
        left = nn(x[...], c1[...])
        right = nn(x[...], c2[...])
        inner = (left * right).astype(BF16)
        upstream = nt(cot[...], cd[...])
        grad_left = (upstream * right).astype(BF16)
        grad_right = (upstream * left).astype(BF16)
        slot = lax.rem(step, 2)
        for k, buffer in enumerate((reducer.given, reducer.kept)):
            buffer[slot, 0] = nn(rows_of(xt, k), grad_left).astype(BF16)
            buffer[slot, 1] = nn(rows_of(xt, k), grad_right).astype(BF16)
            buffer[slot, 2] = nn(rows_of(cott, k), inner).astype(BF16)
            if k == 0:
                reducer.begin(step)
        term[...] += nn(inner, cd[...])
        part[...] += nt(grad_left, c1[...]) + nt(grad_right, c2[...])

    @pl.when(step == blocks - 1)
    def _():
        for copy in done:
            copy.start()

    ride.after(step, had_b, pieces[15:], refs)
    reducer.run(step, out)

    @pl.when(step == reducer.last)
    def _():
        for copy in done:
            copy.wait()


def rows_of(ref, k):
    block = ref[k]
    return block.reshape(block.shape[0] * block.shape[1], block.shape[2])


def run_units(matrices, second, cot, second_t, cot_t, pieces, ride, cut, depth, ident):
    n, d = second.shape
    units = matrices[0].shape[1]
    blocks = units // HEAD
    pairs, _, rows, _ = second_t.shape
    reducer = Reducer(0, blocks, 3, depth, rows, (1, 3, 5, 7))
    geo = dict(blocks=blocks, cut=cut, d=d, units=units)
    at = lambda s: jnp.minimum(s, blocks - 1)
    columns = pl.BlockSpec((d, HEAD), lambda s: (0, at(s)))
    turned = pltpu.VMEM((2, pairs, rows, n), BF16)
    size = max(cut, units - cut)
    return launch(
        functools.partial(units_kernel, geo, reducer, ride),
        "sglu_and_gradients",
        reducer.last + 1,
        list(matrices) + [second, cot, second_t, cot_t] + list(pieces) + ride.inputs,
        [columns, columns, pl.BlockSpec((HEAD, d), lambda s: (at(s), 0)), once(second.shape)]
        + [anywhere()] * (3 + len(pieces) + len(ride.inputs)),
        [struct((n, d), F32), struct((n, d), F32), struct((3, rows, units), F32)] + ride.outs,
        [anywhere(), anywhere(), whole_block((3, rows, units))] + [anywhere()] * len(ride.outs),
        [
            pltpu.VMEM((n, d), F32),
            pltpu.VMEM((n, d), F32),
            pltpu.VMEM((n, d), BF16),
            turned,
            turned,
            pltpu.VMEM((d, size), BF16),
            pltpu.VMEM((d, size), BF16),
            pltpu.VMEM((size, d), BF16),
            pltpu.VMEM((d, 2 * HEAD), BF16),
            pltpu.VMEM((d, 2 * HEAD), BF16),
            pltpu.VMEM((2 * HEAD, d), BF16),
            pltpu.SemaphoreType.DMA((2, 3, 8)),
            pltpu.SemaphoreType.DMA((7,)),
        ]
        + reducer.scratch
        + ride.scratch,
        36 * n * d * units,
        partners=reducer.partners + ride.partners,
        ident=ident,
    )[:3]


def after_kernel(chunks, heads, info, slopes, term, part, cot, mid, sel, att, wo, qpre, rot, out_o, gmid_o, pair_o, gatt_o, et_o, e0_o, state):
    step = pl.program_id(0)
    c = chunks - 1 - step

    @pl.when(step == 0)
    def _():
        state[...] = jnp.zeros_like(state)

    middle = mid[...]
    out_o[...] = (middle + term[...]).astype(BF16)
    grad_middle = cot[...].astype(F32) + norm_back(middle, scale_of(middle), part[...])
    gmid_o[...] = grad_middle
    branch = grad_middle.astype(BF16)
    pair_o[0] = branch
    grad_mixed = nt(branch, wo[...])
    attended = att[...].astype(F32)
    scale = scale_of(attended)
    pair_o[1] = (grad_mixed * attended * scale).astype(BF16)
    alive = (row_index((CHUNK, 1)) + c * CHUNK < info[4 * chunks]).astype(F32)
    grad_att = norm_back(attended, scale, grad_mixed * sel[...].astype(F32)) * alive
    gatt_o[...] = grad_att.astype(BF16)
    cs, sn = rot[:, :HEAD], rot[:, HEAD:]
    keep = info[chunks + c].astype(F32)
    for h in range(heads):
        slope = slopes[h]
        query = featured(qpre[:, head_slice(h)].astype(F32), cs, sn)
        faded = (grad_att[:, head_slice(h)] * fade_from_start(slope, HEAD)).astype(BF16)
        old = state[h]
        et_o[0, h] = old.astype(BF16)
        state[h] = keep * (
            jnp.exp(jnp.full((1, 2 * HEAD), -slope * CHUNK, F32)) * old + nn(faded.T, query)
        )
    e0_o[...] = state[...].astype(BF16)


def run_after(info, slopes, term, part, cot, mid, sel, att, wo, qpre, rot, **ride):
    n, d = cot.shape
    heads, chunks = d // HEAD, n // CHUNK
    back = lambda s: chunks - 1 - s
    tile = pl.BlockSpec((CHUNK, d), lambda s: (back(s), 0))
    return launch(
        functools.partial(after_kernel, chunks, heads),
        "output_and_row_gradients",
        chunks,
        [info, slopes, term, part, cot, mid, sel, att, wo, qpre, rot],
        [smem(), smem()]
        + [tile] * 6
        + [whole_block(wo.shape), tile, pl.BlockSpec((CHUNK, 2 * HEAD), lambda s: (back(s), 0))],
        [
            struct((n, d)),
            struct((n, d), F32),
            struct((2, n, d)),
            struct((n, d)),
            struct((chunks, heads, HEAD, 2 * HEAD)),
            struct((heads, HEAD, 2 * HEAD)),
        ],
        [
            tile,
            tile,
            pl.BlockSpec((2, CHUNK, d), lambda s: (0, back(s), 0)),
            tile,
            pl.BlockSpec((1, heads, HEAD, 2 * HEAD), lambda s: (back(s), 0, 0, 0)),
            whole_block((heads, HEAD, 2 * HEAD)),
        ],
        [pltpu.VMEM((heads, HEAD, 2 * HEAD), F32)],
        3 * n * d * d,
        **ride,
    )


def weights_kernel(items, peers, *refs):
    item = lax.div(pl.program_id(0), peers)
    lefts, right, out = refs[:-2], refs[-2], refs[-1]
    for i, left in enumerate(lefts):

        @pl.when(functools.reduce(jnp.logical_or, [item == t for t, w in enumerate(items) if w == i]))
        def _(left=left):
            block = left[...]
            block = block.reshape(-1, block.shape[-1])
            out[...] = nn(block, right[...]).astype(BF16).reshape(out.shape)


def run_weights(lefts, items, rights, right_spec, peers, width):
    pairs, _, rows, n = lefts[0].shape
    shape = (peers, len(items), pairs, 2, rows, width)
    which = lambda s: (lax.div(s, peers), lax.rem(s, peers))
    (out,) = launch(
        functools.partial(weights_kernel, items, peers),
        "weight_gradients",
        peers * len(items),
        list(lefts) + [rights],
        [whole_block(left.shape) for left in lefts] + [right_spec(which)],
        [struct(shape)],
        [pl.BlockSpec((None, None) + shape[2:], lambda s: (which(s)[1], which(s)[0], 0, 0, 0, 0))],
        [],
        4 * n * pairs * rows * width * len(items) * peers,
    )
    return out


def head_back(slope, qpre, kpre, value, grad, state, ending, cs, sn):
    qp, kp = qpre.astype(F32), kpre.astype(F32)
    qs, ks = sigmoid(qp), sigmoid(kp)
    qa, ka = qp * qs, kp * ks
    query = jnp.concatenate([qa * cs, qa * sn], axis=-1).astype(BF16)
    key = jnp.concatenate([ka * cs, ka * sn], axis=-1).astype(BF16)
    state, ending = state.astype(BF16), ending.astype(BF16)
    table, turned = decay_table(slope, False), decay_table(slope, True)
    scores_t = (nt(key, query) * turned).astype(BF16)
    slope_s = (nt(grad, value) * table).astype(BF16)
    slope_t = (nt(value, grad) * turned).astype(BF16)
    start = fade_from_start(slope, HEAD)
    end = fade_to_end(slope, HEAD)
    grad_start = (grad.astype(F32) * start).astype(BF16)
    value_end = (value.astype(F32) * end).astype(BF16)
    dq = nn(slope_s, key) + nn(grad_start, state)
    dk = nn(slope_t, query) + nn(value_end, ending)
    dv = nn(scores_t, grad) + end * nt(key, ending)
    dq = dq[:, :HEAD] * cs + dq[:, HEAD:] * sn
    dk = dk[:, :HEAD] * cs + dk[:, HEAD:] * sn
    gq = (dq * (qs * (1.0 + qp * (1.0 - qs)))).astype(BF16)
    gk = (dk * (ks * (1.0 + kp * (1.0 - ks)))).astype(BF16)
    return gq, gk, dv.astype(BF16)


def attention_back_kernel(chunks, first_head, info, slopes, qpre, kpre, values, gatt, st, came, et, left, rot, grads_o):
    pair, c = lax.div(pl.program_id(0), chunks), lax.rem(pl.program_id(0), chunks)
    cs, sn = rot[:, :HEAD], rot[:, HEAD:]
    before = info[2 * chunks + c].astype(F32)
    after = info[3 * chunks + c].astype(F32)
    span = (CHUNK * c).astype(F32)
    rest = (CHUNK * (chunks - 1 - c)).astype(F32)
    for h in range(2):
        slope = slopes[first_head + 2 * pair + h]
        cols = head_slice(h)
        lane = jnp.zeros((1, 2 * HEAD), F32)
        state = st[0, h].astype(F32) + came[h].astype(F32) * (jnp.exp(lane - slope * span) * before)
        ending = et[0, h].astype(F32) + left[h].astype(F32) * (jnp.exp(lane - slope * rest) * after)
        three = head_back(
            slope, qpre[:, cols], kpre[:, cols], values[:, cols], gatt[:, cols], state, ending, cs, sn
        )
        for i in range(3):
            grads_o[i, :, cols] = three[i]


def run_attention_back(info, slopes, qpre, kpre, values, gatt, st, came, et, left, rot, first_head, heads, **ride):
    n, d = qpre.shape
    chunks = n // CHUNK
    skip = first_head // 2
    pair = lambda s: lax.div(s, chunks)
    chunk = lambda s: lax.rem(s, chunks)
    tile = pl.BlockSpec((CHUNK, 2 * HEAD), lambda s: (chunk(s), skip + pair(s)))
    states = pl.BlockSpec((1, 2, HEAD, 2 * HEAD), lambda s: (chunk(s), skip + pair(s), 0, 0))
    ends = pl.BlockSpec((2, HEAD, 2 * HEAD), lambda s: (skip + pair(s), 0, 0))
    return launch(
        functools.partial(attention_back_kernel, chunks, first_head),
        "attention_backward",
        chunks * heads // 2,
        [info, slopes, qpre, kpre, values, gatt, st, came, et, left, rot],
        [smem(), smem(), tile, tile, tile, tile, states, ends, states, ends, pl.BlockSpec((CHUNK, 2 * HEAD), lambda s: (chunk(s), 0))],
        [struct((3, n, heads * HEAD))],
        [pl.BlockSpec((3, CHUNK, 2 * HEAD), lambda s: (0, chunk(s), pair(s)))],
        [],
        18 * n * 256 * 256 * heads // 2,
        **ride,
    )


def projections_kernel(geo, outer, inner, info, slopes, *refs):
    chunks, blocks, d, n = geo["chunks"], geo["blocks"], geo["d"], geo["n"]
    refs = list(refs)
    take = lambda k: [refs.pop(0) for _ in range(k)]
    columns = [take(2) for _ in range(4)]
    states = [take(2) for _ in range(2)]
    (came, leaving, rot, branch_a, branch_b, sel_a, sel_b, sel, hid, gmid, mixt_h, normt_h) = take(12)
    weights_h = take(4)
    hidden_o, out, out2 = take(3)
    grads, block, mixt, normt, w4, left, sems, state_sems = take(8)
    outer.bind(take(len(outer.scratch)))
    inner.bind(refs)
    step = pl.program_id(0)
    core = lax.rem(lax.axis_index("dp"), 2)
    me = lax.axis_index("mp")
    loads = [
        pltpu.make_async_copy(mixt_h.at[:, 1 - core], mixt.at[0], sems.at[0]),
        pltpu.make_async_copy(mixt_h.at[:, core], mixt.at[1], sems.at[1]),
        pltpu.make_async_copy(normt_h.at[:, 1 - core], normt.at[0], sems.at[2]),
        pltpu.make_async_copy(normt_h.at[:, core], normt.at[1], sems.at[3]),
    ]
    matrices = [pltpu.make_async_copy(w, w4.at[i], sems.at[4 + i]) for i, w in enumerate(weights_h)]
    exchange = remote(leaving, left, state_sems.at[0], state_sems.at[1], "mp", 1)

    @pl.when(step == 0)
    def _():
        exchange.start()
        for copy in loads:
            copy.start()
        for copy in matrices:
            copy.start()
        for copy in loads:
            copy.wait()

    @pl.when(step < blocks)
    def _():
        slot = lax.rem(step, 2)
        gb = jnp.concatenate([branch_a[...], branch_b[...]], axis=1)
        gs = jnp.concatenate([sel_a[...], sel_b[...]], axis=1)
        for k, buffer in enumerate((outer.given, outer.kept)):
            buffer[slot, 0] = nn(rows_of(mixt, k), gb).astype(BF16)
            buffer[slot, 1] = nn(rows_of(normt, k), gs).astype(BF16)
            if k == 0:
                outer.begin(step)

    @pl.when(step == blocks - 1)
    def _():
        exchange.wait()

    @pl.when(jnp.logical_and(step >= blocks, step < 2 * blocks))
    def _():
        j = step - blocks

        def one(c, carry):
            here = pl.ds(pl.multiple_of(c * CHUNK, CHUNK), CHUNK)
            cs, sn = rot[here, :HEAD], rot[here, HEAD:]
            before = info[2 * chunks + c].astype(F32)
            after = info[3 * chunks + c].astype(F32)
            span = (CHUNK * c).astype(F32)
            rest = (CHUNK * (chunks - 1 - c)).astype(F32)
            for side in range(2):
                h = (me if side == 0 else 1 - me) * blocks + j
                slope = slopes[h]
                qpre, kpre, values, gatt = [pair[side][here, :] for pair in columns]
                st, et = [pair[side][c, 0].astype(F32) for pair in states]
                lane = jnp.zeros((1, 2 * HEAD), F32)
                state = st + came[h].astype(F32) * (jnp.exp(lane - slope * span) * before)
                ending = et + left[h].astype(F32) * (jnp.exp(lane - slope * rest) * after)
                three = head_back(slope, qpre, kpre, values, gatt, state, ending, cs, sn)
                cols = pl.ds(pl.multiple_of(h * HEAD, HEAD), HEAD)
                for i in range(3):
                    block[i, here, head_slice(side)] = three[i]
                    grads[i, here, cols] = three[i]
            return carry

        lax.fori_loop(0, chunks, one, 0)
        slot = lax.rem(j, 2)
        for k, buffer in enumerate((inner.given, inner.kept)):
            for i in range(3):
                buffer[slot, i] = nn(rows_of(normt, k), block[i]).astype(BF16)
            if k == 0:
                inner.begin(j)

    @pl.when(step == 2 * blocks)
    def _():
        for copy in matrices:
            copy.wait()

    @pl.when(jnp.logical_and(step >= 2 * blocks, step < 2 * blocks + chunks))
    def _():
        here = pl.ds(pl.multiple_of((step - 2 * blocks) * CHUNK, CHUNK), CHUNK)
        total = nt(sel[...], w4[3])
        for i in range(3):
            total = total + nt(grads[i, here, :], w4[i])
        x = hid[...].astype(F32)
        hidden_o[...] = (gmid[...] + norm_back(x, scale_of(x), total)).astype(BF16)

    outer.run(step, out)
    inner.run(step, out2)


def run_projections(info, slopes, qpre, kpre, values, gatt, st, et, came, leaving, rot, pair, hidden, gmid, mixed_t, normed_t, weights, depth, ident):
    n, d = qpre.shape
    heads, chunks = d // HEAD, n // CHUNK
    blocks = heads // 2
    pairs, _, rows, _ = mixed_t.shape
    outer = Reducer(0, blocks, 2, depth, rows, (1, 3, 5, 7))
    inner = Reducer(blocks, blocks, 3, depth, rows, (1, 2, 4, 5))
    steps = max(outer.last, inner.last, 2 * blocks + chunks - 1) + 1
    geo = dict(chunks=chunks, blocks=blocks, d=d, n=n)
    early = lambda s: jnp.minimum(s, blocks - 1)
    mid = lambda s: jnp.clip(s - blocks, 0, blocks - 1)
    late = lambda s: jnp.clip(s - 2 * blocks, 0, chunks - 1)
    side = lambda k: blocks * (lax.axis_index("mp") if k == 0 else 1 - lax.axis_index("mp"))
    column = lambda k: pl.BlockSpec((n, HEAD), lambda s: (0, side(k) + mid(s)))
    state = lambda k: pl.BlockSpec((chunks, 1, HEAD, 2 * HEAD), lambda s: (0, side(k) + mid(s), 0, 0))
    pair_column = lambda i, k: pl.BlockSpec((None, n, HEAD), lambda s: (i, 0, side(k) + early(s)))
    tile = pl.BlockSpec((CHUNK, d), lambda s: (late(s), 0))
    turned = pltpu.VMEM((2, pairs, rows, n), BF16)
    return launch(
        functools.partial(projections_kernel, geo, outer, inner),
        "attention_backward_and_gradients",
        steps,
        [info, slopes]
        + [a for a in (qpre, kpre, values, gatt, st, et) for _ in range(2)]
        + [came, leaving, rot, pair, pair, pair, pair, pair, hidden, gmid, mixed_t, normed_t]
        + list(weights),
        [smem(), smem()]
        + [column(k) for _ in range(4) for k in range(2)]
        + [state(k) for _ in range(2) for k in range(2)]
        + [once(came.shape), anywhere(), once(rot.shape)]
        + [pair_column(i, k) for i in range(2) for k in range(2)]
        + [pl.BlockSpec((None, CHUNK, d), lambda s: (1, late(s), 0)), tile, tile]
        + [anywhere()] * 6,
        [struct((n, d)), struct((2, rows, d // 2), F32), struct((3, rows, d // 2), F32)],
        [tile, whole_block((2, rows, d // 2)), whole_block((3, rows, d // 2))],
        [
            pltpu.VMEM((3, n, d), BF16),
            pltpu.VMEM((3, n, 2 * HEAD), BF16),
            turned,
            turned,
            pltpu.VMEM((4, d, d), BF16),
            pltpu.VMEM(leaving.shape, BF16),
            pltpu.SemaphoreType.DMA((8,)),
            pltpu.SemaphoreType.DMA((2,)),
        ]
        + outer.scratch
        + inner.scratch,
        30 * n * d * d,
        partners=outer.partners,
        ident=ident,
    )


def input_kernel(wq, wk, wv, ws, grads, pair, hid, gmid, out):
    total = nt(grads[0], wq[...]) + nt(grads[1], wk[...]) + nt(grads[2], wv[...]) + nt(pair[...], ws[...])
    x = hid[...].astype(F32)
    out[...] = (gmid[...] + norm_back(x, scale_of(x), total)).astype(BF16)


def run_input(weights, grads, pair, hidden, gmid, **ride):
    n, d = hidden.shape
    tile = pl.BlockSpec((CHUNK, d), lambda c: (c, 0))
    return launch(
        input_kernel,
        "input_gradient",
        n // CHUNK,
        list(weights) + [grads, pair, hidden, gmid],
        [whole_block(w.shape) for w in weights]
        + [
            pl.BlockSpec((3, CHUNK, d), lambda c: (0, c, 0)),
            pl.BlockSpec((None, CHUNK, d), lambda c: (1, c, 0)),
            tile,
            tile,
        ],
        [struct((n, d))],
        [tile],
        [],
        8 * n * d * d,
        **ride,
    )


def reduced(lefts, items, rights, spec, peers, width):
    full = run_weights(lefts, items, rights, spec, peers, width)
    full = full.reshape(peers, len(items), -1, full.shape[4], width)
    mine = lax.psum_scatter(full, "dp", scatter_dimension=2, tiled=False)
    return lax.psum_scatter(mine, "mp", scatter_dimension=0, tiled=False).astype(F32)


def per_device(
    hidden_in,
    query_weight,
    key_weight,
    value_weight,
    select_weight,
    out_weight,
    first_weight,
    second_weight,
    down_weight,
    decay_slope,
    doc_lengths,
    cotangent,
):
    count, d = hidden_in.shape
    heads, chunks = d // HEAD, count // CHUNK
    peers, parts = lax.axis_size("mp"), lax.axis_size("dp")
    me = lax.axis_index("mp")
    depth = parts // 4
    group = count * peers
    units = first_weight.shape[1]
    lengths = doc_lengths[0].astype(jnp.int32)
    info = chunk_info(lengths, me, peers, count)
    rot = turning(info, chunks, group // 2)
    slopes = decay_slope
    matrices = (first_weight, second_weight, down_weight)
    riding = peers == 2

    if riding:
        cut = -(-units // 256) * 128
        ranges = [(0, cut), (cut, units - cut)]
    else:
        ranges = [(0, units)]

    def like(arrays, count=None):
        return [struct(a.shape if count is None else (count,) + a.shape) for a in arrays]

    def over_mp(g, steps):
        low, size = ranges[g]

        def source(w):
            def src(i, o):
                eighth = lax.rem(lax.axis_index("dp"), 8)
                if w < 2:
                    rows = d // 8
                    return i[w].at[pl.ds(pl.multiple_of(eighth * rows, 16), rows), pl.ds(low, size)]
                rows = size // 8
                return i[w].at[pl.ds(pl.multiple_of(low + eighth * rows, 16), rows), :]

            return src

        outs = [struct((d // 8, size)), struct((d // 8, size)), struct((size // 8, d))]
        copies = [(source(w), lambda i, o, w=w: o[w], "mp", 1) for w in range(3)]
        return Carry(matrices, outs, [(0, steps, copies)])

    def near(w):
        return [
            (lambda i, o: i[w], lambda i, o: o[w].at[0], "dp", 2),
            (lambda i, o: i[w], lambda i, o: o[w].at[1], "dp", 4),
            (lambda i, o: i[w], lambda i, o: o[w].at[2], "dp", 1),
        ]

    def far(w, src, dst, rows):
        top = -(-rows // 32) * 16
        upper, lower = pl.ds(0, top), pl.ds(top, rows - top)
        return [
            (lambda i, o: src(i, o).at[1, upper, :], lambda i, o: dst(i, o).at[0, upper, :], "dp", 2),
            (lambda i, o: src(i, o).at[0, lower, :], lambda i, o: dst(i, o).at[0, lower, :], "dp", 4),
            (lambda i, o: src(i, o).at[0], lambda i, o: dst(i, o).at[1], "dp", 1),
            (lambda i, o: src(i, o).at[1], lambda i, o: dst(i, o).at[2], "dp", 1),
        ]

    ride = dict(guests=[over_mp(0, chunks - 1)], ident=1) if riding else {}
    normed, normed_t, kpre, values, st, final, *had = run_keys(
        info, slopes, hidden_in, key_weight, value_weight, rot, parts, **ride
    )
    whole_keep = info[2 * chunks + chunks - 1].astype(F32)
    decay = jnp.exp(-slopes * count)
    ride = {}
    if riding:
        state_copy = [(lambda i, o: i[0], lambda i, o: o[0], "mp", 1)]
        near_copies = [c for w in range(3) for c in near(w)]
        ride = dict(
            guests=[
                Carry([final], like([final]), [(0, chunks - 1, state_copy)]),
                Carry(had, like(had, 3), [(0, chunks - 1, near_copies)]),
            ],
            ident=2,
        )
    qpre, sel, att, *more = run_inside(
        info, slopes, normed, query_weight, select_weight, kpre, values, st, rot, **ride
    )
    if riding:
        came, close = more[0], more[1:]
    else:
        finals = lax.all_gather(final, "mp")
        keeps = lax.all_gather(whole_keep.reshape(1), "mp")[:, 0]

        def ahead(k, total):
            new = finals[k].astype(F32) + (keeps[k] * decay)[:, None, None] * total
            return jnp.where(k < me, new, total)

        came = lax.fori_loop(0, peers, ahead, jnp.zeros(final.shape, F32)).astype(BF16)
    ride = {}
    if riding:
        first_phase = []
        for w in range(3):
            src, dst = (lambda i, o, w=w: i[w]), (lambda i, o, w=w: o[w])
            first_phase += far(w, src, dst, close[w].shape[1])
        second_phase = [
            (lambda i, o, w=w: o[w].at[0], lambda i, o, w=w: o[3 + w], "dp", 1) for w in range(3)
        ]
        ride = dict(
            guests=[
                Carry(
                    close,
                    like(close) + like(had),
                    [(0, chunks // 2, first_phase), (chunks // 2 + 1, chunks - 1, second_phase)],
                ),
                over_mp(1, chunks - 1),
            ],
            ident=3,
        )
    attended, mixed_t, middle, second, second_t, cot_t, *more = run_mix(
        info, slopes, att, qpre, came, sel, out_weight, hidden_in, cotangent, rot, parts, **ride
    )

    if riding:
        wide, corner, had_b = more[:3], more[3:6], more[6:9]
        one = [c for w in range(3) for c in near(w)]
        two = []
        for w in range(3):
            src, dst = (lambda i, o, w=w: o[w]), (lambda i, o, w=w: o[3 + w])
            two += far(w, src, dst, had_b[w].shape[0])
        three = [
            (lambda i, o, w=w: o[3 + w].at[0], lambda i, o, w=w: o[6 + w], "dp", 1) for w in range(3)
        ]
        turn = ranges[0][1] // HEAD
        ride = Carry(
            had_b,
            like(had_b, 3) + like(had_b, 3) + like(had_b),
            [(0, 1, one), (2, 3, two), (4, 4, three)],
        )
        pieces = list(had) + list(close) + list(wide) + list(corner)
        term, part, sglu = run_units(
            matrices, second, cotangent, second_t, cot_t, pieces, ride, ranges[0][1], depth, ident=4
        )
    else:
        sources = [lax.all_gather(w, "mp") for w in matrices]
        grads, term, part = run_sglu(second, cotangent, *sources)
        units_spec = lambda at: pl.BlockSpec((None, None, count, units), lambda s: at(s) + (0, 0))
        sglu = reduced([second_t, cot_t], (0, 0, 1), grads, units_spec, peers, units)
    output, grad_middle, pair, grad_att, et, leaving = run_after(
        info, slopes, term, part, cotangent, middle, sel, attended, out_weight, qpre, rot
    )
    inputs_weights = [query_weight, key_weight, value_weight, select_weight]
    if riding:
        grad_hidden, out_sel, inputs = run_projections(
            info, slopes, qpre, kpre, values, grad_att, st, et, came, leaving, rot, pair,
            hidden_in, grad_middle, mixed_t, normed_t, inputs_weights, depth, ident=5,
        )
    else:
        leavings = lax.all_gather(leaving, "mp")

        def behind(step, total):
            k = peers - 1 - step
            new = leavings[k].astype(F32) + (keeps[k] * decay)[:, None, None] * total
            return jnp.where(k > me, new, total)

        left = lax.fori_loop(0, peers, behind, jnp.zeros(leaving.shape, F32)).astype(BF16)
        share = d // peers
        wide_spec = lambda at: pl.BlockSpec((None, count, share), lambda s: (at(s)[0], 0, at(s)[1]))
        out_sel = reduced([mixed_t, normed_t], (0, 1), pair, wide_spec, peers, share)
        (qkv,) = run_attention_back(
            info, slopes, qpre, kpre, values, grad_att, st, came, et, left, rot, 0, heads
        )
        inputs = reduced([normed_t], (0, 0, 0), qkv, wide_spec, peers, share)
        (grad_hidden,) = run_input(inputs_weights, qkv, pair, hidden_in, grad_middle)
    return (
        output,
        grad_hidden,
        inputs[0],
        inputs[1],
        inputs[2],
        out_sel[1],
        out_sel[0],
        sglu[0],
        sglu[1],
        jnp.transpose(sglu[2]),
    )


def solution(mesh):
    rows = P(("dp", "mp"), None)
    in_specs = (
        rows,
        P(),
        P(),
        P(),
        P(),
        P(),
        P(None, "mp"),
        P(None, "mp"),
        P("mp", None),
        P(),
        P("dp", None),
        rows,
    )
    out_specs = (rows, rows) + (P("dp", "mp"),) * 7 + (P("mp", "dp"),)
    return jax.shard_map(
        per_device, mesh=mesh, in_specs=in_specs, out_specs=out_specs, check_vma=False
    )
```

profile of v0, /device:TPU:12, one launch (start us, length us, event | category | flops | bytes accessed | tf_op | source)
XLA Modules:
  0.0 299.2 jit_solution(4748710330955884630)
XLA Ops:
  0.6 1.4 fusion.3
  4.0 0.7 compare_convert_fusion
  4.6 0.6 slice.53
  5.2 0.7 compare_convert_fusion.1
  5.9 0.6 concatenate.6.refs_0_
  6.5 0.6 fusion.2
  14.8 1.3 constant_dynamic-slice_fusion.3
  16.1 1.0 pad_maximum_fusion.refs_5_.refs_8_.refs_9_.refs_10_.refs_16_
  17.2 19.7 %keys_values_states.1 = (bf16[1024,1024]{1,0:T(8,128)(2,1)}, bf16[8,2,64,1024]{3,2,1,0:T(8,128)(2,1)}, bf16[1024,1024]{1,0:T(8,128)(2,1)}, bf16[1024,1024]{1,0:T...) custom-call(s32[17]{0:T(128)} %concatenate.6.refs_0_, ...), custom_call_target="tpu_custom_call" | custom-call | flops 4294967296 | bytes 27590756 | tf_op jit(solution)/shard_map/keys_values_states/pallas_call | solution.py:307
  36.9 20.7 %queries_attention.1 = (bf16[1024,1024]{1,0:T(8,128)(2,1)}, bf16[1024,1024]{1,0:T(8,128)(2,1)}, f32[1024,1024]{1,0:T(8,128)}, bf16[8,128,256]{2,1,0:T(8,128)(2,1...) custom-call(s32[17]{0:T(128)} %concatenate.6.refs_0_, f32[8]{0:T(128)} %refs_1_.11, ...), custom_call_target="tpu_custom_call" | custom-call | flops 6442450944 | bytes 25428068 | tf_op jit(solution)/shard_map/queries_attention/pallas_call | solution.py:307
  57.6 18.4 %carried_mixed_middle.1 = (bf16[1024,1024]{1,0:T(8,128)(2,1)}, bf16[8,2,64,1024]{3,2,1,0:T(8,128)(2,1)}, f32[1024,1024]{1,0:T(8,128)}, bf16[1024,1024]{1,0:T(8,1...) custom-call(s32[17]{0:T(128)} %concatenate.6.refs_0_, ...), custom_call_target="tpu_custom_call" | custom-call | flops 3221225472 | bytes 44204132 | tf_op jit(solution)/shard_map/carried_mixed_middle/pallas_call | solution.py:307
  76.0 114.1 %sglu_and_gradients.1 = (f32[1024,1024]{1,0:T(8,128)}, f32[1024,1024]{1,0:T(8,128)}, f32[3,64,1408]{2,1,0:T(8,128)}, bf16[3,128,640]{2,1,0:T(8,128)(2,1)}, bf16[...) custom-call(bf16[1024,1408]{1,0:T(8,128)(2,1)} %refs_0_.1, ...), custom_call_target="tpu_custom_call" | custom-call | flops 53150220288 | bytes 35160064 | tf_op jit(solution)/shard_map/sglu_and_gradients/pallas_call | solution.py:307
  190.1 17.7 %output_and_row_gradients.1 = (bf16[1024,1024]{1,0:T(8,128)(2,1)}, f32[1024,1024]{1,0:T(8,128)}, bf16[2,1024,1024]{2,1,0:T(8,128)(2,1)}, bf16[1024,1024]{1,0:T(8...) custom-call(s32[17]{0:T(128)} %concatenate.6.refs_0_, f32[8]{0:T(128)} %refs_1_.11, ...), custom_call_target="tpu_custom_call" | custom-call | flops 3221225472 | bytes 39321700 | tf_op jit(solution)/shard_map/output_and_row_gradients/pallas_call | solution.py:307
  207.9 0.0 copy-start.1
  207.9 85.3 %attention_backward_and_gradients.1 = (bf16[1024,1024]{1,0:T(8,128)(2,1)}, f32[2,64,512]{2,1,0:T(8,128)}, f32[3,64,512]{2,1,0:T(8,128)}) custom-call(s32[17]{0:T(128)} %concatenate.6.refs_0_, f32[8]{0:T(128)} %refs_1_.11, bf16[1024,1024]{1,0:T(8,128)(2,1)} %get-tuple-element.62.refs_3_.refs_9_.refs_2_, ...), custom_call_target="tpu_custom_call" | custom-call | flops 32212254720 | bytes 69861472 | tf_op jit(solution)/shard_map/attention_backward_and_gradients/pallas_call | solution.py:307
  293.3 0.0 copy-start
  293.3 1.8 slice_bitcast_fusion.3
  295.1 1.8 slice_bitcast_fusion.5
  296.9 0.0 copy-done.1
  296.9 1.0 slice_bitcast_fusion
  297.9 0.0 copy-done
  297.9 1.3 copy.24
Async XLA Ops:
  207.9 89.0 %copy-start.1 = (f32[3,64,1408]{2,1,0:T(8,128)S(1)}, f32[3,64,1408]{2,1,0:T(8,128)}, u32[]{:S(2)}) copy-start(f32[3,64,1408]{2,1,0:T(8,128)} %get-tuple-element.95) | copy-start | bytes 3244036
  293.3 4.6 %copy-start = (bf16[1024,1024]{1,0:T(8,128)(2,1)S(1)}, bf16[1024,1024]{1,0:T(8,128)(2,1)}, u32[]{:S(2)}) copy-start(bf16[1024,1024]{1,0:T(8,128)(2,1)} %get-tuple-element.131) | copy-start | bytes 6291460
where the time goes:
time: 302 us; the launch traced here: 299 us
  Pallas kernels  276 us (91%)
  between operations  10.5 us (3%)
  local copies, waits for them, and re-layouts  10.4 us (3%)
    pallas_call x6, Pallas kernels, launch(): pl.pallas_call(body, grid=(steps,), in_specs=all_specs, out_specs=all_out...  276 us

commit v1 on v0

--- a/solution.py
+++ b/solution.py
@@ -13,7 +13,7 @@
 EPSILON = 1e-06
 BF16 = jnp.bfloat16
 F32 = jnp.float32
-VMEM_LIMIT = 58 * 1024 * 1024
+VMEM_LIMIT = 61 * 1024 * 1024
 
 
 def nn(left, right):
@@ -179,18 +179,18 @@
             buf(4, items, n, wide),
             buf(2, *pair),
             buf(2, *pair),
-            buf(blocks, *pair),
+            buf(4, *pair),
             buf(2, *flat),
             buf(2, *flat),
-            buf(blocks, *flat),
+            buf(4, *flat),
             buf(2, *one),
             buf(2, *one),
-            buf(blocks, *one),
+            buf(4, *one),
             buf(2, *one),
             buf(2, *one),
-            buf(blocks, *one),
+            buf(4, *one),
             buf(2, depth, items, rows, HEAD),
-            buf(blocks, depth - 1, items, rows, HEAD),
+            buf(4, depth - 1, items, rows, HEAD),
             pltpu.SemaphoreType.DMA((self.KINDS, blocks)),
             pltpu.SemaphoreType.DMA((self.KINDS, blocks)),
         ]
@@ -205,16 +205,16 @@
 
     def copies(self, stage, j):
         (given, kept, got, ps, pk, pr, qs, qk, qr, ps2, pk2, pr2, qs2, qk2, qr2, line, zr, send, recv) = self.refs
-        slot = lax.rem(j, 2)
+        slot, four = lax.rem(j, 2), lax.rem(j, 4)
         if stage == 0:
-            plan = [(0, given.at[slot], got.at[lax.rem(j, 4)], "dp", 1)]
+            plan = [(0, given.at[slot], got.at[four], "dp", 1)]
         elif stage == 1:
-            plan = [(1, ps.at[slot], pr.at[j], "dp", 2), (2, qs.at[slot], qr.at[j], "mp", 1)]
+            plan = [(1, ps.at[slot], pr.at[four], "dp", 2), (2, qs.at[slot], qr.at[four], "mp", 1)]
         elif stage == 2:
-            plan = [(3, ps2.at[slot], pr2.at[j], "mp", 1), (4, qs2.at[slot], qr2.at[j], "dp", 2)]
+            plan = [(3, ps2.at[slot], pr2.at[four], "mp", 1), (4, qs2.at[slot], qr2.at[four], "dp", 2)]
         else:
             plan = [
-                (4 + k, line.at[slot, flipped(self.z, k)], zr.at[j, k - 1], "dp", 4 * k)
+                (4 + k, line.at[slot, flipped(self.z, k)], zr.at[four, k - 1], "dp", 4 * k)
                 for k in range(1, self.depth)
             ]
         return [remote(src, dst, send.at[i, j], recv.at[i, j], axis, mask) for i, src, dst, axis, mask in plan]
@@ -238,10 +238,9 @@
 
     def add(self, stage, j, out):
         (given, kept, got, ps, pk, pr, qs, qk, qr, ps2, pk2, pr2, qs2, qk2, qr2, line, zr, send, recv) = self.refs
-        slot, x, rows = lax.rem(j, 2), self.x, self.rows
+        slot, four, x, rows = lax.rem(j, 2), lax.rem(j, 4), self.x, self.rows
         half = self.depth // 2
         if stage == 1:
-            four = lax.rem(j, 4)
 
             def total(t, z, at):
                 here = pl.ds(pl.multiple_of((2 * z + at) * rows, rows), rows)
@@ -257,17 +256,17 @@
                         qs[slot, at, z, t] = block[:, HEAD:]
         elif stage == 2:
             for z in range(half):
-                block = plus(pk[slot, z], pr[j, z]).astype(BF16)
+                block = plus(pk[slot, z], pr[four, z]).astype(BF16)
                 pk2[slot, z] = block[:, :, :HEAD]
                 ps2[slot, z] = block[:, :, HEAD:]
-                qs2[slot, z] = plus(qk[slot, 1 - x, z], qr[j, 1 - x, z]).astype(BF16)
-                qk2[slot, z] = plus(qk[slot, x, z], qr[j, x, z]).astype(BF16)
+                qs2[slot, z] = plus(qk[slot, 1 - x, z], qr[four, 1 - x, z]).astype(BF16)
+                qk2[slot, z] = plus(qk[slot, x, z], qr[four, x, z]).astype(BF16)
         elif stage == 3:
             for z in range(half):
-                line[slot, z] = plus(pk2[slot, z], pr2[j, z]).astype(BF16)
-                line[slot, half + z] = plus(qk2[slot, z], qr2[j, z]).astype(BF16)
+                line[slot, z] = plus(pk2[slot, z], pr2[four, z]).astype(BF16)
+                line[slot, half + z] = plus(qk2[slot, z], qr2[four, z]).astype(BF16)
         else:
-            total = plus(line[slot, self.z], *[zr[j, k] for k in range(self.depth - 1)])
+            total = plus(line[slot, self.z], *[zr[four, k] for k in range(self.depth - 1)])
             out[:, :, pl.ds(pl.multiple_of(j * HEAD, HEAD), HEAD)] = total
 
 
@@ -319,197 +318,406 @@
     )(*all_inputs)
 
 
-def chunk_info(lengths, me, peers, count):
-    chunks = count // CHUNK
-    offset = me * count
-    first = offset + CHUNK * jnp.arange(chunks, dtype=jnp.int32)
-    begin, start = jnp.zeros_like(first), jnp.int32(0)
-    for i in range(lengths.shape[0]):
-        begin = jnp.where(first >= start, start, begin)
-        start = start + lengths[i]
-    base = first - begin
-    keep = (base > 0).astype(jnp.int32)
-    before = (begin < offset).astype(jnp.int32)
-    after = ((begin[-1] <= first) & (me < peers - 1)).astype(jnp.int32)
-    live = jnp.clip(start - offset, 0, count)
-    return jnp.concatenate([base, keep, before, after, live[None]]).astype(jnp.int32)
-
-
-def turning(info, chunks, longest):
+def tables(longest):
     freq = 10000.0 ** (-np.arange(HEAD, dtype=np.float64) / HEAD)
-    phase = np.arange(longest, dtype=np.float64)[:, None] * freq[None, :]
-    table = jnp.asarray(np.concatenate([np.cos(phase), np.sin(phase)], axis=1), F32)
-    return jnp.concatenate(
-        [lax.dynamic_slice(table, (info[c], 0), (CHUNK, 2 * HEAD)) for c in range(chunks)], axis=0
-    )
-
-
-def keys_kernel(chunks, heads, info, slopes, hid, wk, wv, rot, normed_o, turned_o, kpre_o, val_o, st_o, fin_o, state):
+
+    def both(places):
+        phase = places[:, None] * freq[None, :]
+        return jnp.asarray(np.concatenate([np.cos(phase), np.sin(phase)], axis=1), F32)
+
+    return both(np.arange(CHUNK)), both(np.arange(0, longest, CHUNK))
+
+
+class Layout:
+    def __init__(self, lengths, peers, count):
+        self.lengths, self.peers, self.count = lengths, peers, count
+        self.me = lax.axis_index("mp")
+        self.offset = self.me * count
+
+    def begin(self, first):
+        begin = start = jnp.int32(0)
+        for i in range(self.lengths.shape[1]):
+            begin = jnp.where(first >= start, start, begin)
+            start = start + self.lengths[0, i]
+        return begin
+
+    def first(self, c):
+        return self.offset + c * CHUNK
+
+    def keep(self, c):
+        return jnp.where(self.begin(self.first(c)) < self.first(c), 1.0, 0.0)
+
+    def before(self, c):
+        return jnp.where(self.begin(self.first(c)) < self.offset, 1.0, 0.0)
+
+    def after(self, c):
+        last = self.begin(self.offset + self.count - CHUNK)
+        return jnp.where(last <= self.first(c), 1.0, 0.0) * jnp.where(self.me < self.peers - 1, 1.0, 0.0)
+
+    def alive(self, c, width):
+        end = jnp.int32(0)
+        for i in range(self.lengths.shape[1]):
+            end = end + self.lengths[0, i]
+        return (row_index((CHUNK, width)) + self.first(c) < end).astype(F32)
+
+    def angles(self, c, fine, coarse):
+        base = self.first(c) - self.begin(self.first(c))
+        start = jnp.zeros((1, 2 * HEAD), F32)
+        for k in range(coarse.shape[0]):
+            start = start + coarse[k : k + 1, :] * jnp.where(base == k * CHUNK, 1.0, 0.0)
+        cb, sb = start[:, :HEAD], start[:, HEAD:]
+        cf, sf = fine[:, :HEAD], fine[:, HEAD:]
+        return cf * cb - sf * sb, sf * cb + cf * sb
+
+
+def normed_of(hid):
+    x = hid[...].astype(F32)
+    return (x * scale_of(x)).astype(BF16)
+
+
+def states_chunk(heads, slopes, keep, kpre, values, cs, sn, state, put):
+    for h in range(heads):
+        slope = slopes[h]
+        key = featured(kpre[:, head_slice(h)], cs, sn)
+        faded = (values[:, head_slice(h)] * fade_to_end(slope, HEAD)).astype(BF16)
+        old = state[h] * keep
+        put(h, old.astype(BF16))
+        state[h] = jnp.exp(jnp.full((1, 2 * HEAD), -slope * CHUNK, F32)) * old + nn(faded.T, key)
+
+
+def inside_chunk(heads, slopes, qpre, kpre, values, st, cs, sn, put):
+    for h in range(heads):
+        slope = slopes[h]
+        query = featured(qpre[:, head_slice(h)], cs, sn)
+        key = featured(kpre(h).astype(F32), cs, sn)
+        weights = (nt(query, key) * decay_table(slope, False)).astype(BF16)
+        put(h, nn(weights, values(h)) + fade_from_start(slope, HEAD) * nt(query, st(h)))
+
+
+def carried_chunk(heads, slopes, layout, c, att, qpre, came, cs, sn, total):
+    reached = layout.before(c)
+    lag = (c * CHUNK).astype(F32)
+    alive = layout.alive(c, HEAD)
+    for h in range(heads):
+        query = featured(qpre(h).astype(F32), cs, sn)
+        fade = jnp.exp(-slopes[h] * (row_index((CHUNK, HEAD)).astype(F32) + (lag + 1.0))) * reached
+        total[:, head_slice(h)] = (att(h) + fade * nt(query, came[h])) * alive
+
+
+def mix_chunk(total, sel, wo, hid, att_o, mixt_o, mid_o, sec_o, sect_o):
+    attended = total[...]
+    att_o[...] = attended.astype(BF16)
+    mixed = (attended * scale_of(attended) * sel.astype(F32)).astype(BF16)
+    mixt_o[...] = mixed.T.reshape(mixt_o.shape)
+    middle = hid[...].astype(F32) + nn(mixed, wo)
+    mid_o[...] = middle.astype(BF16)
+    second = (middle * scale_of(middle)).astype(BF16)
+    sec_o[...] = second
+    sect_o[...] = second.T.reshape(sect_o.shape)
+
+
+def state_shape(d):
+    return (d // HEAD, HEAD, 2 * HEAD)
+
+
+def keys_kernel(peers, count, lengths, slopes, hid, wk, wv, fine, coarse, normed_o, turned_o, kpre_o, val_o, st_o, fin_o, state):
     c = pl.program_id(0)
+    layout = Layout(lengths, peers, count)
 
     @pl.when(c == 0)
     def _():
         state[...] = jnp.zeros_like(state)
 
-    x = hid[...].astype(F32)
-    normed = (x * scale_of(x)).astype(BF16)
+    normed = normed_of(hid)
     normed_o[...] = normed
     turned_o[...] = normed.T.reshape(turned_o.shape)
     kpre = nn(normed, wk[...])
     kpre_o[...] = kpre.astype(BF16)
     values = nn(normed, wv[...])
     val_o[...] = values.astype(BF16)
-    cs, sn = rot[:, :HEAD], rot[:, HEAD:]
-    keep = info[chunks + c].astype(F32)
-    for h in range(heads):
-        slope = slopes[h]
-        key = featured(kpre[:, head_slice(h)], cs, sn)
-        faded = (values[:, head_slice(h)] * fade_to_end(slope, HEAD)).astype(BF16)
-        old = state[h] * keep
-        st_o[0, h] = old.astype(BF16)
-        state[h] = jnp.exp(jnp.full((1, 2 * HEAD), -slope * CHUNK, F32)) * old + nn(faded.T, key)
+    cs, sn = layout.angles(c, fine, coarse)
+
+    def put(h, value):
+        st_o[0, h] = value
+
+    states_chunk(state.shape[0], slopes, layout.keep(c), kpre, values, cs, sn, state, put)
     fin_o[...] = state[...].astype(BF16)
 
 
-def run_keys(info, slopes, hidden, wk, wv, rot, parts, **ride):
+def run_keys(peers, lengths, slopes, hidden, wk, wv, angles, parts):
     n, d = hidden.shape
     heads, chunks = d // HEAD, n // CHUNK
     turned = (parts // 2, 2, d // parts, n)
     tile = pl.BlockSpec((CHUNK, d), lambda c: (c, 0))
-    outs = [
-        struct((n, d)),
-        struct(turned),
-        struct((n, d)),
-        struct((n, d)),
-        struct((chunks, heads, HEAD, 2 * HEAD)),
-        struct((heads, HEAD, 2 * HEAD)),
-    ]
+    outs = [struct((n, d)), struct(turned), struct((n, d)), struct((n, d)), struct((chunks,) + state_shape(d)), struct(state_shape(d))]
     return launch(
-        functools.partial(keys_kernel, chunks, heads),
+        functools.partial(keys_kernel, peers, n),
         "keys_values_states",
         chunks,
-        [info, slopes, hidden, wk, wv, rot],
-        [smem(), smem(), tile, whole_block(wk.shape), whole_block(wv.shape), pl.BlockSpec((CHUNK, 2 * HEAD), lambda c: (c, 0))],
+        [lengths, slopes, hidden, wk, wv, *angles],
+        [smem(), smem(), tile, whole_block(wk.shape), whole_block(wv.shape)] + [whole_block(a.shape) for a in angles],
         outs,
         [
             tile,
             pl.BlockSpec(turned[:3] + (CHUNK,), lambda c: (0, 0, 0, c)),
             tile,
             tile,
-            pl.BlockSpec((1, heads, HEAD, 2 * HEAD), lambda c: (c, 0, 0, 0)),
-            whole_block((heads, HEAD, 2 * HEAD)),
+            pl.BlockSpec((1,) + state_shape(d), lambda c: (c, 0, 0, 0)),
+            whole_block(state_shape(d)),
         ],
-        [pltpu.VMEM((heads, HEAD, 2 * HEAD), F32)],
+        [pltpu.VMEM(state_shape(d), F32)],
         4 * n * d * d,
-        **ride,
-    )
-
-
-def inside_kernel(chunks, heads, info, slopes, normed, wq, ws, kpre, values, st, rot, qpre_o, sel_o, att_o):
+    )
+
+
+def inside_kernel(peers, count, lengths, slopes, normed, wq, ws, kpre, values, st, fine, coarse, qpre_o, sel_o, att_o):
     c = pl.program_id(0)
+    layout = Layout(lengths, peers, count)
     x = normed[...]
     qpre = nn(x, wq[...])
     qpre_o[...] = qpre.astype(BF16)
     sel_o[...] = nn(x, ws[...]).astype(BF16)
-    cs, sn = rot[:, :HEAD], rot[:, HEAD:]
-    for h in range(heads):
-        slope = slopes[h]
-        query = featured(qpre[:, head_slice(h)], cs, sn)
-        key = featured(kpre[:, head_slice(h)].astype(F32), cs, sn)
-        weights = (nt(query, key) * decay_table(slope, False)).astype(BF16)
-        att_o[:, head_slice(h)] = nn(weights, values[:, head_slice(h)]) + fade_from_start(
-            slope, HEAD
-        ) * nt(query, st[0, h])
-
-
-def run_inside(info, slopes, normed, wq, ws, kpre, values, st, rot, **ride):
+    cs, sn = layout.angles(c, fine, coarse)
+
+    def put(h, value):
+        att_o[:, head_slice(h)] = value
+
+    inside_chunk(
+        st.shape[1],
+        slopes,
+        qpre,
+        lambda h: kpre[:, head_slice(h)],
+        lambda h: values[:, head_slice(h)],
+        lambda h: st[0, h],
+        cs,
+        sn,
+        put,
+    )
+
+
+def run_inside(peers, lengths, slopes, normed, wq, ws, kpre, values, st, angles):
     n, d = normed.shape
-    heads, chunks = d // HEAD, n // CHUNK
+    chunks = n // CHUNK
     tile = pl.BlockSpec((CHUNK, d), lambda c: (c, 0))
-    outs = [struct((n, d)), struct((n, d)), struct((n, d), F32)]
     return launch(
-        functools.partial(inside_kernel, chunks, heads),
+        functools.partial(inside_kernel, peers, n),
         "queries_attention",
         chunks,
-        [info, slopes, normed, wq, ws, kpre, values, st, rot],
+        [lengths, slopes, normed, wq, ws, kpre, values, st, *angles],
+        [smem(), smem(), tile, whole_block(wq.shape), whole_block(ws.shape), tile, tile]
+        + [pl.BlockSpec((1,) + state_shape(d), lambda c: (c, 0, 0, 0))]
+        + [whole_block(a.shape) for a in angles],
+        [struct((n, d)), struct((n, d)), struct((n, d), F32)],
+        [tile, tile, tile],
+        [],
+        6 * n * d * d,
+    )
+
+
+def mix_kernel(peers, count, lengths, slopes, att, qpre, came, sel, wo, hid, cot, fine, coarse, att_o, mixt_o, mid_o, sec_o, sect_o, cott_o, total):
+    c = pl.program_id(0)
+    layout = Layout(lengths, peers, count)
+    cs, sn = layout.angles(c, fine, coarse)
+    carried_chunk(
+        came.shape[0],
+        slopes,
+        layout,
+        c,
+        lambda h: att[:, head_slice(h)],
+        lambda h: qpre[:, head_slice(h)],
+        came,
+        cs,
+        sn,
+        total,
+    )
+    mix_chunk(total, sel[...], wo[...], hid, att_o, mixt_o, mid_o, sec_o, sect_o)
+    cott_o[...] = cot[...].T.reshape(cott_o.shape)
+
+
+def run_mix(peers, lengths, slopes, att, qpre, came, sel, wo, hidden, cot, angles, parts):
+    n, d = hidden.shape
+    chunks = n // CHUNK
+    turned = (parts // 2, 2, d // parts, n)
+    tile = pl.BlockSpec((CHUNK, d), lambda c: (c, 0))
+    turned_tile = pl.BlockSpec(turned[:3] + (CHUNK,), lambda c: (0, 0, 0, c))
+    return launch(
+        functools.partial(mix_kernel, peers, n),
+        "carried_mixed_middle",
+        chunks,
+        [lengths, slopes, att, qpre, came, sel, wo, hidden, cot, *angles],
+        [smem(), smem(), tile, tile, whole_block(came.shape), tile, whole_block(wo.shape), tile, tile]
+        + [whole_block(a.shape) for a in angles],
+        [struct((n, d)), struct(turned), struct((n, d)), struct((n, d)), struct(turned), struct(turned)],
+        [tile, turned_tile, tile, tile, turned_tile, turned_tile],
+        [pltpu.VMEM((CHUNK, d), F32)],
+        3 * n * d * d,
+    )
+
+
+def forward_kernel(chunks, lengths, slopes, hid, cot, fine, coarse, *refs):
+    refs = list(refs)
+    take = lambda k: [refs.pop(0) for _ in range(k)]
+    weights_h = take(5)
+    (kpre_o, val_o, st_o, qpre_o, sel_o) = take(5)
+    (turned_o, att_o, mixt_o, mid_o, sec_o, sect_o, cott_o, came_o) = take(8)
+    (weights, normed, kpre, val, st, qpre, sel, att, state, final, came, total) = take(12)
+    (load_sems, out_sems, state_sems) = take(3)
+    heads = state.shape[0]
+    step = pl.program_id(0)
+    c = lax.rem(step, chunks)
+    here = pl.ds(pl.multiple_of(c * CHUNK, CHUNK), CHUNK)
+    layout = Layout(lengths, 2, chunks * CHUNK)
+    loads = [pltpu.make_async_copy(w, weights.at[i], load_sems.at[i]) for i, w in enumerate(weights_h)]
+    saves = [
+        pltpu.make_async_copy(src, dst, out_sems.at[i])
+        for i, (src, dst) in enumerate([(kpre, kpre_o), (val, val_o), (st, st_o), (qpre, qpre_o), (sel, sel_o)])
+    ]
+    exchange = remote(final, came, state_sems.at[0], state_sems.at[1], "mp", 1)
+
+    @pl.when(step == 0)
+    def _():
+        for copy in loads:
+            copy.start()
+        state[...] = jnp.zeros_like(state)
+        for copy in loads[:2]:
+            copy.wait()
+
+    @pl.when(step < chunks)
+    def _():
+        x = normed_of(hid)
+        normed[here, :] = x
+        turned_o[...] = x.T.reshape(turned_o.shape)
+        keys = nn(x, weights[0])
+        kpre[here, :] = keys.astype(BF16)
+        values = nn(x, weights[1])
+        val[here, :] = values.astype(BF16)
+        cs, sn = layout.angles(c, fine, coarse)
+
+        def put(h, value):
+            st[c, h] = value
+
+        states_chunk(heads, slopes, layout.keep(c), keys, values, cs, sn, state, put)
+
+    @pl.when(step == chunks - 1)
+    def _():
+        final[...] = state[...].astype(BF16)
+        exchange.start()
+        for copy in saves[:3]:
+            copy.start()
+
+    @pl.when(step == chunks)
+    def _():
+        for copy in loads[2:4]:
+            copy.wait()
+
+    @pl.when(jnp.logical_and(step >= chunks, step < 2 * chunks))
+    def _():
+        x = normed[here, :]
+        queries = nn(x, weights[2])
+        qpre[here, :] = queries.astype(BF16)
+        sel[here, :] = nn(x, weights[3]).astype(BF16)
+        cs, sn = layout.angles(c, fine, coarse)
+
+        def put(h, value):
+            att[here, head_slice(h)] = value
+
+        inside_chunk(
+            heads,
+            slopes,
+            queries,
+            lambda h: kpre[here, head_slice(h)],
+            lambda h: val[here, head_slice(h)],
+            lambda h: st[c, h],
+            cs,
+            sn,
+            put,
+        )
+        cott_o[...] = cot[...].T.reshape(cott_o.shape)
+
+    @pl.when(step == 2 * chunks - 1)
+    def _():
+        for copy in saves[3:]:
+            copy.start()
+
+    @pl.when(step == 2 * chunks)
+    def _():
+        loads[4].wait()
+        exchange.wait()
+        came_o[...] = came[...]
+
+    @pl.when(step >= 2 * chunks)
+    def _():
+        cs, sn = layout.angles(c, fine, coarse)
+        carried_chunk(
+            heads,
+            slopes,
+            layout,
+            c,
+            lambda h: att[here, head_slice(h)],
+            lambda h: qpre[here, head_slice(h)],
+            came,
+            cs,
+            sn,
+            total,
+        )
+        mix_chunk(total, sel[here, :], weights[4], hid, att_o, mixt_o, mid_o, sec_o, sect_o)
+
+    @pl.when(step == 3 * chunks - 1)
+    def _():
+        for copy in saves:
+            copy.wait()
+
+
+def run_forward(lengths, slopes, hidden, cot, weights, angles, parts, guests, ident):
+    n, d = hidden.shape
+    chunks = n // CHUNK
+    turned = (parts // 2, 2, d // parts, n)
+    late = lambda s: jnp.maximum(s - 2 * chunks, 0)
+    mid = lambda s: jnp.clip(s - chunks, 0, chunks - 1)
+    early = lambda s: jnp.minimum(s, chunks - 1)
+    tile = pl.BlockSpec((CHUNK, d), lambda s: (late(s), 0))
+    turned_tile = lambda at: pl.BlockSpec(turned[:3] + (CHUNK,), lambda s: (0, 0, 0, at(s)))
+    whole = pltpu.VMEM((n, d), BF16)
+    return launch(
+        functools.partial(forward_kernel, chunks),
+        "forward_to_sglu",
+        3 * chunks,
+        [lengths, slopes, hidden, cot, *angles, *weights],
         [
             smem(),
             smem(),
-            tile,
-            whole_block(wq.shape),
-            whole_block(ws.shape),
-            tile,
-            tile,
-            pl.BlockSpec((1, heads, HEAD, 2 * HEAD), lambda c: (c, 0, 0, 0)),
-            pl.BlockSpec((CHUNK, 2 * HEAD), lambda c: (c, 0)),
+            pl.BlockSpec((CHUNK, d), lambda s: (jnp.where(s < 2 * chunks, early(s), late(s)), 0)),
+            pl.BlockSpec((CHUNK, d), lambda s: (mid(s), 0)),
+        ]
+        + [whole_block(a.shape) for a in angles]
+        + [anywhere()] * 5,
+        [struct((n, d)), struct((n, d)), struct((chunks,) + state_shape(d)), struct((n, d)), struct((n, d))]
+        + [struct(turned), struct((n, d)), struct(turned), struct((n, d)), struct((n, d)), struct(turned), struct(turned)]
+        + [struct(state_shape(d))],
+        [anywhere()] * 5
+        + [turned_tile(early), tile, turned_tile(late), tile, tile, turned_tile(late), turned_tile(mid)]
+        + [whole_block(state_shape(d))],
+        [
+            pltpu.VMEM((5, d, d), BF16),
+            whole,
+            whole,
+            whole,
+            pltpu.VMEM((chunks,) + state_shape(d), BF16),
+            whole,
+            whole,
+            pltpu.VMEM((n, d), F32),
+            pltpu.VMEM(state_shape(d), F32),
+            pltpu.VMEM(state_shape(d), BF16),
+            pltpu.VMEM(state_shape(d), BF16),
+            pltpu.VMEM((CHUNK, d), F32),
+            pltpu.SemaphoreType.DMA((5,)),
+            pltpu.SemaphoreType.DMA((5,)),
+            pltpu.SemaphoreType.DMA((2,)),
         ],
-        outs,
-        [tile, tile, tile],
-        [],
-        6 * n * d * d,
-        **ride,
-    )
-
-
-def mix_kernel(chunks, heads, info, slopes, att, qpre, came, sel, wo, hid, cot, rot, att_o, mixt_o, mid_o, sec_o, sect_o, cott_o, total):
-    c = pl.program_id(0)
-    cs, sn = rot[:, :HEAD], rot[:, HEAD:]
-    reached = info[2 * chunks + c].astype(F32)
-    lag = (c * CHUNK).astype(F32)
-    alive = (row_index((CHUNK, HEAD)) + c * CHUNK < info[4 * chunks]).astype(F32)
-    for h in range(heads):
-        slope = slopes[h]
-        query = featured(qpre[:, head_slice(h)].astype(F32), cs, sn)
-        fade = jnp.exp(-slope * (row_index((CHUNK, HEAD)).astype(F32) + (lag + 1.0))) * reached
-        total[:, head_slice(h)] = (att[:, head_slice(h)] + fade * nt(query, came[h])) * alive
-    attended = total[...]
-    att_o[...] = attended.astype(BF16)
-    mixed = (attended * scale_of(attended) * sel[...].astype(F32)).astype(BF16)
-    mixt_o[...] = mixed.T.reshape(mixt_o.shape)
-    middle = hid[...].astype(F32) + nn(mixed, wo[...])
-    mid_o[...] = middle
-    second = (middle * scale_of(middle)).astype(BF16)
-    sec_o[...] = second
-    sect_o[...] = second.T.reshape(sect_o.shape)
-    cott_o[...] = cot[...].T.reshape(cott_o.shape)
-
-
-def run_mix(info, slopes, att, qpre, came, sel, wo, hidden, cot, rot, parts, **ride):
-    n, d = hidden.shape
-    heads, chunks = d // HEAD, n // CHUNK
-    turned = (parts // 2, 2, d // parts, n)
-    tile = pl.BlockSpec((CHUNK, d), lambda c: (c, 0))
-    turned_tile = pl.BlockSpec(turned[:3] + (CHUNK,), lambda c: (0, 0, 0, c))
-    outs = [
-        struct((n, d)),
-        struct(turned),
-        struct((n, d), F32),
-        struct((n, d)),
-        struct(turned),
-        struct(turned),
-    ]
-    return launch(
-        functools.partial(mix_kernel, chunks, heads),
-        "carried_mixed_middle",
-        chunks,
-        [info, slopes, att, qpre, came, sel, wo, hidden, cot, rot],
-        [
-            smem(),
-            smem(),
-            tile,
-            tile,
-            whole_block(came.shape),
-            tile,
-            whole_block(wo.shape),
-            tile,
-            tile,
-            pl.BlockSpec((CHUNK, 2 * HEAD), lambda c: (c, 0)),
-        ],
-        outs,
-        [tile, turned_tile, tile, tile, turned_tile, turned_tile],
-        [pltpu.VMEM((CHUNK, d), F32)],
-        3 * n * d * d,
-        **ride,
+        12 * n * d * d,
+        guests=guests,
+        ident=ident,
+        partners=[("mp", 1)],
     )
 
 
@@ -562,21 +770,24 @@
     )
 
 
-def units_kernel(geo, reducer, ride, first_weight, second_weight, down_weight, x, *refs):
-    blocks, cut, d, units = geo["blocks"], geo["cut"], geo["d"], geo["units"]
+def units_kernel(geo, reducer, ride, lengths, slopes, first_weight, second_weight, down_weight, x, *refs):
+    blocks, cut, d, units, chunks = geo["blocks"], geo["cut"], geo["d"], geo["units"], geo["chunks"]
     refs = list(refs)
     take = lambda k: [refs.pop(0) for _ in range(k)]
-    cot_h, xt_h, cott_h = take(3)
+    (mid, sel, att, qpre, fine, coarse) = take(6)
+    cot_h, xt_h, cott_h, wo_h = take(4)
     pieces = take(12)
     had_b = take(3)
-    term_o, part_o, out = take(3)
+    (out_o, gmid_o, gsel_o, gatt_o, et_o, e0_o, sums_o) = take(7)
     pieces = pieces + had_b + take(9)
-    term, part, cot, xt, cott, o1, o2, od, c1, c2, cd, sems, out_sems = take(13)
+    term, part, cot, xt, cott, o1, o2, od, c1, c2, cd, state, sums, sems, own_sems, wo_sems = take(16)
     reducer.bind(take(len(reducer.scratch)))
     step = pl.program_id(0)
     ride.before(step, had_b, pieces[15:], refs)
     core = lax.rem(lax.axis_index("dp"), 2)
     eighth = lax.rem(lax.axis_index("dp"), 8)
+    heads = state.shape[0]
+    layout = Layout(lengths, 2, chunks * CHUNK)
 
     def fetch(g):
         size = cut if g == 0 else units - cut
@@ -593,16 +804,21 @@
         return copies
 
     own = [
-        pltpu.make_async_copy(cot_h, cot, out_sems.at[2]),
-        pltpu.make_async_copy(xt_h.at[:, 1 - core], xt.at[0], out_sems.at[3]),
-        pltpu.make_async_copy(xt_h.at[:, core], xt.at[1], out_sems.at[4]),
-        pltpu.make_async_copy(cott_h.at[:, 1 - core], cott.at[0], out_sems.at[5]),
-        pltpu.make_async_copy(cott_h.at[:, core], cott.at[1], out_sems.at[6]),
+        pltpu.make_async_copy(cot_h, cot, own_sems.at[0]),
+        pltpu.make_async_copy(xt_h.at[:, 1 - core], xt.at[0], own_sems.at[1]),
+        pltpu.make_async_copy(xt_h.at[:, core], xt.at[1], own_sems.at[2]),
+        pltpu.make_async_copy(cott_h.at[:, 1 - core], cott.at[0], own_sems.at[3]),
+        pltpu.make_async_copy(cott_h.at[:, core], cott.at[1], own_sems.at[4]),
     ]
-    done = [
-        pltpu.make_async_copy(term, term_o, out_sems.at[0]),
-        pltpu.make_async_copy(part, part_o, out_sems.at[1]),
+    pairs, rows = xt.shape[1], xt.shape[2]
+    out_weight = [
+        pltpu.make_async_copy(
+            wo_h.at[pl.ds((k * pairs + i) * rows, rows), :], xt.at[k, i], wo_sems.at[k * pairs + i]
+        )
+        for k in range(2)
+        for i in range(pairs)
     ]
+    saved = pltpu.make_async_copy(sums, sums_o, own_sems.at[5])
     turn = cut // HEAD
 
     @pl.when(step == 0)
@@ -611,6 +827,7 @@
             copy.start()
         term[...] = jnp.zeros_like(term)
         part[...] = jnp.zeros_like(part)
+        state[...] = jnp.zeros_like(state)
         for copy in fetch(0):
             copy.wait()
 
@@ -660,16 +877,36 @@
 
     @pl.when(step == blocks - 1)
     def _():
-        for copy in done:
+        for copy in out_weight:
             copy.start()
 
+    @pl.when(step == blocks)
+    def _():
+        for copy in out_weight:
+            copy.wait()
+
+    @pl.when(jnp.logical_and(step >= blocks, step < blocks + chunks))
+    def _():
+        c = chunks - 1 - (step - blocks)
+        here = pl.ds(pl.multiple_of(c * CHUNK, CHUNK), CHUNK)
+        cs, sn = layout.angles(c, fine, coarse)
+        wo = xt[...].reshape(d, d)
+        after_chunk(
+            layout, c, heads, slopes, term[here, :], part[here, :], cot[here, :], mid, sel, att, wo, qpre, cs, sn,
+            out_o, gmid_o, gsel_o, gatt_o, et_o, state,
+        )
+
+    @pl.when(step == blocks + chunks - 1)
+    def _():
+        e0_o[...] = state[...].astype(BF16)
+
     ride.after(step, had_b, pieces[15:], refs)
-    reducer.run(step, out)
+    reducer.run(step, sums)
 
     @pl.when(step == reducer.last)
     def _():
-        for copy in done:
-            copy.wait()
+        saved.start()
+        saved.wait()
 
 
 def rows_of(ref, k):
@@ -677,26 +914,37 @@
     return block.reshape(block.shape[0] * block.shape[1], block.shape[2])
 
 
-def run_units(matrices, second, cot, second_t, cot_t, pieces, ride, cut, depth, ident):
+def run_units(lengths, slopes, matrices, second, cot, second_t, cot_t, rows_in, angles, wo, pieces, ride, cut, depth, ident):
     n, d = second.shape
+    chunks = n // CHUNK
     units = matrices[0].shape[1]
     blocks = units // HEAD
     pairs, _, rows, _ = second_t.shape
     reducer = Reducer(0, blocks, 3, depth, rows, (1, 3, 5, 7))
-    geo = dict(blocks=blocks, cut=cut, d=d, units=units)
+    geo = dict(blocks=blocks, cut=cut, d=d, units=units, chunks=chunks)
     at = lambda s: jnp.minimum(s, blocks - 1)
+    back = lambda s: chunks - 1 - jnp.clip(s - blocks, 0, chunks - 1)
+    tile = pl.BlockSpec((CHUNK, d), lambda s: (back(s), 0))
     columns = pl.BlockSpec((d, HEAD), lambda s: (0, at(s)))
     turned = pltpu.VMEM((2, pairs, rows, n), BF16)
     size = max(cut, units - cut)
+    sums = (3, rows, units)
     return launch(
         functools.partial(units_kernel, geo, reducer, ride),
         "sglu_and_gradients",
-        reducer.last + 1,
-        list(matrices) + [second, cot, second_t, cot_t] + list(pieces) + ride.inputs,
-        [columns, columns, pl.BlockSpec((HEAD, d), lambda s: (at(s), 0)), once(second.shape)]
-        + [anywhere()] * (3 + len(pieces) + len(ride.inputs)),
-        [struct((n, d), F32), struct((n, d), F32), struct((3, rows, units), F32)] + ride.outs,
-        [anywhere(), anywhere(), whole_block((3, rows, units))] + [anywhere()] * len(ride.outs),
+        max(reducer.last, blocks + chunks - 1) + 1,
+        [lengths, slopes] + list(matrices) + [second] + list(rows_in) + list(angles)
+        + [cot, second_t, cot_t, wo] + list(pieces) + ride.inputs,
+        [smem(), smem(), columns, columns, pl.BlockSpec((HEAD, d), lambda s: (at(s), 0)), once(second.shape)]
+        + [tile] * 4
+        + [once(a.shape) for a in angles]
+        + [anywhere()] * (4 + len(pieces) + len(ride.inputs)),
+        [struct((n, d))] * 4
+        + [struct((chunks,) + state_shape(d)), struct(state_shape(d)), struct(sums, F32)]
+        + ride.outs,
+        [tile] * 4
+        + [pl.BlockSpec((1,) + state_shape(d), lambda s: (back(s), 0, 0, 0)), whole_block(state_shape(d))]
+        + [anywhere()] * (1 + len(ride.outs)),
         [
             pltpu.VMEM((n, d), F32),
             pltpu.VMEM((n, d), F32),
@@ -709,40 +957,33 @@
             pltpu.VMEM((d, 2 * HEAD), BF16),
             pltpu.VMEM((d, 2 * HEAD), BF16),
             pltpu.VMEM((2 * HEAD, d), BF16),
+            pltpu.VMEM(state_shape(d), F32),
+            pltpu.VMEM(sums, F32),
             pltpu.SemaphoreType.DMA((2, 3, 8)),
-            pltpu.SemaphoreType.DMA((7,)),
+            pltpu.SemaphoreType.DMA((6,)),
+            pltpu.SemaphoreType.DMA((2 * pairs,)),
         ]
         + reducer.scratch
         + ride.scratch,
         36 * n * d * units,
         partners=reducer.partners + ride.partners,
         ident=ident,
-    )[:3]
-
-
-def after_kernel(chunks, heads, info, slopes, term, part, cot, mid, sel, att, wo, qpre, rot, out_o, gmid_o, pair_o, gatt_o, et_o, e0_o, state):
-    step = pl.program_id(0)
-    c = chunks - 1 - step
-
-    @pl.when(step == 0)
-    def _():
-        state[...] = jnp.zeros_like(state)
-
-    middle = mid[...]
-    out_o[...] = (middle + term[...]).astype(BF16)
-    grad_middle = cot[...].astype(F32) + norm_back(middle, scale_of(middle), part[...])
-    gmid_o[...] = grad_middle
+    )[:7]
+
+
+def after_chunk(layout, c, heads, slopes, term, part, cot, mid, sel, att, wo, qpre, cs, sn, out_o, gmid_o, pair_o, gatt_o, et_o, state):
+    middle = mid[...].astype(F32)
+    out_o[...] = (middle + term).astype(BF16)
+    grad_middle = cot.astype(F32) + norm_back(middle, scale_of(middle), part)
     branch = grad_middle.astype(BF16)
-    pair_o[0] = branch
-    grad_mixed = nt(branch, wo[...])
+    gmid_o[...] = branch
+    grad_mixed = nt(branch, wo)
     attended = att[...].astype(F32)
     scale = scale_of(attended)
-    pair_o[1] = (grad_mixed * attended * scale).astype(BF16)
-    alive = (row_index((CHUNK, 1)) + c * CHUNK < info[4 * chunks]).astype(F32)
-    grad_att = norm_back(attended, scale, grad_mixed * sel[...].astype(F32)) * alive
+    pair_o[...] = (grad_mixed * attended * scale).astype(BF16)
+    grad_att = norm_back(attended, scale, grad_mixed * sel[...].astype(F32)) * layout.alive(c, 1)
     gatt_o[...] = grad_att.astype(BF16)
-    cs, sn = rot[:, :HEAD], rot[:, HEAD:]
-    keep = info[chunks + c].astype(F32)
+    keep = layout.keep(c)
     for h in range(heads):
         slope = slopes[h]
         query = featured(qpre[:, head_slice(h)].astype(F32), cs, sn)
@@ -752,41 +993,41 @@
         state[h] = keep * (
             jnp.exp(jnp.full((1, 2 * HEAD), -slope * CHUNK, F32)) * old + nn(faded.T, query)
         )
+
+
+def after_kernel(peers, count, lengths, slopes, term, part, cot, mid, sel, att, wo, qpre, fine, coarse, out_o, gmid_o, gsel_o, gatt_o, et_o, e0_o, state):
+    step = pl.program_id(0)
+    c = count // CHUNK - 1 - step
+    layout = Layout(lengths, peers, count)
+
+    @pl.when(step == 0)
+    def _():
+        state[...] = jnp.zeros_like(state)
+
+    cs, sn = layout.angles(c, fine, coarse)
+    after_chunk(
+        layout, c, state.shape[0], slopes, term[...], part[...], cot[...], mid, sel, att, wo[...], qpre, cs, sn,
+        out_o, gmid_o, gsel_o, gatt_o, et_o, state,
+    )
     e0_o[...] = state[...].astype(BF16)
 
 
-def run_after(info, slopes, term, part, cot, mid, sel, att, wo, qpre, rot, **ride):
+def run_after(peers, lengths, slopes, term, part, cot, mid, sel, att, wo, qpre, angles):
     n, d = cot.shape
-    heads, chunks = d // HEAD, n // CHUNK
+    chunks = n // CHUNK
     back = lambda s: chunks - 1 - s
     tile = pl.BlockSpec((CHUNK, d), lambda s: (back(s), 0))
     return launch(
-        functools.partial(after_kernel, chunks, heads),
+        functools.partial(after_kernel, peers, n),
         "output_and_row_gradients",
         chunks,
-        [info, slopes, term, part, cot, mid, sel, att, wo, qpre, rot],
-        [smem(), smem()]
-        + [tile] * 6
-        + [whole_block(wo.shape), tile, pl.BlockSpec((CHUNK, 2 * HEAD), lambda s: (back(s), 0))],
-        [
-            struct((n, d)),
-            struct((n, d), F32),
-            struct((2, n, d)),
-            struct((n, d)),
-            struct((chunks, heads, HEAD, 2 * HEAD)),
-            struct((heads, HEAD, 2 * HEAD)),
-        ],
-        [
-            tile,
-            tile,
-            pl.BlockSpec((2, CHUNK, d), lambda s: (0, back(s), 0)),
-            tile,
-            pl.BlockSpec((1, heads, HEAD, 2 * HEAD), lambda s: (back(s), 0, 0, 0)),
-            whole_block((heads, HEAD, 2 * HEAD)),
-        ],
-        [pltpu.VMEM((heads, HEAD, 2 * HEAD), F32)],
+        [lengths, slopes, term, part, cot, mid, sel, att, wo, qpre, *angles],
+        [smem(), smem()] + [tile] * 6 + [whole_block(wo.shape), tile] + [whole_block(a.shape) for a in angles],
+        [struct((n, d))] * 4 + [struct((chunks,) + state_shape(d)), struct(state_shape(d))],
+        [tile] * 4
+        + [pl.BlockSpec((1,) + state_shape(d), lambda s: (back(s), 0, 0, 0)), whole_block(state_shape(d))],
+        [pltpu.VMEM(state_shape(d), F32)],
         3 * n * d * d,
-        **ride,
     )
 
 
@@ -845,15 +1086,16 @@
     return gq, gk, dv.astype(BF16)
 
 
-def attention_back_kernel(chunks, first_head, info, slopes, qpre, kpre, values, gatt, st, came, et, left, rot, grads_o):
+def attention_back_kernel(peers, count, lengths, slopes, qpre, kpre, values, gatt, st, came, et, left, fine, coarse, grads_o):
+    chunks = count // CHUNK
+    layout = Layout(lengths, peers, count)
     pair, c = lax.div(pl.program_id(0), chunks), lax.rem(pl.program_id(0), chunks)
-    cs, sn = rot[:, :HEAD], rot[:, HEAD:]
-    before = info[2 * chunks + c].astype(F32)
-    after = info[3 * chunks + c].astype(F32)
+    cs, sn = layout.angles(c, fine, coarse)
+    before, after = layout.before(c), layout.after(c)
     span = (CHUNK * c).astype(F32)
     rest = (CHUNK * (chunks - 1 - c)).astype(F32)
     for h in range(2):
-        slope = slopes[first_head + 2 * pair + h]
+        slope = slopes[2 * pair + h]
         cols = head_slice(h)
         lane = jnp.zeros((1, 2 * HEAD), F32)
         state = st[0, h].astype(F32) + came[h].astype(F32) * (jnp.exp(lane - slope * span) * before)
@@ -865,36 +1107,34 @@
             grads_o[i, :, cols] = three[i]
 
 
-def run_attention_back(info, slopes, qpre, kpre, values, gatt, st, came, et, left, rot, first_head, heads, **ride):
+def run_attention_back(peers, lengths, slopes, qpre, kpre, values, gatt, st, came, et, left, angles):
     n, d = qpre.shape
     chunks = n // CHUNK
-    skip = first_head // 2
     pair = lambda s: lax.div(s, chunks)
     chunk = lambda s: lax.rem(s, chunks)
-    tile = pl.BlockSpec((CHUNK, 2 * HEAD), lambda s: (chunk(s), skip + pair(s)))
-    states = pl.BlockSpec((1, 2, HEAD, 2 * HEAD), lambda s: (chunk(s), skip + pair(s), 0, 0))
-    ends = pl.BlockSpec((2, HEAD, 2 * HEAD), lambda s: (skip + pair(s), 0, 0))
+    tile = pl.BlockSpec((CHUNK, 2 * HEAD), lambda s: (chunk(s), pair(s)))
+    states = pl.BlockSpec((1, 2, HEAD, 2 * HEAD), lambda s: (chunk(s), pair(s), 0, 0))
+    ends = pl.BlockSpec((2, HEAD, 2 * HEAD), lambda s: (pair(s), 0, 0))
     return launch(
-        functools.partial(attention_back_kernel, chunks, first_head),
+        functools.partial(attention_back_kernel, peers, n),
         "attention_backward",
-        chunks * heads // 2,
-        [info, slopes, qpre, kpre, values, gatt, st, came, et, left, rot],
-        [smem(), smem(), tile, tile, tile, tile, states, ends, states, ends, pl.BlockSpec((CHUNK, 2 * HEAD), lambda s: (chunk(s), 0))],
-        [struct((3, n, heads * HEAD))],
+        chunks * d // (2 * HEAD),
+        [lengths, slopes, qpre, kpre, values, gatt, st, came, et, left, *angles],
+        [smem(), smem(), tile, tile, tile, tile, states, ends, states, ends] + [whole_block(a.shape) for a in angles],
+        [struct((3, n, d))],
         [pl.BlockSpec((3, CHUNK, 2 * HEAD), lambda s: (0, chunk(s), pair(s)))],
         [],
-        18 * n * 256 * 256 * heads // 2,
-        **ride,
-    )
-
-
-def projections_kernel(geo, outer, inner, info, slopes, *refs):
+        18 * n * 256 * d,
+    )
+
+
+def projections_kernel(geo, outer, inner, lengths, slopes, *refs):
     chunks, blocks, d, n = geo["chunks"], geo["blocks"], geo["d"], geo["n"]
     refs = list(refs)
     take = lambda k: [refs.pop(0) for _ in range(k)]
     columns = [take(2) for _ in range(4)]
     states = [take(2) for _ in range(2)]
-    (came, leaving, rot, branch_a, branch_b, sel_a, sel_b, sel, hid, gmid, mixt_h, normt_h) = take(12)
+    (came, leaving, fine, coarse, branch_a, branch_b, sel_a, sel_b, sel, hid, gmid, mixt_h, normt_h) = take(13)
     weights_h = take(4)
     hidden_o, out, out2 = take(3)
     grads, block, mixt, normt, w4, left, sems, state_sems = take(8)
@@ -903,6 +1143,7 @@
     step = pl.program_id(0)
     core = lax.rem(lax.axis_index("dp"), 2)
     me = lax.axis_index("mp")
+    layout = Layout(lengths, 2, n)
     loads = [
         pltpu.make_async_copy(mixt_h.at[:, 1 - core], mixt.at[0], sems.at[0]),
         pltpu.make_async_copy(mixt_h.at[:, core], mixt.at[1], sems.at[1]),
@@ -910,11 +1151,19 @@
         pltpu.make_async_copy(normt_h.at[:, core], normt.at[1], sems.at[3]),
     ]
     matrices = [pltpu.make_async_copy(w, w4.at[i], sems.at[4 + i]) for i, w in enumerate(weights_h)]
-    exchange = remote(leaving, left, state_sems.at[0], state_sems.at[1], "mp", 1)
+
+    def exchange(j):
+        pair = []
+        for k in range(2):
+            h = k * blocks + j
+            pair.append(remote(leaving.at[h], left.at[h], state_sems.at[0, h], state_sems.at[1, h], "mp", 1))
+        return pair
 
     @pl.when(step == 0)
     def _():
-        exchange.start()
+        for j in range(blocks):
+            for copy in exchange(j):
+                copy.start()
         for copy in loads:
             copy.start()
         for copy in matrices:
@@ -933,19 +1182,16 @@
             if k == 0:
                 outer.begin(step)
 
-    @pl.when(step == blocks - 1)
-    def _():
-        exchange.wait()
-
     @pl.when(jnp.logical_and(step >= blocks, step < 2 * blocks))
     def _():
         j = step - blocks
+        for copy in exchange(j):
+            copy.wait()
 
         def one(c, carry):
             here = pl.ds(pl.multiple_of(c * CHUNK, CHUNK), CHUNK)
-            cs, sn = rot[here, :HEAD], rot[here, HEAD:]
-            before = info[2 * chunks + c].astype(F32)
-            after = info[3 * chunks + c].astype(F32)
+            cs, sn = layout.angles(c, fine, coarse)
+            before, after = layout.before(c), layout.after(c)
             span = (CHUNK * c).astype(F32)
             rest = (CHUNK * (chunks - 1 - c)).astype(F32)
             for side in range(2):
@@ -983,13 +1229,13 @@
         for i in range(3):
             total = total + nt(grads[i, here, :], w4[i])
         x = hid[...].astype(F32)
-        hidden_o[...] = (gmid[...] + norm_back(x, scale_of(x), total)).astype(BF16)
+        hidden_o[...] = (gmid[...].astype(F32) + norm_back(x, scale_of(x), total)).astype(BF16)
 
     outer.run(step, out)
     inner.run(step, out2)
 
 
-def run_projections(info, slopes, qpre, kpre, values, gatt, st, et, came, leaving, rot, pair, hidden, gmid, mixed_t, normed_t, weights, depth, ident):
+def run_projections(lengths, slopes, qpre, kpre, values, gatt, st, et, came, leaving, angles, gsel, hidden, gmid, mixed_t, normed_t, weights, depth, ident):
     n, d = qpre.shape
     heads, chunks = d // HEAD, n // CHUNK
     blocks = heads // 2
@@ -1004,23 +1250,24 @@
     side = lambda k: blocks * (lax.axis_index("mp") if k == 0 else 1 - lax.axis_index("mp"))
     column = lambda k: pl.BlockSpec((n, HEAD), lambda s: (0, side(k) + mid(s)))
     state = lambda k: pl.BlockSpec((chunks, 1, HEAD, 2 * HEAD), lambda s: (0, side(k) + mid(s), 0, 0))
-    pair_column = lambda i, k: pl.BlockSpec((None, n, HEAD), lambda s: (i, 0, side(k) + early(s)))
+    early_column = lambda k: pl.BlockSpec((n, HEAD), lambda s: (0, side(k) + early(s)))
     tile = pl.BlockSpec((CHUNK, d), lambda s: (late(s), 0))
     turned = pltpu.VMEM((2, pairs, rows, n), BF16)
     return launch(
         functools.partial(projections_kernel, geo, outer, inner),
         "attention_backward_and_gradients",
         steps,
-        [info, slopes]
+        [lengths, slopes]
         + [a for a in (qpre, kpre, values, gatt, st, et) for _ in range(2)]
-        + [came, leaving, rot, pair, pair, pair, pair, pair, hidden, gmid, mixed_t, normed_t]
+        + [came, leaving, *angles, gmid, gmid, gsel, gsel, gsel, hidden, gmid, mixed_t, normed_t]
         + list(weights),
         [smem(), smem()]
         + [column(k) for _ in range(4) for k in range(2)]
         + [state(k) for _ in range(2) for k in range(2)]
-        + [once(came.shape), anywhere(), once(rot.shape)]
-        + [pair_column(i, k) for i in range(2) for k in range(2)]
-        + [pl.BlockSpec((None, CHUNK, d), lambda s: (1, late(s), 0)), tile, tile]
+        + [once(came.shape), anywhere()]
+        + [once(a.shape) for a in angles]
+        + [early_column(k) for _ in range(2) for k in range(2)]
+        + [tile, tile, tile]
         + [anywhere()] * 6,
         [struct((n, d)), struct((2, rows, d // 2), F32), struct((3, rows, d // 2), F32)],
         [tile, whole_block((2, rows, d // 2)), whole_block((3, rows, d // 2))],
@@ -1032,7 +1279,7 @@
             pltpu.VMEM((4, d, d), BF16),
             pltpu.VMEM(leaving.shape, BF16),
             pltpu.SemaphoreType.DMA((8,)),
-            pltpu.SemaphoreType.DMA((2,)),
+            pltpu.SemaphoreType.DMA((2, heads)),
         ]
         + outer.scratch
         + inner.scratch,
@@ -1042,24 +1289,24 @@
     )
 
 
-def input_kernel(wq, wk, wv, ws, grads, pair, hid, gmid, out):
-    total = nt(grads[0], wq[...]) + nt(grads[1], wk[...]) + nt(grads[2], wv[...]) + nt(pair[...], ws[...])
+def input_kernel(wq, wk, wv, ws, grads, gsel, hid, gmid, out):
+    total = nt(grads[0], wq[...]) + nt(grads[1], wk[...]) + nt(grads[2], wv[...]) + nt(gsel[...], ws[...])
     x = hid[...].astype(F32)
-    out[...] = (gmid[...] + norm_back(x, scale_of(x), total)).astype(BF16)
-
-
-def run_input(weights, grads, pair, hidden, gmid, **ride):
+    out[...] = (gmid[...].astype(F32) + norm_back(x, scale_of(x), total)).astype(BF16)
+
+
+def run_input(weights, grads, gsel, hidden, gmid):
     n, d = hidden.shape
     tile = pl.BlockSpec((CHUNK, d), lambda c: (c, 0))
     return launch(
         input_kernel,
         "input_gradient",
         n // CHUNK,
-        list(weights) + [grads, pair, hidden, gmid],
+        list(weights) + [grads, gsel, hidden, gmid],
         [whole_block(w.shape) for w in weights]
         + [
             pl.BlockSpec((3, CHUNK, d), lambda c: (0, c, 0)),
-            pl.BlockSpec((None, CHUNK, d), lambda c: (1, c, 0)),
+            tile,
             tile,
             tile,
         ],
@@ -1067,7 +1314,6 @@
         [tile],
         [],
         8 * n * d * d,
-        **ride,
     )
 
 
@@ -1099,9 +1345,8 @@
     depth = parts // 4
     group = count * peers
     units = first_weight.shape[1]
-    lengths = doc_lengths[0].astype(jnp.int32)
-    info = chunk_info(lengths, me, peers, count)
-    rot = turning(info, chunks, group // 2)
+    lengths = doc_lengths.astype(jnp.int32)
+    angles = tables(group // 2)
     slopes = decay_slope
     matrices = (first_weight, second_weight, down_weight)
     riding = peers == 2
@@ -1115,7 +1360,7 @@
     def like(arrays, count=None):
         return [struct(a.shape if count is None else (count,) + a.shape) for a in arrays]
 
-    def over_mp(g, steps):
+    def over_mp(g):
         low, size = ranges[g]
 
         def source(w):
@@ -1130,17 +1375,16 @@
             return src
 
         outs = [struct((d // 8, size)), struct((d // 8, size)), struct((size // 8, d))]
-        copies = [(source(w), lambda i, o, w=w: o[w], "mp", 1) for w in range(3)]
-        return Carry(matrices, outs, [(0, steps, copies)])
-
-    def near(w):
+        return outs, [(source(w), lambda i, o, w=w: o[w], "mp", 1) for w in range(3)]
+
+    def near(src, dst):
         return [
-            (lambda i, o: i[w], lambda i, o: o[w].at[0], "dp", 2),
-            (lambda i, o: i[w], lambda i, o: o[w].at[1], "dp", 4),
-            (lambda i, o: i[w], lambda i, o: o[w].at[2], "dp", 1),
+            (lambda i, o: src(i, o), lambda i, o: dst(i, o).at[0], "dp", 2),
+            (lambda i, o: src(i, o), lambda i, o: dst(i, o).at[1], "dp", 4),
+            (lambda i, o: src(i, o), lambda i, o: dst(i, o).at[2], "dp", 1),
         ]
 
-    def far(w, src, dst, rows):
+    def far(src, dst, rows):
         top = -(-rows // 32) * 16
         upper, lower = pl.ds(0, top), pl.ds(top, rows - top)
         return [
@@ -1150,94 +1394,74 @@
             (lambda i, o: src(i, o).at[1], lambda i, o: dst(i, o).at[2], "dp", 1),
         ]
 
-    ride = dict(guests=[over_mp(0, chunks - 1)], ident=1) if riding else {}
-    normed, normed_t, kpre, values, st, final, *had = run_keys(
-        info, slopes, hidden_in, key_weight, value_weight, rot, parts, **ride
-    )
-    whole_keep = info[2 * chunks + chunks - 1].astype(F32)
-    decay = jnp.exp(-slopes * count)
-    ride = {}
+    def onward(pieces, out, at):
+        ref = lambda k: lambda i, o: o[k]
+        one, two, three = [], [], []
+        for w in range(3):
+            one += near(pieces(w), ref(at + w))
+            two += far(ref(at + w), ref(at + 3 + w), out[w].shape[0])
+            three.append((lambda i, o, w=w: o[at + 3 + w].at[0], ref(at + 6 + w), "dp", 1))
+        return like(out, 3) + like(out, 3) + like(out), [one, two, three]
+
     if riding:
-        state_copy = [(lambda i, o: i[0], lambda i, o: o[0], "mp", 1)]
-        near_copies = [c for w in range(3) for c in near(w)]
-        ride = dict(
-            guests=[
-                Carry([final], like([final]), [(0, chunks - 1, state_copy)]),
-                Carry(had, like(had, 3), [(0, chunks - 1, near_copies)]),
-            ],
-            ident=2,
+        outs, copies = over_mp(0)
+        more, phases = onward(lambda w: lambda i, o: o[w], outs, 3)
+        outs_b, copies_b = over_mp(1)
+        spans = [(0, chunks), (chunks + 1, 2 * chunks), (2 * chunks + 1, 3 * chunks - 2), (3 * chunks - 1,) * 2]
+        guests = [
+            Carry(matrices, outs + more, [span + (c,) for span, c in zip(spans, [copies] + phases)]),
+            Carry(matrices, outs_b, [(chunks + 2, 3 * chunks - 1, copies_b)]),
+        ]
+        weights = [key_weight, value_weight, query_weight, select_weight, out_weight]
+        kpre, values, st, qpre, sel, normed_t, attended, mixed_t, middle, second, second_t, cot_t, came, *got = run_forward(
+            lengths, slopes, hidden_in, cotangent, weights, angles, parts, guests, ident=1
         )
-    qpre, sel, att, *more = run_inside(
-        info, slopes, normed, query_weight, select_weight, kpre, values, st, rot, **ride
-    )
-    if riding:
-        came, close = more[0], more[1:]
     else:
+        normed, normed_t, kpre, values, st, final = run_keys(
+            peers, lengths, slopes, hidden_in, key_weight, value_weight, angles, parts
+        )
+        begin, start, last = jnp.int32(0), jnp.int32(0), (me + 1) * count - CHUNK
+        for i in range(lengths.shape[1]):
+            begin = jnp.where(last >= start, start, begin)
+            start = start + lengths[0, i]
+        passes = (begin < me * count).astype(F32)
+        decay = jnp.exp(-slopes * count)
         finals = lax.all_gather(final, "mp")
-        keeps = lax.all_gather(whole_keep.reshape(1), "mp")[:, 0]
+        keeps = lax.all_gather(passes.reshape(1), "mp")[:, 0]
 
         def ahead(k, total):
             new = finals[k].astype(F32) + (keeps[k] * decay)[:, None, None] * total
             return jnp.where(k < me, new, total)
 
         came = lax.fori_loop(0, peers, ahead, jnp.zeros(final.shape, F32)).astype(BF16)
-    ride = {}
+        qpre, sel, att = run_inside(
+            peers, lengths, slopes, normed, query_weight, select_weight, kpre, values, st, angles
+        )
+        attended, mixed_t, middle, second, second_t, cot_t = run_mix(
+            peers, lengths, slopes, att, qpre, came, sel, out_weight, hidden_in, cotangent, angles, parts
+        )
+
     if riding:
-        first_phase = []
-        for w in range(3):
-            src, dst = (lambda i, o, w=w: i[w]), (lambda i, o, w=w: o[w])
-            first_phase += far(w, src, dst, close[w].shape[1])
-        second_phase = [
-            (lambda i, o, w=w: o[w].at[0], lambda i, o, w=w: o[3 + w], "dp", 1) for w in range(3)
-        ]
-        ride = dict(
-            guests=[
-                Carry(
-                    close,
-                    like(close) + like(had),
-                    [(0, chunks // 2, first_phase), (chunks // 2 + 1, chunks - 1, second_phase)],
-                ),
-                over_mp(1, chunks - 1),
-            ],
-            ident=3,
-        )
-    attended, mixed_t, middle, second, second_t, cot_t, *more = run_mix(
-        info, slopes, att, qpre, came, sel, out_weight, hidden_in, cotangent, rot, parts, **ride
-    )
-
-    if riding:
-        wide, corner, had_b = more[:3], more[3:6], more[6:9]
-        one = [c for w in range(3) for c in near(w)]
-        two = []
-        for w in range(3):
-            src, dst = (lambda i, o, w=w: o[w]), (lambda i, o, w=w: o[3 + w])
-            two += far(w, src, dst, had_b[w].shape[0])
-        three = [
-            (lambda i, o, w=w: o[3 + w].at[0], lambda i, o, w=w: o[6 + w], "dp", 1) for w in range(3)
-        ]
-        turn = ranges[0][1] // HEAD
-        ride = Carry(
-            had_b,
-            like(had_b, 3) + like(had_b, 3) + like(had_b),
-            [(0, 1, one), (2, 3, two), (4, 4, three)],
-        )
-        pieces = list(had) + list(close) + list(wide) + list(corner)
-        term, part, sglu = run_units(
-            matrices, second, cotangent, second_t, cot_t, pieces, ride, ranges[0][1], depth, ident=4
+        had_b = got[12:15]
+        more, phases = onward(lambda w: lambda i, o: i[w], had_b, 0)
+        ride = Carry(had_b, more, [(0, 1, phases[0]), (2, 3, phases[1]), (4, 4, phases[2])])
+        output, grad_middle, grad_sel, grad_att, et, leaving, sglu = run_units(
+            lengths, slopes, matrices, second, cotangent, second_t, cot_t, [middle, sel, attended, qpre],
+            angles, out_weight, got[:12], ride, ranges[0][1], depth, ident=2,
         )
     else:
         sources = [lax.all_gather(w, "mp") for w in matrices]
         grads, term, part = run_sglu(second, cotangent, *sources)
         units_spec = lambda at: pl.BlockSpec((None, None, count, units), lambda s: at(s) + (0, 0))
         sglu = reduced([second_t, cot_t], (0, 0, 1), grads, units_spec, peers, units)
-    output, grad_middle, pair, grad_att, et, leaving = run_after(
-        info, slopes, term, part, cotangent, middle, sel, attended, out_weight, qpre, rot
-    )
+        output, grad_middle, grad_sel, grad_att, et, leaving = run_after(
+            peers, lengths, slopes, term, part, cotangent, middle, sel, attended, out_weight, qpre, angles
+        )
     inputs_weights = [query_weight, key_weight, value_weight, select_weight]
     if riding:
         grad_hidden, out_sel, inputs = run_projections(
-            info, slopes, qpre, kpre, values, grad_att, st, et, came, leaving, rot, pair,
-            hidden_in, grad_middle, mixed_t, normed_t, inputs_weights, depth, ident=5,
+            lengths, slopes, qpre, kpre, values, grad_att, st, et, came, leaving, angles, grad_sel,
+            hidden_in, grad_middle, mixed_t, normed_t, inputs_weights, depth, ident=3,
         )
     else:
         leavings = lax.all_gather(leaving, "mp")
@@ -1250,12 +1474,13 @@
         left = lax.fori_loop(0, peers, behind, jnp.zeros(leaving.shape, F32)).astype(BF16)
         share = d // peers
         wide_spec = lambda at: pl.BlockSpec((None, count, share), lambda s: (at(s)[0], 0, at(s)[1]))
+        pair = jnp.stack([grad_middle, grad_sel])
         out_sel = reduced([mixed_t, normed_t], (0, 1), pair, wide_spec, peers, share)
         (qkv,) = run_attention_back(
-            info, slopes, qpre, kpre, values, grad_att, st, came, et, left, rot, 0, heads
+            peers, lengths, slopes, qpre, kpre, values, grad_att, st, came, et, left, angles
         )
         inputs = reduced([normed_t], (0, 0, 0), qkv, wide_spec, peers, share)
-        (grad_hidden,) = run_input(inputs_weights, qkv, pair, hidden_in, grad_middle)
+        (grad_hidden,) = run_input(inputs_weights, qkv, grad_sel, hidden_in, grad_middle)
     return (
         output,
         grad_hidden,

time: 302 us -> 258 us (0.85)
  Pallas kernels: 276 us -> 247 us
  between operations: 10.5 us -> 0.69 us
  local copies, waits for them, and re-layouts: 10.4 us -> 6.81 us
    pallas_call x6 -> x3, Pallas kernels: 276 us -> 247 us  [launch(): pl.pallas_call(body, grid=(steps,), in_specs=all_specs, out_specs=all_out...]
where the time goes in v1:
time: 258 us; the launch traced here: 254 us
  Pallas kernels  247 us (96%)
  local copies, waits for them, and re-layouts  6.81 us (3%)
    pallas_call x3, Pallas kernels, launch(): pl.pallas_call(body, grid=(steps,), in_specs=all_specs, out_specs=all_out...  247 us

profile of v1, /device:TPU:12, one launch (start us, length us, event | category | flops | bytes accessed | tf_op | source)
XLA Modules:
  0.0 254.4 jit_solution(8524320874938206414)
XLA Ops:
  0.6 42.9 %forward_to_sglu.1 = (bf16[1024,1024]{1,0:T(8,128)(2,1)}, bf16[1024,1024]{1,0:T(8,128)(2,1)}, bf16[4,8,128,256]{3,2,1,0:T(8,128)(2,1)}, bf16[1024,1024]{1,0:T(8,...) custom-call(s32[1,3]{1,0:T(1,128)} %refs_0_.5, ...), custom_call_target="tpu_custom_call" | custom-call | flops 12884901888 | bytes 63148076 | tf_op jit(solution)/shard_map/forward_to_sglu/pallas_call | solution.py:306
  43.6 119.9 %sglu_and_gradients.1 = (bf16[1024,1024]{1,0:T(8,128)(2,1)}, bf16[1024,1024]{1,0:T(8,128)(2,1)}, bf16[1024,1024]{1,0:T(8,128)(2,1)}, bf16[1024,1024]{1,0:T(8,128...) custom-call(s32[1,3]{1,0:T(1,128)} %refs_0_.5, ...), custom_call_target="tpu_custom_call" | custom-call | flops 53150220288 | bytes 48533548 | tf_op jit(solution)/shard_map/sglu_and_gradients/pallas_call | solution.py:306
  163.5 0.0 copy-start.2
  163.6 84.0 %attention_backward_and_gradients.1 = (bf16[1024,1024]{1,0:T(8,128)(2,1)}, f32[2,64,512]{2,1,0:T(8,128)}, f32[3,64,512]{2,1,0:T(8,128)}) custom-call(s32[1,3]{1,0:T(1,128)} %refs_0_.5, f32[8]{0:T(128)} %refs_1_.5, bf16[1024,1024]{1,0:T(8,128)(2,1)} %get-tuple-element.52.refs_9_.refs_2_.refs_3_, bf16[1024,1024]{1,0:T(8,128)(2,1)} %get-tuple-element.52.refs_9_.refs_2_.refs_3_, ...), custom_call_target="tpu_custom_call" | custom-call | flops 32212254720 | bytes 56496172 | tf_op jit(solution)/shard_map/attention_backward_and_gradients/pallas_call | solution.py:306
  247.6 0.0 copy-start
  247.6 2.1 slice_bitcast_fusion.3
  249.7 0.0 copy-done.2
  249.7 1.0 slice_bitcast_fusion
  250.7 0.0 copy-done
  250.7 0.0 copy-start.1
  250.7 1.3 copy.26
  252.0 1.0 copy-done.1
  253.1 1.3 copy.27
Async XLA Ops:
  163.5 86.2 %copy-start.2 = (f32[3,64,1408]{2,1,0:T(8,128)S(1)}, f32[3,64,1408]{2,1,0:T(8,128)}, u32[]{:S(2)}) copy-start(f32[3,64,1408]{2,1,0:T(8,128)} %get-tuple-element.85) | copy-start | bytes 3244036
  247.6 3.2 %copy-start = (bf16[1024,1024]{1,0:T(8,128)(2,1)S(1)}, bf16[1024,1024]{1,0:T(8,128)(2,1)}, u32[]{:S(2)}) copy-start(bf16[1024,1024]{1,0:T(8,128)(2,1)} %get-tuple-element.107) | copy-start | bytes 6291460
  250.7 2.3 copy-start.1

commit v2 on v1

--- a/solution.py
+++ b/solution.py
@@ -13,7 +13,7 @@
 EPSILON = 1e-06
 BF16 = jnp.bfloat16
 F32 = jnp.float32
-VMEM_LIMIT = 61 * 1024 * 1024
+VMEM_LIMIT = 62 * 1024 * 1024
 
 
 def nn(left, right):
@@ -35,7 +35,7 @@
 
 
 def sigmoid(v):
-    return 1.0 / (1.0 + jnp.exp(-v))
+    return 0.5 * jnp.tanh(0.5 * v) + 0.5
 
 
 def featured(pre, cos, sin):
@@ -45,6 +45,21 @@
 
 def head_slice(h):
     return slice(h * HEAD, (h + 1) * HEAD)
+
+
+def turned_shape(d, n):
+    return (2, d // 2, n)
+
+
+def put_turned(ref, value, parts):
+    turned = value.T
+    rows = turned.shape[0] // parts
+    for i in range(parts):
+        ref[i % 2, (i // 2) * rows : (i // 2 + 1) * rows, :] = turned[i * rows : (i + 1) * rows, :]
+
+
+def feature_slice(h):
+    return slice(2 * h * HEAD, 2 * (h + 1) * HEAD)
 
 
 def row_index(shape):
@@ -165,31 +180,34 @@
 class Reducer:
     KINDS = 8
 
-    def __init__(self, start, blocks, items, depth, rows, delays):
+    def __init__(self, start, blocks, items, depth, rows, delays, slots, order, over_x):
         self.start, self.blocks, self.items = start, blocks, items
+        self.slots, self.order = slots, order
+        self.made = 2 if delays[0] else 1
         self.depth, self.rows, self.delays = depth, rows, delays
-        half, n, wide = depth // 2, 2 * depth * rows, 2 * HEAD
+        self.upper = [(t, z) for t in range(items) for z in range(over_x[t])]
+        self.lower = [(t, z) for t in range(items) for z in range(over_x[t], depth)]
+        n, wide = 2 * depth * rows, 2 * HEAD
         buf = lambda *shape: pltpu.VMEM(shape, BF16)
-        pair = (half, items, rows, wide)
-        flat = (2, half, items, rows, HEAD)
-        one = (half, items, rows, HEAD)
+        up, low = len(self.upper), len(self.lower)
+        pair, flat = (up, rows, wide), (2, low, rows, HEAD)
         self.scratch = [
-            buf(2, items, n, wide),
-            buf(2, items, n, wide),
-            buf(4, items, n, wide),
-            buf(2, *pair),
-            buf(2, *pair),
+            buf(self.made, items, n, wide),
+            buf(self.made, items, n, wide),
+            buf(4 if delays[0] else 2, items, n, wide),
+            buf(slots, *pair),
+            buf(slots, *pair),
             buf(4, *pair),
-            buf(2, *flat),
-            buf(2, *flat),
+            buf(slots, *flat),
+            buf(slots, *flat),
             buf(4, *flat),
-            buf(2, *one),
-            buf(2, *one),
-            buf(4, *one),
-            buf(2, *one),
-            buf(2, *one),
-            buf(4, *one),
-            buf(2, depth, items, rows, HEAD),
+            buf(slots, up, rows, HEAD),
+            buf(slots, up, rows, HEAD),
+            buf(4, up, rows, HEAD),
+            buf(slots, low, rows, HEAD),
+            buf(slots, low, rows, HEAD),
+            buf(4, low, rows, HEAD),
+            buf(slots, depth, items, rows, HEAD),
             buf(4, depth - 1, items, rows, HEAD),
             pltpu.SemaphoreType.DMA((self.KINDS, blocks)),
             pltpu.SemaphoreType.DMA((self.KINDS, blocks)),
@@ -205,9 +223,9 @@
 
     def copies(self, stage, j):
         (given, kept, got, ps, pk, pr, qs, qk, qr, ps2, pk2, pr2, qs2, qk2, qr2, line, zr, send, recv) = self.refs
-        slot, four = lax.rem(j, 2), lax.rem(j, 4)
+        slot, four = lax.rem(j, self.slots), lax.rem(j, 4)
         if stage == 0:
-            plan = [(0, given.at[slot], got.at[four], "dp", 1)]
+            plan = [(0, given.at[lax.rem(j, self.made)], got.at[lax.rem(j, got.shape[0])], "dp", 1)]
         elif stage == 1:
             plan = [(1, ps.at[slot], pr.at[four], "dp", 2), (2, qs.at[slot], qr.at[four], "mp", 1)]
         elif stage == 2:
@@ -224,7 +242,7 @@
             copy.start()
 
     def run(self, step, out):
-        for stage in (4, 3, 2, 1):
+        for stage in self.order:
             j = step - self.start - self.delays[stage - 1]
 
             @pl.when(jnp.logical_and(j >= 0, j < self.blocks))
@@ -238,33 +256,35 @@
 
     def add(self, stage, j, out):
         (given, kept, got, ps, pk, pr, qs, qk, qr, ps2, pk2, pr2, qs2, qk2, qr2, line, zr, send, recv) = self.refs
-        slot, four, x, rows = lax.rem(j, 2), lax.rem(j, 4), self.x, self.rows
-        half = self.depth // 2
+        slot, four, x, rows = lax.rem(j, self.slots), lax.rem(j, 4), self.x, self.rows
         if stage == 1:
+            two, came = lax.rem(j, self.made), lax.rem(j, got.shape[0])
 
             def total(t, z, at):
                 here = pl.ds(pl.multiple_of((2 * z + at) * rows, rows), rows)
-                return plus(kept[slot, t, here, :], got[four, t, here, :]).astype(BF16)
-
-            for z in range(half):
-                for t in range(self.items):
-                    ps[slot, z, t] = total(t, z, 1 - x)
-                    pk[slot, z, t] = total(t, z, x)
-                    for at in range(2):
-                        block = total(t, half + z, at)
-                        qk[slot, at, z, t] = block[:, :HEAD]
-                        qs[slot, at, z, t] = block[:, HEAD:]
+                return kept[two, t, here, :] + got[came, t, here, :]
+
+            for i, (t, z) in enumerate(self.upper):
+                ps[slot, i] = total(t, z, 1 - x)
+                pk[slot, i] = total(t, z, x)
+            for i, (t, z) in enumerate(self.lower):
+                for at in range(2):
+                    block = total(t, z, at)
+                    qk[slot, at, i] = block[:, :HEAD]
+                    qs[slot, at, i] = block[:, HEAD:]
         elif stage == 2:
-            for z in range(half):
-                block = plus(pk[slot, z], pr[four, z]).astype(BF16)
-                pk2[slot, z] = block[:, :, :HEAD]
-                ps2[slot, z] = block[:, :, HEAD:]
-                qs2[slot, z] = plus(qk[slot, 1 - x, z], qr[four, 1 - x, z]).astype(BF16)
-                qk2[slot, z] = plus(qk[slot, x, z], qr[four, x, z]).astype(BF16)
+            for i in range(len(self.upper)):
+                block = pk[slot, i] + pr[four, i]
+                pk2[slot, i] = block[:, :HEAD]
+                ps2[slot, i] = block[:, HEAD:]
+            for i in range(len(self.lower)):
+                qs2[slot, i] = qk[slot, 1 - x, i] + qr[four, 1 - x, i]
+                qk2[slot, i] = qk[slot, x, i] + qr[four, x, i]
         elif stage == 3:
-            for z in range(half):
-                line[slot, z] = plus(pk2[slot, z], pr2[four, z]).astype(BF16)
-                line[slot, half + z] = plus(qk2[slot, z], qr2[four, z]).astype(BF16)
+            for i, (t, z) in enumerate(self.upper):
+                line[slot, z, t] = pk2[slot, i] + pr2[four, i]
+            for i, (t, z) in enumerate(self.lower):
+                line[slot, z, t] = qk2[slot, i] + qr2[four, i]
         else:
             total = plus(line[slot, self.z], *[zr[four, k] for k in range(self.depth - 1)])
             out[:, :, pl.ds(pl.multiple_of(j * HEAD, HEAD), HEAD)] = total
@@ -375,52 +395,48 @@
     return (x * scale_of(x)).astype(BF16)
 
 
-def states_chunk(heads, slopes, keep, kpre, values, cs, sn, state, put):
+def states_chunk(heads, slopes, keep, key, values, state, put):
     for h in range(heads):
         slope = slopes[h]
-        key = featured(kpre[:, head_slice(h)], cs, sn)
         faded = (values[:, head_slice(h)] * fade_to_end(slope, HEAD)).astype(BF16)
         old = state[h] * keep
         put(h, old.astype(BF16))
-        state[h] = jnp.exp(jnp.full((1, 2 * HEAD), -slope * CHUNK, F32)) * old + nn(faded.T, key)
-
-
-def inside_chunk(heads, slopes, qpre, kpre, values, st, cs, sn, put):
+        state[h] = jnp.exp(jnp.full((1, 2 * HEAD), -slope * CHUNK, F32)) * old + nn(faded.T, key(h))
+
+
+def inside_chunk(heads, slopes, query, key, values, st, table, put):
     for h in range(heads):
-        slope = slopes[h]
-        query = featured(qpre[:, head_slice(h)], cs, sn)
-        key = featured(kpre(h).astype(F32), cs, sn)
-        weights = (nt(query, key) * decay_table(slope, False)).astype(BF16)
-        put(h, nn(weights, values(h)) + fade_from_start(slope, HEAD) * nt(query, st(h)))
-
-
-def carried_chunk(heads, slopes, layout, c, att, qpre, came, cs, sn, total):
+        asked = query(h)
+        weights = (nt(asked, key(h)) * table(h)).astype(BF16)
+        put(h, nn(weights, values(h)) + fade_from_start(slopes[h], HEAD) * nt(asked, st(h)))
+
+
+def carried_chunk(heads, slopes, layout, c, att, query, came, total):
     reached = layout.before(c)
     lag = (c * CHUNK).astype(F32)
     alive = layout.alive(c, HEAD)
     for h in range(heads):
-        query = featured(qpre(h).astype(F32), cs, sn)
         fade = jnp.exp(-slopes[h] * (row_index((CHUNK, HEAD)).astype(F32) + (lag + 1.0))) * reached
-        total[:, head_slice(h)] = (att(h) + fade * nt(query, came[h])) * alive
-
-
-def mix_chunk(total, sel, wo, hid, att_o, mixt_o, mid_o, sec_o, sect_o):
+        total[:, head_slice(h)] = (att(h) + fade * nt(query(h), came[h])) * alive
+
+
+def mix_chunk(parts, total, sel, wo, hid, att_o, mixt_o, mid_o, sec_o, sect_o):
     attended = total[...]
     att_o[...] = attended.astype(BF16)
     mixed = (attended * scale_of(attended) * sel.astype(F32)).astype(BF16)
-    mixt_o[...] = mixed.T.reshape(mixt_o.shape)
+    put_turned(mixt_o, mixed, parts)
     middle = hid[...].astype(F32) + nn(mixed, wo)
     mid_o[...] = middle.astype(BF16)
     second = (middle * scale_of(middle)).astype(BF16)
     sec_o[...] = second
-    sect_o[...] = second.T.reshape(sect_o.shape)
+    put_turned(sect_o, second, parts)
 
 
 def state_shape(d):
     return (d // HEAD, HEAD, 2 * HEAD)
 
 
-def keys_kernel(peers, count, lengths, slopes, hid, wk, wv, fine, coarse, normed_o, turned_o, kpre_o, val_o, st_o, fin_o, state):
+def keys_kernel(peers, parts, count, lengths, slopes, hid, wk, wv, fine, coarse, normed_o, turned_o, kpre_o, val_o, st_o, fin_o, state):
     c = pl.program_id(0)
     layout = Layout(lengths, peers, count)
 
@@ -430,7 +446,7 @@
 
     normed = normed_of(hid)
     normed_o[...] = normed
-    turned_o[...] = normed.T.reshape(turned_o.shape)
+    put_turned(turned_o, normed, parts)
     kpre = nn(normed, wk[...])
     kpre_o[...] = kpre.astype(BF16)
     values = nn(normed, wv[...])
@@ -440,18 +456,19 @@
     def put(h, value):
         st_o[0, h] = value
 
-    states_chunk(state.shape[0], slopes, layout.keep(c), kpre, values, cs, sn, state, put)
+    key = lambda h: featured(kpre[:, head_slice(h)], cs, sn)
+    states_chunk(state.shape[0], slopes, layout.keep(c), key, values, state, put)
     fin_o[...] = state[...].astype(BF16)
 
 
 def run_keys(peers, lengths, slopes, hidden, wk, wv, angles, parts):
     n, d = hidden.shape
     heads, chunks = d // HEAD, n // CHUNK
-    turned = (parts // 2, 2, d // parts, n)
+    turned = turned_shape(d, n)
     tile = pl.BlockSpec((CHUNK, d), lambda c: (c, 0))
     outs = [struct((n, d)), struct(turned), struct((n, d)), struct((n, d)), struct((chunks,) + state_shape(d)), struct(state_shape(d))]
     return launch(
-        functools.partial(keys_kernel, peers, n),
+        functools.partial(keys_kernel, peers, parts, n),
         "keys_values_states",
         chunks,
         [lengths, slopes, hidden, wk, wv, *angles],
@@ -459,7 +476,7 @@
         outs,
         [
             tile,
-            pl.BlockSpec(turned[:3] + (CHUNK,), lambda c: (0, 0, 0, c)),
+            pl.BlockSpec(turned[:2] + (CHUNK,), lambda c: (0, 0, c)),
             tile,
             tile,
             pl.BlockSpec((1,) + state_shape(d), lambda c: (c, 0, 0, 0)),
@@ -485,12 +502,11 @@
     inside_chunk(
         st.shape[1],
         slopes,
-        qpre,
-        lambda h: kpre[:, head_slice(h)],
+        lambda h: featured(qpre[:, head_slice(h)], cs, sn),
+        lambda h: featured(kpre[:, head_slice(h)].astype(F32), cs, sn),
         lambda h: values[:, head_slice(h)],
         lambda h: st[0, h],
-        cs,
-        sn,
+        lambda h: decay_table(slopes[h], False),
         put,
     )
 
@@ -514,7 +530,7 @@
     )
 
 
-def mix_kernel(peers, count, lengths, slopes, att, qpre, came, sel, wo, hid, cot, fine, coarse, att_o, mixt_o, mid_o, sec_o, sect_o, cott_o, total):
+def mix_kernel(peers, parts, count, lengths, slopes, att, qpre, came, sel, wo, hid, cot, fine, coarse, att_o, mixt_o, mid_o, sec_o, sect_o, cott_o, total):
     c = pl.program_id(0)
     layout = Layout(lengths, peers, count)
     cs, sn = layout.angles(c, fine, coarse)
@@ -524,24 +540,22 @@
         layout,
         c,
         lambda h: att[:, head_slice(h)],
-        lambda h: qpre[:, head_slice(h)],
+        lambda h: featured(qpre[:, head_slice(h)].astype(F32), cs, sn),
         came,
-        cs,
-        sn,
         total,
     )
-    mix_chunk(total, sel[...], wo[...], hid, att_o, mixt_o, mid_o, sec_o, sect_o)
-    cott_o[...] = cot[...].T.reshape(cott_o.shape)
+    mix_chunk(parts, total, sel[...], wo[...], hid, att_o, mixt_o, mid_o, sec_o, sect_o)
+    put_turned(cott_o, cot[...], parts)
 
 
 def run_mix(peers, lengths, slopes, att, qpre, came, sel, wo, hidden, cot, angles, parts):
     n, d = hidden.shape
     chunks = n // CHUNK
-    turned = (parts // 2, 2, d // parts, n)
+    turned = turned_shape(d, n)
     tile = pl.BlockSpec((CHUNK, d), lambda c: (c, 0))
-    turned_tile = pl.BlockSpec(turned[:3] + (CHUNK,), lambda c: (0, 0, 0, c))
+    turned_tile = pl.BlockSpec(turned[:2] + (CHUNK,), lambda c: (0, 0, c))
     return launch(
-        functools.partial(mix_kernel, peers, n),
+        functools.partial(mix_kernel, peers, parts, n),
         "carried_mixed_middle",
         chunks,
         [lengths, slopes, att, qpre, came, sel, wo, hidden, cot, *angles],
@@ -554,13 +568,13 @@
     )
 
 
-def forward_kernel(chunks, lengths, slopes, hid, cot, fine, coarse, *refs):
+def forward_kernel(chunks, parts, lengths, slopes, hid, cot, fine, coarse, *refs):
     refs = list(refs)
     take = lambda k: [refs.pop(0) for _ in range(k)]
     weights_h = take(5)
     (kpre_o, val_o, st_o, qpre_o, sel_o) = take(5)
     (turned_o, att_o, mixt_o, mid_o, sec_o, sect_o, cott_o, came_o) = take(8)
-    (weights, normed, kpre, val, st, qpre, sel, att, state, final, came, total) = take(12)
+    (weights, normed, kpre, val, st, qpre, sel, att, state, final, came, total, keyed, asked, table) = take(15)
     (load_sems, out_sems, state_sems) = take(3)
     heads = state.shape[0]
     step = pl.program_id(0)
@@ -586,7 +600,7 @@
     def _():
         x = normed_of(hid)
         normed[here, :] = x
-        turned_o[...] = x.T.reshape(turned_o.shape)
+        put_turned(turned_o, x, parts)
         keys = nn(x, weights[0])
         kpre[here, :] = keys.astype(BF16)
         values = nn(x, weights[1])
@@ -596,7 +610,12 @@
         def put(h, value):
             st[c, h] = value
 
-        states_chunk(heads, slopes, layout.keep(c), keys, values, cs, sn, state, put)
+        def key(h):
+            value = featured(keys[:, head_slice(h)], cs, sn)
+            keyed[here, feature_slice(h)] = value
+            return value
+
+        states_chunk(heads, slopes, layout.keep(c), key, values, state, put)
 
     @pl.when(step == chunks - 1)
     def _():
@@ -607,6 +626,8 @@
 
     @pl.when(step == chunks)
     def _():
+        for h in range(heads):
+            table[h] = decay_table(slopes[h], False)
         for copy in loads[2:4]:
             copy.wait()
 
@@ -621,18 +642,22 @@
         def put(h, value):
             att[here, head_slice(h)] = value
 
+        def query(h):
+            value = featured(queries[:, head_slice(h)], cs, sn)
+            asked[here, feature_slice(h)] = value
+            return value
+
         inside_chunk(
             heads,
             slopes,
-            queries,
-            lambda h: kpre[here, head_slice(h)],
+            query,
+            lambda h: keyed[here, feature_slice(h)],
             lambda h: val[here, head_slice(h)],
             lambda h: st[c, h],
-            cs,
-            sn,
+            lambda h: table[h],
             put,
         )
-        cott_o[...] = cot[...].T.reshape(cott_o.shape)
+        put_turned(cott_o, cot[...], parts)
 
     @pl.when(step == 2 * chunks - 1)
     def _():
@@ -647,20 +672,17 @@
 
     @pl.when(step >= 2 * chunks)
     def _():
-        cs, sn = layout.angles(c, fine, coarse)
         carried_chunk(
             heads,
             slopes,
             layout,
             c,
             lambda h: att[here, head_slice(h)],
-            lambda h: qpre[here, head_slice(h)],
+            lambda h: asked[here, feature_slice(h)],
             came,
-            cs,
-            sn,
             total,
         )
-        mix_chunk(total, sel[here, :], weights[4], hid, att_o, mixt_o, mid_o, sec_o, sect_o)
+        mix_chunk(parts, total, sel[here, :], weights[4], hid, att_o, mixt_o, mid_o, sec_o, sect_o)
 
     @pl.when(step == 3 * chunks - 1)
     def _():
@@ -671,15 +693,15 @@
 def run_forward(lengths, slopes, hidden, cot, weights, angles, parts, guests, ident):
     n, d = hidden.shape
     chunks = n // CHUNK
-    turned = (parts // 2, 2, d // parts, n)
+    turned = turned_shape(d, n)
     late = lambda s: jnp.maximum(s - 2 * chunks, 0)
     mid = lambda s: jnp.clip(s - chunks, 0, chunks - 1)
     early = lambda s: jnp.minimum(s, chunks - 1)
     tile = pl.BlockSpec((CHUNK, d), lambda s: (late(s), 0))
-    turned_tile = lambda at: pl.BlockSpec(turned[:3] + (CHUNK,), lambda s: (0, 0, 0, at(s)))
+    turned_tile = lambda at: pl.BlockSpec(turned[:2] + (CHUNK,), lambda s: (0, 0, at(s)))
     whole = pltpu.VMEM((n, d), BF16)
     return launch(
-        functools.partial(forward_kernel, chunks),
+        functools.partial(forward_kernel, chunks, parts),
         "forward_to_sglu",
         3 * chunks,
         [lengths, slopes, hidden, cot, *angles, *weights],
@@ -710,6 +732,9 @@
             pltpu.VMEM(state_shape(d), BF16),
             pltpu.VMEM(state_shape(d), BF16),
             pltpu.VMEM((CHUNK, d), F32),
+            pltpu.VMEM((n, 2 * d), BF16),
+            pltpu.VMEM((n, 2 * d), BF16),
+            pltpu.VMEM((d // HEAD, CHUNK, CHUNK), F32),
             pltpu.SemaphoreType.DMA((5,)),
             pltpu.SemaphoreType.DMA((5,)),
             pltpu.SemaphoreType.DMA((2,)),
@@ -770,17 +795,21 @@
     )
 
 
-def units_kernel(geo, reducer, ride, lengths, slopes, first_weight, second_weight, down_weight, x, *refs):
+def units_kernel(geo, reducer, ride, lengths, slopes, fine, coarse, *refs):
     blocks, cut, d, units, chunks = geo["blocks"], geo["cut"], geo["d"], geo["units"], geo["chunks"]
     refs = list(refs)
     take = lambda k: [refs.pop(0) for _ in range(k)]
-    (mid, sel, att, qpre, fine, coarse) = take(6)
-    cot_h, xt_h, cott_h, wo_h = take(4)
+    weights_h = take(3)
+    (x_h, cot_h, xt_h, cott_h, wo_h) = take(5)
+    rows_h = take(4)
     pieces = take(12)
     had_b = take(3)
-    (out_o, gmid_o, gsel_o, gatt_o, et_o, e0_o, sums_o) = take(7)
+    rows_out = take(4)
+    (et_o, e0_o, sums_o) = take(3)
     pieces = pieces + had_b + take(9)
-    term, part, cot, xt, cott, o1, o2, od, c1, c2, cd, state, sums, sems, own_sems, wo_sems = take(16)
+    (term, part, x, cot, xt, cott, o1, o2, od, c12, cd, inner, grads, state, e0, sums) = take(16)
+    (tiles, made, ends) = take(3)
+    (sems, own_sems, block_sems, tile_sems, made_sems) = take(5)
     reducer.bind(take(len(reducer.scratch)))
     step = pl.program_id(0)
     ride.before(step, had_b, pieces[15:], refs)
@@ -804,26 +833,49 @@
         return copies
 
     own = [
+        pltpu.make_async_copy(x_h, x, own_sems.at[6]),
         pltpu.make_async_copy(cot_h, cot, own_sems.at[0]),
-        pltpu.make_async_copy(xt_h.at[:, 1 - core], xt.at[0], own_sems.at[1]),
-        pltpu.make_async_copy(xt_h.at[:, core], xt.at[1], own_sems.at[2]),
-        pltpu.make_async_copy(cott_h.at[:, 1 - core], cott.at[0], own_sems.at[3]),
-        pltpu.make_async_copy(cott_h.at[:, core], cott.at[1], own_sems.at[4]),
+        pltpu.make_async_copy(xt_h.at[1 - core], xt.at[pl.ds(0, d // 2), :], own_sems.at[1]),
+        pltpu.make_async_copy(xt_h.at[core], xt.at[pl.ds(d // 2, d // 2), :], own_sems.at[2]),
+        pltpu.make_async_copy(cott_h.at[1 - core], cott.at[pl.ds(0, d // 2), :], own_sems.at[3]),
+        pltpu.make_async_copy(cott_h.at[core], cott.at[pl.ds(d // 2, d // 2), :], own_sems.at[4]),
     ]
-    pairs, rows = xt.shape[1], xt.shape[2]
-    out_weight = [
-        pltpu.make_async_copy(
-            wo_h.at[pl.ds((k * pairs + i) * rows, rows), :], xt.at[k, i], wo_sems.at[k * pairs + i]
-        )
-        for k in range(2)
-        for i in range(pairs)
-    ]
+    out_weight = pltpu.make_async_copy(wo_h, xt, own_sems.at[7])
     saved = pltpu.make_async_copy(sums, sums_o, own_sems.at[5])
+    leaving = pltpu.make_async_copy(e0, e0_o, own_sems.at[8])
+
+    def own_block(j):
+        slot, here = lax.rem(j, 2), pl.ds(pl.multiple_of(j * HEAD, HEAD), HEAD)
+        return [
+            pltpu.make_async_copy(weights_h[0].at[:, here], c12.at[slot, :, pl.ds(0, HEAD)], block_sems.at[slot, 0]),
+            pltpu.make_async_copy(
+                weights_h[1].at[:, here], c12.at[slot, :, pl.ds(2 * HEAD, HEAD)], block_sems.at[slot, 1]
+            ),
+            pltpu.make_async_copy(weights_h[2].at[here, :], cd.at[slot, pl.ds(0, HEAD), :], block_sems.at[slot, 2]),
+        ]
+
+    def rows_at(i):
+        return pl.ds(pl.multiple_of((chunks - 1 - i) * CHUNK, CHUNK), CHUNK)
+
+    def tile(i):
+        slot = lax.rem(i, 2)
+        return [
+            pltpu.make_async_copy(src.at[rows_at(i), :], tiles.at[slot, k], tile_sems.at[slot, k])
+            for k, src in enumerate(rows_h)
+        ]
+
+    def results(i):
+        slot = lax.rem(i, 2)
+        return [
+            pltpu.make_async_copy(made.at[slot, k], dst.at[rows_at(i), :], made_sems.at[slot, k])
+            for k, dst in enumerate(rows_out)
+        ] + [pltpu.make_async_copy(ends.at[slot], et_o.at[chunks - 1 - i], made_sems.at[slot, 4])]
+
     turn = cut // HEAD
 
     @pl.when(step == 0)
     def _():
-        for copy in fetch(0) + own:
+        for copy in own_block(0) + fetch(0) + own:
             copy.start()
         term[...] = jnp.zeros_like(term)
         part[...] = jnp.zeros_like(part)
@@ -840,12 +892,17 @@
     def _():
         local = step - jnp.where(step >= turn, turn, 0)
         here = pl.ds(pl.multiple_of(local * HEAD, HEAD), HEAD)
-        c1[:, :HEAD] = first_weight[...]
-        c1[:, HEAD:] = o1[:, here]
-        c2[:, :HEAD] = second_weight[...]
-        c2[:, HEAD:] = o2[:, here]
-        cd[:HEAD, :] = down_weight[...]
-        cd[HEAD:, :] = od[here, :]
+        at = lax.rem(step, 2)
+        c12[at, :, HEAD : 2 * HEAD] = o1[:, here]
+        c12[at, :, 3 * HEAD :] = o2[:, here]
+        cd[at, HEAD:, :] = od[here, :]
+        for copy in own_block(step):
+            copy.wait()
+
+    @pl.when(step < blocks - 1)
+    def _():
+        for copy in own_block(step + 1):
+            copy.start()
 
     @pl.when(step == turn - 1)
     def _():
@@ -859,46 +916,69 @@
 
     @pl.when(step < blocks)
     def _():
-        left = nn(x[...], c1[...])
-        right = nn(x[...], c2[...])
-        inner = (left * right).astype(BF16)
-        upstream = nt(cot[...], cd[...])
-        grad_left = (upstream * right).astype(BF16)
-        grad_right = (upstream * left).astype(BF16)
-        slot = lax.rem(step, 2)
+        wide, at = 2 * HEAD, lax.rem(step, 2)
+        for k in range(chunks):
+            here = slice(k * CHUNK, (k + 1) * CHUNK)
+            both = nn(x[here, :], c12[at])
+            left, right = both[:, :wide], both[:, wide:]
+            upstream = nt(cot[here, :], cd[at])
+            inner[here, :] = (left * right).astype(BF16)
+            grads[here, :wide] = (upstream * right).astype(BF16)
+            grads[here, wide:] = (upstream * left).astype(BF16)
+        slot = 0
+        both = nn(xt[...], grads[...]).astype(BF16)
+        down = nn(cott[...], inner[...]).astype(BF16)
         for k, buffer in enumerate((reducer.given, reducer.kept)):
-            buffer[slot, 0] = nn(rows_of(xt, k), grad_left).astype(BF16)
-            buffer[slot, 1] = nn(rows_of(xt, k), grad_right).astype(BF16)
-            buffer[slot, 2] = nn(rows_of(cott, k), inner).astype(BF16)
+            here = slice(k * (d // 2), (k + 1) * (d // 2))
+            buffer[slot, 0] = both[here, :wide]
+            buffer[slot, 1] = both[here, wide:]
+            buffer[slot, 2] = down[here, :]
             if k == 0:
                 reducer.begin(step)
-        term[...] += nn(inner, cd[...])
-        part[...] += nt(grad_left, c1[...]) + nt(grad_right, c2[...])
+        term[...] += nn(inner[...], cd[at])
+        part[...] += nt(grads[...], c12[at])
 
     @pl.when(step == blocks - 1)
     def _():
-        for copy in out_weight:
+        out_weight.start()
+        for copy in tile(0):
             copy.start()
 
     @pl.when(step == blocks)
     def _():
-        for copy in out_weight:
+        out_weight.wait()
+
+    @pl.when(jnp.logical_and(step >= blocks, step < blocks + chunks))
+    def _():
+        i = step - blocks
+        c, slot = chunks - 1 - i, lax.rem(i, 2)
+        here = pl.ds(pl.multiple_of(c * CHUNK, CHUNK), CHUNK)
+        for copy in tile(i):
             copy.wait()
 
-    @pl.when(jnp.logical_and(step >= blocks, step < blocks + chunks))
-    def _():
-        c = chunks - 1 - (step - blocks)
-        here = pl.ds(pl.multiple_of(c * CHUNK, CHUNK), CHUNK)
+        @pl.when(i < chunks - 1)
+        def _():
+            for copy in tile(i + 1):
+                copy.start()
+
+        @pl.when(i >= 2)
+        def _():
+            for copy in results(i - 2):
+                copy.wait()
+
         cs, sn = layout.angles(c, fine, coarse)
-        wo = xt[...].reshape(d, d)
+        mid, sel, att, qpre = [tiles.at[slot, k] for k in range(4)]
         after_chunk(
-            layout, c, heads, slopes, term[here, :], part[here, :], cot[here, :], mid, sel, att, wo, qpre, cs, sn,
-            out_o, gmid_o, gsel_o, gatt_o, et_o, state,
+            layout, c, heads, slopes, term[here, :], part[here, :], cot[here, :], mid, sel, att, xt[...], qpre, cs, sn,
+            *[made.at[slot, k] for k in range(4)], ends.at[pl.ds(slot, 1)], state,
         )
+        for copy in results(i):
+            copy.start()
 
     @pl.when(step == blocks + chunks - 1)
     def _():
-        e0_o[...] = state[...].astype(BF16)
+        e0[...] = state[...].astype(BF16)
+        leaving.start()
 
     ride.after(step, had_b, pieces[15:], refs)
     reducer.run(step, sums)
@@ -906,12 +986,11 @@
     @pl.when(step == reducer.last)
     def _():
         saved.start()
+        for i in range(chunks - 2, chunks):
+            for copy in results(i):
+                copy.wait()
+        leaving.wait()
         saved.wait()
-
-
-def rows_of(ref, k):
-    block = ref[k]
-    return block.reshape(block.shape[0] * block.shape[1], block.shape[2])
 
 
 def run_units(lengths, slopes, matrices, second, cot, second_t, cot_t, rows_in, angles, wo, pieces, ride, cut, depth, ident):
@@ -919,49 +998,52 @@
     chunks = n // CHUNK
     units = matrices[0].shape[1]
     blocks = units // HEAD
-    pairs, _, rows, _ = second_t.shape
-    reducer = Reducer(0, blocks, 3, depth, rows, (1, 3, 5, 7))
+    rows = d // (4 * depth)
+    reducer = Reducer(0, blocks, 3, depth, rows, (0, 2, 4, 6), 2, (4, 3, 2, 1), (1, 1, 2))
     geo = dict(blocks=blocks, cut=cut, d=d, units=units, chunks=chunks)
-    at = lambda s: jnp.minimum(s, blocks - 1)
-    back = lambda s: chunks - 1 - jnp.clip(s - blocks, 0, chunks - 1)
-    tile = pl.BlockSpec((CHUNK, d), lambda s: (back(s), 0))
-    columns = pl.BlockSpec((d, HEAD), lambda s: (0, at(s)))
-    turned = pltpu.VMEM((2, pairs, rows, n), BF16)
+    turned = pltpu.VMEM((d, n), BF16)
     size = max(cut, units - cut)
     sums = (3, rows, units)
     return launch(
         functools.partial(units_kernel, geo, reducer, ride),
         "sglu_and_gradients",
         max(reducer.last, blocks + chunks - 1) + 1,
-        [lengths, slopes] + list(matrices) + [second] + list(rows_in) + list(angles)
-        + [cot, second_t, cot_t, wo] + list(pieces) + ride.inputs,
-        [smem(), smem(), columns, columns, pl.BlockSpec((HEAD, d), lambda s: (at(s), 0)), once(second.shape)]
-        + [tile] * 4
-        + [once(a.shape) for a in angles]
-        + [anywhere()] * (4 + len(pieces) + len(ride.inputs)),
+        [lengths, slopes, *angles]
+        + list(matrices)
+        + [second, cot, second_t, cot_t, wo]
+        + list(rows_in)
+        + list(pieces)
+        + ride.inputs,
+        [smem(), smem()] + [once(a.shape) for a in angles] + [anywhere()] * (12 + len(pieces) + len(ride.inputs)),
         [struct((n, d))] * 4
         + [struct((chunks,) + state_shape(d)), struct(state_shape(d)), struct(sums, F32)]
         + ride.outs,
-        [tile] * 4
-        + [pl.BlockSpec((1,) + state_shape(d), lambda s: (back(s), 0, 0, 0)), whole_block(state_shape(d))]
-        + [anywhere()] * (1 + len(ride.outs)),
+        [anywhere()] * (7 + len(ride.outs)),
         [
             pltpu.VMEM((n, d), F32),
             pltpu.VMEM((n, d), F32),
+            pltpu.VMEM((n, d), BF16),
             pltpu.VMEM((n, d), BF16),
             turned,
             turned,
             pltpu.VMEM((d, size), BF16),
             pltpu.VMEM((d, size), BF16),
             pltpu.VMEM((size, d), BF16),
-            pltpu.VMEM((d, 2 * HEAD), BF16),
-            pltpu.VMEM((d, 2 * HEAD), BF16),
-            pltpu.VMEM((2 * HEAD, d), BF16),
+            pltpu.VMEM((2, d, 4 * HEAD), BF16),
+            pltpu.VMEM((2, 2 * HEAD, d), BF16),
+            pltpu.VMEM((n, 2 * HEAD), BF16),
+            pltpu.VMEM((n, 4 * HEAD), BF16),
             pltpu.VMEM(state_shape(d), F32),
+            pltpu.VMEM(state_shape(d), BF16),
             pltpu.VMEM(sums, F32),
+            pltpu.VMEM((2, 4, CHUNK, d), BF16),
+            pltpu.VMEM((2, 4, CHUNK, d), BF16),
+            pltpu.VMEM((2,) + state_shape(d), BF16),
             pltpu.SemaphoreType.DMA((2, 3, 8)),
-            pltpu.SemaphoreType.DMA((6,)),
-            pltpu.SemaphoreType.DMA((2 * pairs,)),
+            pltpu.SemaphoreType.DMA((9,)),
+            pltpu.SemaphoreType.DMA((2, 3)),
+            pltpu.SemaphoreType.DMA((2, 4)),
+            pltpu.SemaphoreType.DMA((2, 5)),
         ]
         + reducer.scratch
         + ride.scratch,
@@ -1040,12 +1122,12 @@
         def _(left=left):
             block = left[...]
             block = block.reshape(-1, block.shape[-1])
-            out[...] = nn(block, right[...]).astype(BF16).reshape(out.shape)
+            out[...] = nn(block, right[...]).astype(BF16)
 
 
 def run_weights(lefts, items, rights, right_spec, peers, width):
-    pairs, _, rows, n = lefts[0].shape
-    shape = (peers, len(items), pairs, 2, rows, width)
+    _, half, n = lefts[0].shape
+    shape = (peers, len(items), 2 * half, width)
     which = lambda s: (lax.div(s, peers), lax.rem(s, peers))
     (out,) = launch(
         functools.partial(weights_kernel, items, peers),
@@ -1054,21 +1136,20 @@
         list(lefts) + [rights],
         [whole_block(left.shape) for left in lefts] + [right_spec(which)],
         [struct(shape)],
-        [pl.BlockSpec((None, None) + shape[2:], lambda s: (which(s)[1], which(s)[0], 0, 0, 0, 0))],
+        [pl.BlockSpec((None, None) + shape[2:], lambda s: (which(s)[1], which(s)[0], 0, 0))],
         [],
-        4 * n * pairs * rows * width * len(items) * peers,
+        4 * n * half * width * len(items) * peers,
     )
     return out
 
 
-def head_back(slope, qpre, kpre, value, grad, state, ending, cs, sn):
+def head_back(slope, table, turned, qpre, kpre, value, grad, state, ending, cs, sn):
     qp, kp = qpre.astype(F32), kpre.astype(F32)
     qs, ks = sigmoid(qp), sigmoid(kp)
     qa, ka = qp * qs, kp * ks
     query = jnp.concatenate([qa * cs, qa * sn], axis=-1).astype(BF16)
     key = jnp.concatenate([ka * cs, ka * sn], axis=-1).astype(BF16)
     state, ending = state.astype(BF16), ending.astype(BF16)
-    table, turned = decay_table(slope, False), decay_table(slope, True)
     scores_t = (nt(key, query) * turned).astype(BF16)
     slope_s = (nt(grad, value) * table).astype(BF16)
     slope_t = (nt(value, grad) * turned).astype(BF16)
@@ -1100,8 +1181,9 @@
         lane = jnp.zeros((1, 2 * HEAD), F32)
         state = st[0, h].astype(F32) + came[h].astype(F32) * (jnp.exp(lane - slope * span) * before)
         ending = et[0, h].astype(F32) + left[h].astype(F32) * (jnp.exp(lane - slope * rest) * after)
+        table, turned = decay_table(slope, False), decay_table(slope, True)
         three = head_back(
-            slope, qpre[:, cols], kpre[:, cols], values[:, cols], gatt[:, cols], state, ending, cs, sn
+            slope, table, turned, qpre[:, cols], kpre[:, cols], values[:, cols], gatt[:, cols], state, ending, cs, sn
         )
         for i in range(3):
             grads_o[i, :, cols] = three[i]
@@ -1132,12 +1214,12 @@
     chunks, blocks, d, n = geo["chunks"], geo["blocks"], geo["d"], geo["n"]
     refs = list(refs)
     take = lambda k: [refs.pop(0) for _ in range(k)]
-    columns = [take(2) for _ in range(4)]
-    states = [take(2) for _ in range(2)]
-    (came, leaving, fine, coarse, branch_a, branch_b, sel_a, sel_b, sel, hid, gmid, mixt_h, normt_h) = take(13)
+    arrays_h = take(6)
+    (came_h, leaving, fine, coarse, gsel_h, hid_h, gmid_h, mixt_h, normt_h) = take(9)
     weights_h = take(4)
     hidden_o, out, out2 = take(3)
-    grads, block, mixt, normt, w4, left, sems, state_sems = take(8)
+    (qpre, kpre, val, gatt, st, et, came, gsel, gmid) = take(9)
+    grads, block, decays, mixt, normt, left, sems, late_sems, state_sems = take(9)
     outer.bind(take(len(outer.scratch)))
     inner.bind(refs)
     step = pl.program_id(0)
@@ -1145,12 +1227,26 @@
     me = lax.axis_index("mp")
     layout = Layout(lengths, 2, n)
     loads = [
-        pltpu.make_async_copy(mixt_h.at[:, 1 - core], mixt.at[0], sems.at[0]),
-        pltpu.make_async_copy(mixt_h.at[:, core], mixt.at[1], sems.at[1]),
-        pltpu.make_async_copy(normt_h.at[:, 1 - core], normt.at[0], sems.at[2]),
-        pltpu.make_async_copy(normt_h.at[:, core], normt.at[1], sems.at[3]),
+        pltpu.make_async_copy(gmid_h, gmid, sems.at[4]),
+        pltpu.make_async_copy(mixt_h.at[1 - core], mixt.at[pl.ds(0, d // 2), :], sems.at[0]),
+        pltpu.make_async_copy(mixt_h.at[core], mixt.at[pl.ds(d // 2, d // 2), :], sems.at[1]),
+        pltpu.make_async_copy(gsel_h, gsel, sems.at[5]),
+        pltpu.make_async_copy(normt_h.at[1 - core], normt.at[pl.ds(0, d // 2), :], sems.at[2]),
+        pltpu.make_async_copy(normt_h.at[core], normt.at[pl.ds(d // 2, d // 2), :], sems.at[3]),
     ]
-    matrices = [pltpu.make_async_copy(w, w4.at[i], sems.at[4 + i]) for i, w in enumerate(weights_h)]
+    more = [
+        pltpu.make_async_copy(src, dst, sems.at[6 + i])
+        for i, (src, dst) in enumerate(zip(arrays_h + [came_h], (qpre, kpre, val, gatt, st, et, came)))
+    ]
+    select = pltpu.make_async_copy(weights_h[3], mixt, sems.at[13])
+
+    def replaced(j):
+        copies = []
+        for side in range(2):
+            cols = pl.ds(pl.multiple_of(((me if side == 0 else 1 - me) * blocks + j) * HEAD, HEAD), HEAD)
+            for i, (src, dst) in enumerate(zip(weights_h[:3] + [hid_h], (qpre, kpre, gatt, val))):
+                copies.append(pltpu.make_async_copy(src.at[:, cols], dst.at[:, cols], late_sems.at[j, side, i]))
+        return copies
 
     def exchange(j):
         pair = []
@@ -1164,9 +1260,7 @@
         for j in range(blocks):
             for copy in exchange(j):
                 copy.start()
-        for copy in loads:
-            copy.start()
-        for copy in matrices:
+        for copy in loads + more:
             copy.start()
         for copy in loads:
             copy.wait()
@@ -1174,11 +1268,14 @@
     @pl.when(step < blocks)
     def _():
         slot = lax.rem(step, 2)
-        gb = jnp.concatenate([branch_a[...], branch_b[...]], axis=1)
-        gs = jnp.concatenate([sel_a[...], sel_b[...]], axis=1)
+        mine = pl.ds(pl.multiple_of((me * blocks + step) * HEAD, HEAD), HEAD)
+        theirs = pl.ds(pl.multiple_of(((1 - me) * blocks + step) * HEAD, HEAD), HEAD)
+        gb = jnp.concatenate([gmid[:, mine], gmid[:, theirs]], axis=1)
+        gs = jnp.concatenate([gsel[:, mine], gsel[:, theirs]], axis=1)
+        made = [nn(mixt[...], gb).astype(BF16), nn(normt[...], gs).astype(BF16)]
         for k, buffer in enumerate((outer.given, outer.kept)):
-            buffer[slot, 0] = nn(rows_of(mixt, k), gb).astype(BF16)
-            buffer[slot, 1] = nn(rows_of(normt, k), gs).astype(BF16)
+            for i in range(2):
+                buffer[slot, i] = made[i][k * (d // 2) : (k + 1) * (d // 2), :]
             if k == 0:
                 outer.begin(step)
 
@@ -1187,6 +1284,10 @@
         j = step - blocks
         for copy in exchange(j):
             copy.wait()
+        for side in range(2):
+            slope = slopes[(me if side == 0 else 1 - me) * blocks + j]
+            for k in range(2):
+                decays[side, k] = decay_table(slope, k == 1)
 
         def one(c, carry):
             here = pl.ds(pl.multiple_of(c * CHUNK, CHUNK), CHUNK)
@@ -1197,39 +1298,51 @@
             for side in range(2):
                 h = (me if side == 0 else 1 - me) * blocks + j
                 slope = slopes[h]
-                qpre, kpre, values, gatt = [pair[side][here, :] for pair in columns]
-                st, et = [pair[side][c, 0].astype(F32) for pair in states]
+                cols = pl.ds(pl.multiple_of(h * HEAD, HEAD), HEAD)
+                four = [ref[here, cols] for ref in (qpre, kpre, val, gatt)]
                 lane = jnp.zeros((1, 2 * HEAD), F32)
-                state = st + came[h].astype(F32) * (jnp.exp(lane - slope * span) * before)
-                ending = et + left[h].astype(F32) * (jnp.exp(lane - slope * rest) * after)
-                three = head_back(slope, qpre, kpre, values, gatt, state, ending, cs, sn)
-                cols = pl.ds(pl.multiple_of(h * HEAD, HEAD), HEAD)
+                state = st[c, h].astype(F32) + came[h].astype(F32) * (jnp.exp(lane - slope * span) * before)
+                ending = et[c, h].astype(F32) + left[h].astype(F32) * (jnp.exp(lane - slope * rest) * after)
+                three = head_back(
+                    slope, decays[side, 0], decays[side, 1], *four, state, ending, cs, sn
+                )
                 for i in range(3):
-                    block[i, here, head_slice(side)] = three[i]
+                    block[here, head_slice(2 * i + side)] = three[i]
                     grads[i, here, cols] = three[i]
             return carry
 
         lax.fori_loop(0, chunks, one, 0)
         slot = lax.rem(j, 2)
+        made = nn(normt[...], block[...]).astype(BF16)
         for k, buffer in enumerate((inner.given, inner.kept)):
             for i in range(3):
-                buffer[slot, i] = nn(rows_of(normt, k), block[i]).astype(BF16)
+                buffer[slot, i] = made[k * (d // 2) : (k + 1) * (d // 2), feature_slice(i)]
             if k == 0:
                 inner.begin(j)
+        for copy in replaced(j):
+            copy.start()
+
+    @pl.when(step == blocks - 1)
+    def _():
+        select.start()
+        for copy in more:
+            copy.wait()
 
     @pl.when(step == 2 * blocks)
     def _():
-        for copy in matrices:
-            copy.wait()
+        select.wait()
+        for j in range(blocks):
+            for copy in replaced(j):
+                copy.wait()
 
     @pl.when(jnp.logical_and(step >= 2 * blocks, step < 2 * blocks + chunks))
     def _():
         here = pl.ds(pl.multiple_of((step - 2 * blocks) * CHUNK, CHUNK), CHUNK)
-        total = nt(sel[...], w4[3])
-        for i in range(3):
-            total = total + nt(grads[i, here, :], w4[i])
-        x = hid[...].astype(F32)
-        hidden_o[...] = (gmid[...].astype(F32) + norm_back(x, scale_of(x), total)).astype(BF16)
+        total = nt(gsel[here, :], mixt[...])
+        for i, w in enumerate((qpre, kpre, gatt)):
+            total = total + nt(grads[i, here, :], w[...])
+        x = val[here, :].astype(F32)
+        hidden_o[...] = (gmid[here, :].astype(F32) + norm_back(x, scale_of(x), total)).astype(BF16)
 
     outer.run(step, out)
     inner.run(step, out2)
@@ -1239,46 +1352,41 @@
     n, d = qpre.shape
     heads, chunks = d // HEAD, n // CHUNK
     blocks = heads // 2
-    pairs, _, rows, _ = mixed_t.shape
-    outer = Reducer(0, blocks, 2, depth, rows, (1, 3, 5, 7))
-    inner = Reducer(blocks, blocks, 3, depth, rows, (1, 2, 4, 5))
+    rows = d // (4 * depth)
+    outer = Reducer(0, blocks, 2, depth, rows, (1, 4, 5, 6), 4, (1, 2, 3, 4), (2, 2))
+    inner = Reducer(blocks, blocks, 3, depth, rows, (1, 2, 3, 4), 4, (1, 2, 3, 4), (2, 2, 2))
     steps = max(outer.last, inner.last, 2 * blocks + chunks - 1) + 1
     geo = dict(chunks=chunks, blocks=blocks, d=d, n=n)
-    early = lambda s: jnp.minimum(s, blocks - 1)
-    mid = lambda s: jnp.clip(s - blocks, 0, blocks - 1)
     late = lambda s: jnp.clip(s - 2 * blocks, 0, chunks - 1)
-    side = lambda k: blocks * (lax.axis_index("mp") if k == 0 else 1 - lax.axis_index("mp"))
-    column = lambda k: pl.BlockSpec((n, HEAD), lambda s: (0, side(k) + mid(s)))
-    state = lambda k: pl.BlockSpec((chunks, 1, HEAD, 2 * HEAD), lambda s: (0, side(k) + mid(s), 0, 0))
-    early_column = lambda k: pl.BlockSpec((n, HEAD), lambda s: (0, side(k) + early(s)))
-    tile = pl.BlockSpec((CHUNK, d), lambda s: (late(s), 0))
-    turned = pltpu.VMEM((2, pairs, rows, n), BF16)
+    whole = pltpu.VMEM((n, d), BF16)
+    states = pltpu.VMEM((chunks,) + state_shape(d), BF16)
+    one = pltpu.VMEM(state_shape(d), BF16)
+    turned = pltpu.VMEM((d, n), BF16)
     return launch(
         functools.partial(projections_kernel, geo, outer, inner),
         "attention_backward_and_gradients",
         steps,
-        [lengths, slopes]
-        + [a for a in (qpre, kpre, values, gatt, st, et) for _ in range(2)]
-        + [came, leaving, *angles, gmid, gmid, gsel, gsel, gsel, hidden, gmid, mixed_t, normed_t]
+        [lengths, slopes, qpre, kpre, values, gatt, st, et, came, leaving, *angles]
+        + [gsel, hidden, gmid, mixed_t, normed_t]
         + list(weights),
-        [smem(), smem()]
-        + [column(k) for _ in range(4) for k in range(2)]
-        + [state(k) for _ in range(2) for k in range(2)]
-        + [once(came.shape), anywhere()]
-        + [once(a.shape) for a in angles]
-        + [early_column(k) for _ in range(2) for k in range(2)]
-        + [tile, tile, tile]
-        + [anywhere()] * 6,
+        [smem(), smem()] + [anywhere()] * 8 + [once(a.shape) for a in angles] + [anywhere()] * 9,
         [struct((n, d)), struct((2, rows, d // 2), F32), struct((3, rows, d // 2), F32)],
-        [tile, whole_block((2, rows, d // 2)), whole_block((3, rows, d // 2))],
         [
+            pl.BlockSpec((CHUNK, d), lambda s: (late(s), 0)),
+            whole_block((2, rows, d // 2)),
+            whole_block((3, rows, d // 2)),
+        ],
+        [whole] * 4
+        + [states, states, one, whole, whole]
+        + [
             pltpu.VMEM((3, n, d), BF16),
-            pltpu.VMEM((3, n, 2 * HEAD), BF16),
+            pltpu.VMEM((n, 6 * HEAD), BF16),
+            pltpu.VMEM((2, 2, CHUNK, CHUNK), F32),
             turned,
             turned,
-            pltpu.VMEM((4, d, d), BF16),
-            pltpu.VMEM(leaving.shape, BF16),
-            pltpu.SemaphoreType.DMA((8,)),
+            one,
+            pltpu.SemaphoreType.DMA((14,)),
+            pltpu.SemaphoreType.DMA((blocks, 2, 4)),
             pltpu.SemaphoreType.DMA((2, heads)),
         ]
         + outer.scratch
@@ -1319,7 +1427,9 @@
 
 def reduced(lefts, items, rights, spec, peers, width):
     full = run_weights(lefts, items, rights, spec, peers, width)
-    full = full.reshape(peers, len(items), -1, full.shape[4], width)
+    parts = lax.axis_size("dp")
+    full = full.reshape(peers, len(items), 2, parts // 2, -1, width)
+    full = jnp.swapaxes(full, 2, 3).reshape(peers, len(items), parts, -1, width)
     mine = lax.psum_scatter(full, "dp", scatter_dimension=2, tiled=False)
     return lax.psum_scatter(mine, "mp", scatter_dimension=0, tiled=False).astype(F32)
 
@@ -1352,7 +1462,7 @@
     riding = peers == 2
 
     if riding:
-        cut = -(-units // 256) * 128
+        cut = units // 256 * 128
         ranges = [(0, cut), (cut, units - cut)]
     else:
         ranges = [(0, units)]
@@ -1384,28 +1494,28 @@
             (lambda i, o: src(i, o), lambda i, o: dst(i, o).at[2], "dp", 1),
         ]
 
-    def far(src, dst, rows):
-        top = -(-rows // 32) * 16
+    def far(src, dst, rows, balanced):
+        top = -(-rows // 32) * 16 if balanced else 0
         upper, lower = pl.ds(0, top), pl.ds(top, rows - top)
-        return [
-            (lambda i, o: src(i, o).at[1, upper, :], lambda i, o: dst(i, o).at[0, upper, :], "dp", 2),
+        over_x = (lambda i, o: src(i, o).at[1, upper, :], lambda i, o: dst(i, o).at[0, upper, :], "dp", 2)
+        return ([over_x] if balanced else []) + [
             (lambda i, o: src(i, o).at[0, lower, :], lambda i, o: dst(i, o).at[0, lower, :], "dp", 4),
             (lambda i, o: src(i, o).at[0], lambda i, o: dst(i, o).at[1], "dp", 1),
             (lambda i, o: src(i, o).at[1], lambda i, o: dst(i, o).at[2], "dp", 1),
         ]
 
-    def onward(pieces, out, at):
+    def onward(pieces, out, at, balanced):
         ref = lambda k: lambda i, o: o[k]
         one, two, three = [], [], []
         for w in range(3):
             one += near(pieces(w), ref(at + w))
-            two += far(ref(at + w), ref(at + 3 + w), out[w].shape[0])
+            two += far(ref(at + w), ref(at + 3 + w), out[w].shape[0], balanced)
             three.append((lambda i, o, w=w: o[at + 3 + w].at[0], ref(at + 6 + w), "dp", 1))
         return like(out, 3) + like(out, 3) + like(out), [one, two, three]
 
     if riding:
         outs, copies = over_mp(0)
-        more, phases = onward(lambda w: lambda i, o: o[w], outs, 3)
+        more, phases = onward(lambda w: lambda i, o: o[w], outs, 3, True)
         outs_b, copies_b = over_mp(1)
         spans = [(0, chunks), (chunks + 1, 2 * chunks), (2 * chunks + 1, 3 * chunks - 2), (3 * chunks - 1,) * 2]
         guests = [
@@ -1443,8 +1553,8 @@
 
     if riding:
         had_b = got[12:15]
-        more, phases = onward(lambda w: lambda i, o: i[w], had_b, 0)
-        ride = Carry(had_b, more, [(0, 1, phases[0]), (2, 3, phases[1]), (4, 4, phases[2])])
+        more, phases = onward(lambda w: lambda i, o: i[w], had_b, 0, True)
+        ride = Carry(had_b, more, [(0, 1, phases[0]), (2, 2, phases[1]), (3, 3, phases[2])])
         output, grad_middle, grad_sel, grad_att, et, leaving, sglu = run_units(
             lengths, slopes, matrices, second, cotangent, second_t, cot_t, [middle, sel, attended, qpre],
             angles, out_weight, got[:12], ride, ranges[0][1], depth, ident=2,

time: 258 us -> 236 us (0.915)
  Pallas kernels: 247 us -> 227 us
    pallas_call x3, Pallas kernels: 247 us -> 227 us  [launch(): pl.pallas_call(body, grid=(steps,), in_specs=all_specs, out_specs=all_out...]
where the time goes in v2:
time: 236 us; the launch traced here: 235 us
  Pallas kernels  227 us (96%)
  local copies, waits for them, and re-layouts  6.81 us (3%)
    pallas_call x3, Pallas kernels, launch(): pl.pallas_call(body, grid=(steps,), in_specs=all_specs, out_specs=all_out...  227 us

profile of v2, /device:TPU:12, one launch (start us, length us, event | category | flops | bytes accessed | tf_op | source)
XLA Modules:
  0.0 234.7 jit_solution(15885002534802907024)
XLA Ops:
  0.6 41.4 %forward_to_sglu.1 = (bf16[1024,1024]{1,0:T(8,128)(2,1)}, bf16[1024,1024]{1,0:T(8,128)(2,1)}, bf16[4,8,128,256]{3,2,1,0:T(8,128)(2,1)}, bf16[1024,1024]{1,0:T(8,...) custom-call(s32[1,3]{1,0:T(1,128)} %refs_0_.5, ...), custom_call_target="tpu_custom_call" | custom-call | flops 12884901888 | bytes 62459948 | tf_op jit(solution)/shard_map/forward_to_sglu/pallas_call | solution.py:326
  42.1 114.6 %sglu_and_gradients.1 = (bf16[1024,1024]{1,0:T(8,128)(2,1)}, bf16[1024,1024]{1,0:T(8,128)(2,1)}, bf16[1024,1024]{1,0:T(8,128)(2,1)}, bf16[1024,1024]{1,0:T(8,128...) custom-call(s32[1,3]{1,0:T(1,128)} %refs_0_.5, ...), custom_call_target="tpu_custom_call" | custom-call | flops 53150220288 | bytes 48533548 | tf_op jit(solution)/shard_map/sglu_and_gradients/pallas_call | solution.py:326
  156.7 0.0 copy-start.2
  156.7 71.2 %attention_backward_and_gradients.1 = (bf16[1024,1024]{1,0:T(8,128)(2,1)}, f32[2,64,512]{2,1,0:T(8,128)}, f32[3,64,512]{2,1,0:T(8,128)}) custom-call(s32[1,3]{1,0:T(1,128)} %refs_0_.5, f32[8]{0:T(128)} %refs_1_.5, bf16[1024,1024]{1,0:T(8,128)(2,1)} %get-tuple-element.54.refs_15_.refs_2_, bf16[1024,1024]{1,0:T(8,128)(2,1)} %get-tuple-element.71.refs_3_, ...), custom_call_target="tpu_custom_call" | custom-call | flops 32212254720 | bytes 35524652 | tf_op jit(solution)/shard_map/attention_backward_and_gradients/pallas_call | solution.py:326
  227.9 0.0 copy-start
  227.9 2.1 slice_bitcast_fusion.3
  230.1 0.0 copy-done.2
  230.1 1.0 slice_bitcast_fusion
  231.1 0.0 copy-done
  231.1 0.0 copy-start.1
  231.1 1.3 copy.26
  232.4 1.0 copy-done.1
  233.4 1.3 copy.27
Async XLA Ops:
  156.7 73.4 %copy-start.2 = (f32[3,64,1408]{2,1,0:T(8,128)S(1)}, f32[3,64,1408]{2,1,0:T(8,128)}, u32[]{:S(2)}) copy-start(f32[3,64,1408]{2,1,0:T(8,128)} %get-tuple-element.85) | copy-start | bytes 3244036
  227.9 3.2 %copy-start = (bf16[1024,1024]{1,0:T(8,128)(2,1)S(1)}, bf16[1024,1024]{1,0:T(8,128)(2,1)}, u32[]{:S(2)}) copy-start(bf16[1024,1024]{1,0:T(8,128)(2,1)} %get-tuple-element.107) | copy-start | bytes 6291460
  231.1 2.3 %copy-start.1 = (bf16[1024,1024]{1,0:T(8,128)(2,1)S(1)}, bf16[1024,1024]{1,0:T(8,128)(2,1)}, u32[]{:S(2)}) copy-start(bf16[1024,1024]{1,0:T(8,128)(2,1)} %get-tuple-element.108) | copy-start | bytes 6291460

commit v3 on v2

--- a/solution.py
+++ b/solution.py
@@ -124,13 +124,13 @@
     return index
 
 
-def remote(src, dst, send, recv, axis, mask):
+def remote(src, dst, send, recv, axis, mask, where=None):
     return pltpu.make_async_remote_copy(
         src_ref=src,
         dst_ref=dst,
         send_sem=send,
         recv_sem=recv,
-        device_id={axis: flipped(lax.axis_index(axis), mask)},
+        device_id={axis: flipped(lax.axis_index(axis), mask) if where is None else where},
         device_id_type=pl.DeviceIdType.MESH,
     )
 
@@ -180,7 +180,8 @@
 class Reducer:
     KINDS = 8
 
-    def __init__(self, start, blocks, items, depth, rows, delays, slots, order, over_x):
+    def __init__(self, start, blocks, items, depth, rows, delays, slots, order, over_x, offset=0):
+        self.offset = offset
         self.start, self.blocks, self.items = start, blocks, items
         self.slots, self.order = slots, order
         self.made = 2 if delays[0] else 1
@@ -215,11 +216,23 @@
         self.partners = [("dp", 1), ("dp", 2), ("mp", 1)] + [("dp", 4 * k) for k in range(1, depth)]
         self.last = start + blocks - 1 + delays[3]
 
-    def bind(self, scratch):
+    def bind(self, scratch, places):
         self.refs = scratch
         self.given, self.kept = scratch[:2]
-        self.x = lax.rem(lax.div(lax.axis_index("dp"), 2), 2)
-        self.z = lax.div(lax.axis_index("dp"), 4)
+        self.x, self.z, self.where, self.partner_z = places
+
+    @staticmethod
+    def places(depth):
+        dp, me = lax.axis_index("dp"), lax.axis_index("mp")
+        z = lax.div(dp, 4)
+        x = lax.div(dp - 4 * z, 2)
+        core = dp - 4 * z - 2 * x
+        where = {("dp", 1): dp + 1 - 2 * core, ("dp", 2): dp + 2 - 4 * x, ("mp", 1): 1 - me}
+        partner_z = {}
+        for k in range(1, depth):
+            partner_z[k] = flipped(z, k)
+            where["dp", 4 * k] = dp + 4 * (partner_z[k] - z)
+        return x, z, where, partner_z
 
     def copies(self, stage, j):
         (given, kept, got, ps, pk, pr, qs, qk, qr, ps2, pk2, pr2, qs2, qk2, qr2, line, zr, send, recv) = self.refs
@@ -232,10 +245,13 @@
             plan = [(3, ps2.at[slot], pr2.at[four], "mp", 1), (4, qs2.at[slot], qr2.at[four], "dp", 2)]
         else:
             plan = [
-                (4 + k, line.at[slot, flipped(self.z, k)], zr.at[four, k - 1], "dp", 4 * k)
+                (4 + k, line.at[slot, self.partner_z[k]], zr.at[four, k - 1], "dp", 4 * k)
                 for k in range(1, self.depth)
             ]
-        return [remote(src, dst, send.at[i, j], recv.at[i, j], axis, mask) for i, src, dst, axis, mask in plan]
+        return [
+            remote(src, dst, send.at[i, j], recv.at[i, j], axis, mask, self.where[axis, mask])
+            for i, src, dst, axis, mask in plan
+        ]
 
     def begin(self, j):
         for copy in self.copies(0, j):
@@ -287,7 +303,7 @@
                 line[slot, z, t] = qk2[slot, i] + qr2[four, i]
         else:
             total = plus(line[slot, self.z], *[zr[four, k] for k in range(self.depth - 1)])
-            out[:, :, pl.ds(pl.multiple_of(j * HEAD, HEAD), HEAD)] = total
+            out[:, :, pl.ds(pl.multiple_of((self.offset + j) * HEAD, HEAD), HEAD)] = total
 
 
 def launch(kernel, name, steps, inputs, specs, outs, out_specs, scratch, flops, guests=(), ident=None, partners=()):
@@ -795,7 +811,7 @@
     )
 
 
-def units_kernel(geo, reducer, ride, lengths, slopes, fine, coarse, *refs):
+def units_kernel(geo, reducers, ride, lengths, slopes, fine, coarse, *refs):
     blocks, cut, d, units, chunks = geo["blocks"], geo["cut"], geo["d"], geo["units"], geo["chunks"]
     refs = list(refs)
     take = lambda k: [refs.pop(0) for _ in range(k)]
@@ -805,12 +821,15 @@
     pieces = take(12)
     had_b = take(3)
     rows_out = take(4)
-    (et_o, e0_o, sums_o) = take(3)
+    (et_o, left_o, sums_o) = take(3)
     pieces = pieces + had_b + take(9)
     (term, part, x, cot, xt, cott, o1, o2, od, c12, cd, inner, grads, state, e0, sums) = take(16)
+    (left,) = take(1)
     (tiles, made, ends) = take(3)
     (sems, own_sems, block_sems, tile_sems, made_sems) = take(5)
-    reducer.bind(take(len(reducer.scratch)))
+    places = Reducer.places(reducers[0].depth)
+    for reducer in reducers:
+        reducer.bind(take(len(reducer.scratch)), places)
     step = pl.program_id(0)
     ride.before(step, had_b, pieces[15:], refs)
     core = lax.rem(lax.axis_index("dp"), 2)
@@ -818,13 +837,13 @@
     heads = state.shape[0]
     layout = Layout(lengths, 2, chunks * CHUNK)
 
-    def fetch(g):
+    def fetch(g, parts=slice(0, 8)):
         size = cut if g == 0 else units - cut
         masks = [(0, None, 0), (3, 0, 2), (3, 1, 4), (3, 2, 1), (6, 0, 6), (6, 1, 3), (6, 2, 5), (9, None, 7)]
         copies = []
         for w, region in enumerate((o1, o2, od)):
             rows = d // 8 if w < 2 else size // 8
-            for k, (at, inner, mask) in enumerate(masks):
+            for k, (at, inner, mask) in list(enumerate(masks))[parts]:
                 src = pieces[12 * g + at + w]
                 src = src if inner is None else src.at[inner]
                 here = pl.ds(pl.multiple_of(flipped(eighth, mask) * rows, 16), rows)
@@ -842,7 +861,8 @@
     ]
     out_weight = pltpu.make_async_copy(wo_h, xt, own_sems.at[7])
     saved = pltpu.make_async_copy(sums, sums_o, own_sems.at[5])
-    leaving = pltpu.make_async_copy(e0, e0_o, own_sems.at[8])
+    arrived = pltpu.make_async_copy(left, left_o, own_sems.at[8])
+    exchange = remote(e0, left, own_sems.at[9], own_sems.at[10], "mp", 1)
 
     def own_block(j):
         slot, here = lax.rem(j, 2), pl.ds(pl.multiple_of(j * HEAD, HEAD), HEAD)
@@ -885,6 +905,8 @@
 
     @pl.when(step == turn)
     def _():
+        for copy in fetch(1, slice(7, 8)):
+            copy.start()
         for copy in fetch(1):
             copy.wait()
 
@@ -906,12 +928,12 @@
 
     @pl.when(step == turn - 1)
     def _():
-        for copy in fetch(1):
+        for copy in fetch(1, slice(0, 7)):
             copy.start()
 
     @pl.when(step == 0)
     def _():
-        for copy in own:
+        for copy in own[:2]:
             copy.wait()
 
     @pl.when(step < blocks)
@@ -925,16 +947,26 @@
             inner[here, :] = (left * right).astype(BF16)
             grads[here, :wide] = (upstream * right).astype(BF16)
             grads[here, wide:] = (upstream * left).astype(BF16)
-        slot = 0
-        both = nn(xt[...], grads[...]).astype(BF16)
-        down = nn(cott[...], inner[...]).astype(BF16)
-        for k, buffer in enumerate((reducer.given, reducer.kept)):
-            here = slice(k * (d // 2), (k + 1) * (d // 2))
-            buffer[slot, 0] = both[here, :wide]
-            buffer[slot, 1] = both[here, wide:]
-            buffer[slot, 2] = down[here, :]
-            if k == 0:
-                reducer.begin(step)
+
+        @pl.when(step == 0)
+        def _():
+            for copy in own[2:]:
+                copy.wait()
+
+        for reducer in reducers:
+
+            @pl.when(jnp.logical_and(step >= reducer.start, step < reducer.start + reducer.blocks))
+            def _(reducer=reducer):
+                both = nn(xt[...], grads[...]).astype(BF16)
+                down = nn(cott[...], inner[...]).astype(BF16)
+                for k, buffer in enumerate((reducer.given, reducer.kept)):
+                    here = slice(k * (d // 2), (k + 1) * (d // 2))
+                    buffer[0, 0] = both[here, :wide]
+                    buffer[0, 1] = both[here, wide:]
+                    buffer[0, 2] = down[here, :]
+                    if k == 0:
+                        reducer.begin(step - reducer.start)
+
         term[...] += nn(inner[...], cd[at])
         part[...] += nt(grads[...], c12[at])
 
@@ -978,18 +1010,21 @@
     @pl.when(step == blocks + chunks - 1)
     def _():
         e0[...] = state[...].astype(BF16)
-        leaving.start()
+        exchange.start()
 
     ride.after(step, had_b, pieces[15:], refs)
-    reducer.run(step, sums)
-
-    @pl.when(step == reducer.last)
+    for reducer in reducers:
+        reducer.run(step, sums)
+
+    @pl.when(step == reducers[-1].last)
     def _():
         saved.start()
+        exchange.wait()
+        arrived.start()
         for i in range(chunks - 2, chunks):
             for copy in results(i):
                 copy.wait()
-        leaving.wait()
+        arrived.wait()
         saved.wait()
 
 
@@ -999,15 +1034,19 @@
     units = matrices[0].shape[1]
     blocks = units // HEAD
     rows = d // (4 * depth)
-    reducer = Reducer(0, blocks, 3, depth, rows, (0, 2, 4, 6), 2, (4, 3, 2, 1), (1, 1, 2))
+    turn = cut // HEAD
+    reducers = [
+        Reducer(0, turn, 3, depth, rows, (0, 2, 4, 6), 2, (4, 3, 2, 1), (1, 1, 1)),
+        Reducer(turn, blocks - turn, 3, depth, rows, (0, 2, 4, 6), 2, (4, 3, 2, 1), (2, 2, 2), turn),
+    ]
     geo = dict(blocks=blocks, cut=cut, d=d, units=units, chunks=chunks)
     turned = pltpu.VMEM((d, n), BF16)
     size = max(cut, units - cut)
     sums = (3, rows, units)
     return launch(
-        functools.partial(units_kernel, geo, reducer, ride),
+        functools.partial(units_kernel, geo, reducers, ride),
         "sglu_and_gradients",
-        max(reducer.last, blocks + chunks - 1) + 1,
+        max(reducers[-1].last, blocks + chunks - 1) + 1,
         [lengths, slopes, *angles]
         + list(matrices)
         + [second, cot, second_t, cot_t, wo]
@@ -1036,19 +1075,20 @@
             pltpu.VMEM(state_shape(d), F32),
             pltpu.VMEM(state_shape(d), BF16),
             pltpu.VMEM(sums, F32),
+            pltpu.VMEM(state_shape(d), BF16),
             pltpu.VMEM((2, 4, CHUNK, d), BF16),
             pltpu.VMEM((2, 4, CHUNK, d), BF16),
             pltpu.VMEM((2,) + state_shape(d), BF16),
             pltpu.SemaphoreType.DMA((2, 3, 8)),
-            pltpu.SemaphoreType.DMA((9,)),
+            pltpu.SemaphoreType.DMA((11,)),
             pltpu.SemaphoreType.DMA((2, 3)),
             pltpu.SemaphoreType.DMA((2, 4)),
             pltpu.SemaphoreType.DMA((2, 5)),
         ]
-        + reducer.scratch
+        + [a for reducer in reducers for a in reducer.scratch]
         + ride.scratch,
         36 * n * d * units,
-        partners=reducer.partners + ride.partners,
+        partners=reducers[0].partners + ride.partners,
         ident=ident,
     )[:7]
 
@@ -1215,13 +1255,14 @@
     refs = list(refs)
     take = lambda k: [refs.pop(0) for _ in range(k)]
     arrays_h = take(6)
-    (came_h, leaving, fine, coarse, gsel_h, hid_h, gmid_h, mixt_h, normt_h) = take(9)
+    (came_h, left_h, fine, coarse, gsel_h, hid_h, gmid_h, mixt_h, normt_h) = take(9)
     weights_h = take(4)
     hidden_o, out, out2 = take(3)
     (qpre, kpre, val, gatt, st, et, came, gsel, gmid) = take(9)
-    grads, block, decays, mixt, normt, left, sems, late_sems, state_sems = take(9)
-    outer.bind(take(len(outer.scratch)))
-    inner.bind(refs)
+    grads, block, decays, mixt, normt, left, sems, late_sems = take(8)
+    places = Reducer.places(outer.depth)
+    outer.bind(take(len(outer.scratch)), places)
+    inner.bind(refs, places)
     step = pl.program_id(0)
     core = lax.rem(lax.axis_index("dp"), 2)
     me = lax.axis_index("mp")
@@ -1236,9 +1277,9 @@
     ]
     more = [
         pltpu.make_async_copy(src, dst, sems.at[6 + i])
-        for i, (src, dst) in enumerate(zip(arrays_h + [came_h], (qpre, kpre, val, gatt, st, et, came)))
+        for i, (src, dst) in enumerate(zip(arrays_h + [came_h, left_h], (qpre, kpre, val, gatt, st, et, came, left)))
     ]
-    select = pltpu.make_async_copy(weights_h[3], mixt, sems.at[13])
+    select = pltpu.make_async_copy(weights_h[3], mixt, sems.at[14])
 
     def replaced(j):
         copies = []
@@ -1248,21 +1289,11 @@
                 copies.append(pltpu.make_async_copy(src.at[:, cols], dst.at[:, cols], late_sems.at[j, side, i]))
         return copies
 
-    def exchange(j):
-        pair = []
-        for k in range(2):
-            h = k * blocks + j
-            pair.append(remote(leaving.at[h], left.at[h], state_sems.at[0, h], state_sems.at[1, h], "mp", 1))
-        return pair
-
     @pl.when(step == 0)
     def _():
-        for j in range(blocks):
-            for copy in exchange(j):
-                copy.start()
         for copy in loads + more:
             copy.start()
-        for copy in loads:
+        for copy in loads[:3]:
             copy.wait()
 
     @pl.when(step < blocks)
@@ -1271,8 +1302,15 @@
         mine = pl.ds(pl.multiple_of((me * blocks + step) * HEAD, HEAD), HEAD)
         theirs = pl.ds(pl.multiple_of(((1 - me) * blocks + step) * HEAD, HEAD), HEAD)
         gb = jnp.concatenate([gmid[:, mine], gmid[:, theirs]], axis=1)
+        first = nn(mixt[...], gb).astype(BF16)
+
+        @pl.when(step == 0)
+        def _():
+            for copy in loads[3:]:
+                copy.wait()
+
         gs = jnp.concatenate([gsel[:, mine], gsel[:, theirs]], axis=1)
-        made = [nn(mixt[...], gb).astype(BF16), nn(normt[...], gs).astype(BF16)]
+        made = [first, nn(normt[...], gs).astype(BF16)]
         for k, buffer in enumerate((outer.given, outer.kept)):
             for i in range(2):
                 buffer[slot, i] = made[i][k * (d // 2) : (k + 1) * (d // 2), :]
@@ -1282,8 +1320,6 @@
     @pl.when(jnp.logical_and(step >= blocks, step < 2 * blocks))
     def _():
         j = step - blocks
-        for copy in exchange(j):
-            copy.wait()
         for side in range(2):
             slope = slopes[(me if side == 0 else 1 - me) * blocks + j]
             for k in range(2):
@@ -1348,7 +1384,7 @@
     inner.run(step, out2)
 
 
-def run_projections(lengths, slopes, qpre, kpre, values, gatt, st, et, came, leaving, angles, gsel, hidden, gmid, mixed_t, normed_t, weights, depth, ident):
+def run_projections(lengths, slopes, qpre, kpre, values, gatt, st, et, came, left, angles, gsel, hidden, gmid, mixed_t, normed_t, weights, depth, ident):
     n, d = qpre.shape
     heads, chunks = d // HEAD, n // CHUNK
     blocks = heads // 2
@@ -1366,7 +1402,7 @@
         functools.partial(projections_kernel, geo, outer, inner),
         "attention_backward_and_gradients",
         steps,
-        [lengths, slopes, qpre, kpre, values, gatt, st, et, came, leaving, *angles]
+        [lengths, slopes, qpre, kpre, values, gatt, st, et, came, left, *angles]
         + [gsel, hidden, gmid, mixed_t, normed_t]
         + list(weights),
         [smem(), smem()] + [anywhere()] * 8 + [once(a.shape) for a in angles] + [anywhere()] * 9,
@@ -1385,9 +1421,8 @@
             turned,
             turned,
             one,
-            pltpu.SemaphoreType.DMA((14,)),
+            pltpu.SemaphoreType.DMA((15,)),
             pltpu.SemaphoreType.DMA((blocks, 2, 4)),
-            pltpu.SemaphoreType.DMA((2, heads)),
         ]
         + outer.scratch
         + inner.scratch,
@@ -1554,8 +1589,8 @@
     if riding:
         had_b = got[12:15]
         more, phases = onward(lambda w: lambda i, o: i[w], had_b, 0, True)
-        ride = Carry(had_b, more, [(0, 1, phases[0]), (2, 2, phases[1]), (3, 3, phases[2])])
-        output, grad_middle, grad_sel, grad_att, et, leaving, sglu = run_units(
+        ride = Carry(had_b, more, [(0, 1, phases[0]), (2, 3, phases[1]), (4, 4, phases[2])])
+        output, grad_middle, grad_sel, grad_att, et, left, sglu = run_units(
             lengths, slopes, matrices, second, cotangent, second_t, cot_t, [middle, sel, attended, qpre],
             angles, out_weight, got[:12], ride, ranges[0][1], depth, ident=2,
         )
@@ -1570,7 +1605,7 @@
     inputs_weights = [query_weight, key_weight, value_weight, select_weight]
     if riding:
         grad_hidden, out_sel, inputs = run_projections(
-            lengths, slopes, qpre, kpre, values, grad_att, st, et, came, leaving, angles, grad_sel,
+            lengths, slopes, qpre, kpre, values, grad_att, st, et, came, left, angles, grad_sel,
             hidden_in, grad_middle, mixed_t, normed_t, inputs_weights, depth, ident=3,
         )
     else:

time: 236 us -> 233 us (0.987)
  Pallas kernels: 227 us -> 222 us
    pallas_call x3, Pallas kernels: 227 us -> 222 us  [launch(): pl.pallas_call(body, grid=(steps,), in_specs=all_specs, out_specs=all_out...]
where the time goes in v3:
time: 233 us; the launch traced here: 230 us
  Pallas kernels  222 us (95%)
  local copies, waits for them, and re-layouts  6.81 us (3%)
    pallas_call x3, Pallas kernels, launch(): pl.pallas_call(body, grid=(steps,), in_specs=all_specs, out_specs=all_out...  222 us

profile of v3, /device:TPU:12, one launch (start us, length us, event | category | flops | bytes accessed | tf_op | source)
XLA Modules:
  0.0 229.5 jit_solution(822432180846680742)
XLA Ops:
  0.6 41.4 %forward_to_sglu.1 = (bf16[1024,1024]{1,0:T(8,128)(2,1)}, bf16[1024,1024]{1,0:T(8,128)(2,1)}, bf16[4,8,128,256]{3,2,1,0:T(8,128)(2,1)}, bf16[1024,1024]{1,0:T(8,...) custom-call(s32[1,3]{1,0:T(1,128)} %refs_0_.5, ...), custom_call_target="tpu_custom_call" | custom-call | flops 12884901888 | bytes 62459948 | tf_op jit(solution)/shard_map/forward_to_sglu/pallas_call | solution.py:342
  42.1 109.9 %sglu_and_gradients.1 = (bf16[1024,1024]{1,0:T(8,128)(2,1)}, bf16[1024,1024]{1,0:T(8,128)(2,1)}, bf16[1024,1024]{1,0:T(8,128)(2,1)}, bf16[1024,1024]{1,0:T(8,128...) custom-call(s32[1,3]{1,0:T(1,128)} %refs_0_.5, ...), custom_call_target="tpu_custom_call" | custom-call | flops 53150220288 | bytes 48533548 | tf_op jit(solution)/shard_map/sglu_and_gradients/pallas_call | solution.py:342
  152.0 0.0 copy-start.2
  152.0 70.7 %attention_backward_and_gradients.1 = (bf16[1024,1024]{1,0:T(8,128)(2,1)}, f32[2,64,512]{2,1,0:T(8,128)}, f32[3,64,512]{2,1,0:T(8,128)}) custom-call(s32[1,3]{1,0:T(1,128)} %refs_0_.5, f32[8]{0:T(128)} %refs_1_.5, bf16[1024,1024]{1,0:T(8,128)(2,1)} %get-tuple-element.54.refs_15_.refs_2_, bf16[1024,1024]{1,0:T(8,128)(2,1)} %get-tuple-element.71.refs_3_, ...), custom_call_target="tpu_custom_call" | custom-call | flops 32212254720 | bytes 35524652 | tf_op jit(solution)/shard_map/attention_backward_and_gradients/pallas_call | solution.py:342
  222.7 0.0 copy-start
  222.7 2.1 slice_bitcast_fusion.3
  224.9 0.0 copy-done.2
  224.9 1.0 slice_bitcast_fusion
  225.9 0.0 copy-done
  225.9 0.0 copy-start.1
  225.9 1.3 copy.26
  227.2 1.0 copy-done.1
  228.2 1.3 copy.27
Async XLA Ops:
  152.0 72.8 %copy-start.2 = (f32[3,64,1408]{2,1,0:T(8,128)S(1)}, f32[3,64,1408]{2,1,0:T(8,128)}, u32[]{:S(2)}) copy-start(f32[3,64,1408]{2,1,0:T(8,128)} %get-tuple-element.85) | copy-start | bytes 3244036
  222.7 3.2 %copy-start = (bf16[1024,1024]{1,0:T(8,128)(2,1)S(1)}, bf16[1024,1024]{1,0:T(8,128)(2,1)}, u32[]{:S(2)}) copy-start(bf16[1024,1024]{1,0:T(8,128)(2,1)} %get-tuple-element.107) | copy-start | bytes 6291460
  225.9 2.3 %copy-start.1 = (bf16[1024,1024]{1,0:T(8,128)(2,1)S(1)}, bf16[1024,1024]{1,0:T(8,128)(2,1)}, u32[]{:S(2)}) copy-start(bf16[1024,1024]{1,0:T(8,128)(2,1)} %get-tuple-element.108) | copy-start | bytes 6291460

commit v4 on v3

--- a/solution.py
+++ b/solution.py
@@ -56,6 +56,14 @@
     rows = turned.shape[0] // parts
     for i in range(parts):
         ref[i % 2, (i // 2) * rows : (i // 2 + 1) * rows, :] = turned[i * rows : (i + 1) * rows, :]
+
+
+def put_turned_at(ref, value, parts, cols):
+    turned = value.T
+    half, rows = turned.shape[0] // 2, turned.shape[0] // parts
+    for i in range(parts):
+        at = (i % 2) * half + (i // 2) * rows
+        ref[at : at + rows, cols] = turned[i * rows : (i + 1) * rows, :]
 
 
 def feature_slice(h):
@@ -436,16 +444,12 @@
         total[:, head_slice(h)] = (att(h) + fade * nt(query(h), came[h])) * alive
 
 
-def mix_chunk(parts, total, sel, wo, hid, att_o, mixt_o, mid_o, sec_o, sect_o):
+def mix_chunk(total, sel, wo, hid, put):
     attended = total[...]
-    att_o[...] = attended.astype(BF16)
     mixed = (attended * scale_of(attended) * sel.astype(F32)).astype(BF16)
-    put_turned(mixt_o, mixed, parts)
-    middle = hid[...].astype(F32) + nn(mixed, wo)
-    mid_o[...] = middle.astype(BF16)
+    middle = hid.astype(F32) + nn(mixed, wo)
     second = (middle * scale_of(middle)).astype(BF16)
-    sec_o[...] = second
-    put_turned(sect_o, second, parts)
+    put(attended.astype(BF16), mixed, middle.astype(BF16), second)
 
 
 def state_shape(d):
@@ -560,7 +564,15 @@
         came,
         total,
     )
-    mix_chunk(parts, total, sel[...], wo[...], hid, att_o, mixt_o, mid_o, sec_o, sect_o)
+
+    def put(attended, mixed, middle, second):
+        att_o[...] = attended
+        put_turned(mixt_o, mixed, parts)
+        mid_o[...] = middle
+        sec_o[...] = second
+        put_turned(sect_o, second, parts)
+
+    mix_chunk(total, sel[...], wo[...], hid[...], put)
     put_turned(cott_o, cot[...], parts)
 
 
@@ -584,14 +596,16 @@
     )
 
 
-def forward_kernel(chunks, parts, lengths, slopes, hid, cot, fine, coarse, *refs):
+def forward_kernel(chunks, parts, lengths, slopes, fine, coarse, *refs):
     refs = list(refs)
     take = lambda k: [refs.pop(0) for _ in range(k)]
+    hid_h, cot_h = take(2)
     weights_h = take(5)
     (kpre_o, val_o, st_o, qpre_o, sel_o) = take(5)
     (turned_o, att_o, mixt_o, mid_o, sec_o, sect_o, cott_o, came_o) = take(8)
     (weights, normed, kpre, val, st, qpre, sel, att, state, final, came, total, keyed, asked, table) = take(15)
-    (load_sems, out_sems, state_sems) = take(3)
+    (hid, cot, normt, cott) = take(4)
+    (load_sems, out_sems, state_sems, chunk_sems) = take(4)
     heads = state.shape[0]
     step = pl.program_id(0)
     c = lax.rem(step, chunks)
@@ -603,20 +617,48 @@
         for i, (src, dst) in enumerate([(kpre, kpre_o), (val, val_o), (st, st_o), (qpre, qpre_o), (sel, sel_o)])
     ]
     exchange = remote(final, came, state_sems.at[0], state_sems.at[1], "mp", 1)
+    d = hid.shape[1]
+    half = d // 2
+    rows_in = [
+        pltpu.make_async_copy(hid_h, hid, load_sems.at[5]),
+        pltpu.make_async_copy(cot_h, cot, load_sems.at[6]),
+    ]
+
+    def both_halves(src, dst, at):
+        return [
+            pltpu.make_async_copy(src.at[pl.ds(k * half, half), :], dst.at[k], out_sems.at[at + k]) for k in range(2)
+        ]
+
+    turned = both_halves(normt, turned_o, 5)
+    turned_cot = both_halves(cott, cott_o, 7)
+    arrived = pltpu.make_async_copy(came, came_o, out_sems.at[9])
+
+    def finished(c):
+        here = pl.ds(pl.multiple_of(c * CHUNK, CHUNK), CHUNK)
+        copies = [
+            pltpu.make_async_copy(src.at[here, :], dst.at[here, :], chunk_sems.at[c, i])
+            for i, (src, dst) in enumerate([(kpre, att_o), (val, mid_o), (normed, sec_o)])
+        ]
+        for i, dst in enumerate((mixt_o, sect_o)):
+            cols = pl.ds(pl.multiple_of(i * d + c * CHUNK, CHUNK), CHUNK)
+            for k in range(2):
+                src = keyed.at[pl.ds(k * half, half), cols]
+                copies.append(pltpu.make_async_copy(src, dst.at[k, :, here], chunk_sems.at[c, 3 + 2 * i + k]))
+        return copies
 
     @pl.when(step == 0)
     def _():
-        for copy in loads:
+        for copy in rows_in[:1] + loads + rows_in[1:]:
             copy.start()
         state[...] = jnp.zeros_like(state)
-        for copy in loads[:2]:
+        for copy in rows_in[:1] + loads[:2]:
             copy.wait()
 
     @pl.when(step < chunks)
     def _():
-        x = normed_of(hid)
+        x = normed_of(hid.at[here, :])
         normed[here, :] = x
-        put_turned(turned_o, x, parts)
+        put_turned_at(normt, x, parts, here)
         keys = nn(x, weights[0])
         kpre[here, :] = keys.astype(BF16)
         values = nn(x, weights[1])
@@ -637,14 +679,14 @@
     def _():
         final[...] = state[...].astype(BF16)
         exchange.start()
-        for copy in saves[:3]:
+        for copy in saves[:3] + turned:
             copy.start()
 
     @pl.when(step == chunks)
     def _():
         for h in range(heads):
             table[h] = decay_table(slopes[h], False)
-        for copy in loads[2:4]:
+        for copy in loads[2:4] + rows_in[1:]:
             copy.wait()
 
     @pl.when(jnp.logical_and(step >= chunks, step < 2 * chunks))
@@ -673,18 +715,20 @@
             lambda h: table[h],
             put,
         )
-        put_turned(cott_o, cot[...], parts)
+        put_turned_at(cott, cot[here, :], parts, here)
 
     @pl.when(step == 2 * chunks - 1)
     def _():
-        for copy in saves[3:]:
+        for copy in saves[3:] + turned_cot:
             copy.start()
+        for copy in saves[:3]:
+            copy.wait()
 
     @pl.when(step == 2 * chunks)
     def _():
         loads[4].wait()
         exchange.wait()
-        came_o[...] = came[...]
+        arrived.start()
 
     @pl.when(step >= 2 * chunks)
     def _():
@@ -698,43 +742,42 @@
             came,
             total,
         )
-        mix_chunk(parts, total, sel[here, :], weights[4], hid, att_o, mixt_o, mid_o, sec_o, sect_o)
+
+        def put(attended, mixed, middle, second):
+            kpre[here, :] = attended
+            val[here, :] = middle
+            normed[here, :] = second
+            put_turned_at(keyed, mixed, parts, here)
+            put_turned_at(keyed, second, parts, pl.ds(pl.multiple_of(d + c * CHUNK, CHUNK), CHUNK))
+
+        mix_chunk(total, sel[here, :], weights[4], hid[here, :], put)
+        for copy in finished(c):
+            copy.start()
 
     @pl.when(step == 3 * chunks - 1)
     def _():
-        for copy in saves:
+        for copy in saves[3:] + turned + turned_cot + [arrived]:
             copy.wait()
+        for i in range(chunks):
+            for copy in finished(i):
+                copy.wait()
 
 
 def run_forward(lengths, slopes, hidden, cot, weights, angles, parts, guests, ident):
     n, d = hidden.shape
     chunks = n // CHUNK
     turned = turned_shape(d, n)
-    late = lambda s: jnp.maximum(s - 2 * chunks, 0)
-    mid = lambda s: jnp.clip(s - chunks, 0, chunks - 1)
-    early = lambda s: jnp.minimum(s, chunks - 1)
-    tile = pl.BlockSpec((CHUNK, d), lambda s: (late(s), 0))
-    turned_tile = lambda at: pl.BlockSpec(turned[:2] + (CHUNK,), lambda s: (0, 0, at(s)))
     whole = pltpu.VMEM((n, d), BF16)
     return launch(
         functools.partial(forward_kernel, chunks, parts),
         "forward_to_sglu",
         3 * chunks,
-        [lengths, slopes, hidden, cot, *angles, *weights],
-        [
-            smem(),
-            smem(),
-            pl.BlockSpec((CHUNK, d), lambda s: (jnp.where(s < 2 * chunks, early(s), late(s)), 0)),
-            pl.BlockSpec((CHUNK, d), lambda s: (mid(s), 0)),
-        ]
-        + [whole_block(a.shape) for a in angles]
-        + [anywhere()] * 5,
+        [lengths, slopes, *angles, hidden, cot, *weights],
+        [smem(), smem()] + [once(a.shape) for a in angles] + [anywhere()] * 7,
         [struct((n, d)), struct((n, d)), struct((chunks,) + state_shape(d)), struct((n, d)), struct((n, d))]
         + [struct(turned), struct((n, d)), struct(turned), struct((n, d)), struct((n, d)), struct(turned), struct(turned)]
         + [struct(state_shape(d))],
-        [anywhere()] * 5
-        + [turned_tile(early), tile, turned_tile(late), tile, tile, turned_tile(late), turned_tile(mid)]
-        + [whole_block(state_shape(d))],
+        [anywhere()] * 13,
         [
             pltpu.VMEM((5, d, d), BF16),
             whole,
@@ -751,9 +794,14 @@
             pltpu.VMEM((n, 2 * d), BF16),
             pltpu.VMEM((n, 2 * d), BF16),
             pltpu.VMEM((d // HEAD, CHUNK, CHUNK), F32),
-            pltpu.SemaphoreType.DMA((5,)),
-            pltpu.SemaphoreType.DMA((5,)),
+            whole,
+            whole,
+            pltpu.VMEM((d, n), BF16),
+            pltpu.VMEM((d, n), BF16),
+            pltpu.SemaphoreType.DMA((7,)),
+            pltpu.SemaphoreType.DMA((10,)),
             pltpu.SemaphoreType.DMA((2,)),
+            pltpu.SemaphoreType.DMA((chunks, 7)),
         ],
         12 * n * d * d,
         guests=guests,

time: 233 us -> 230 us (0.987)
  no operation moved by 1% of the time
where the time goes in v4:
time: 230 us; the launch traced here: 227 us
  Pallas kernels  220 us (96%)
  local copies, waits for them, and re-layouts  6.81 us (3%)
    pallas_call x3, Pallas kernels, launch(): pl.pallas_call(body, grid=(steps,), in_specs=all_specs, out_specs=all_out...  220 us

profile of v4, /device:TPU:12, one launch (start us, length us, event | category | flops | bytes accessed | tf_op | source)
XLA Modules:
  0.0 227.4 jit_solution(5738652372876448200)
XLA Ops:
  0.6 39.3 %forward_to_sglu.1 = (bf16[1024,1024]{1,0:T(8,128)(2,1)}, bf16[1024,1024]{1,0:T(8,128)(2,1)}, bf16[4,8,128,256]{3,2,1,0:T(8,128)(2,1)}, bf16[1024,1024]{1,0:T(8,...) custom-call(s32[1,3]{1,0:T(1,128)} %refs_0_.5, ...), custom_call_target="tpu_custom_call" | custom-call | flops 12884901888 | bytes 62459948 | tf_op jit(solution)/shard_map/forward_to_sglu/pallas_call | solution.py:350
  39.9 110.0 %sglu_and_gradients.1 = (bf16[1024,1024]{1,0:T(8,128)(2,1)}, bf16[1024,1024]{1,0:T(8,128)(2,1)}, bf16[1024,1024]{1,0:T(8,128)(2,1)}, bf16[1024,1024]{1,0:T(8,128...) custom-call(s32[1,3]{1,0:T(1,128)} %refs_0_.5, ...), custom_call_target="tpu_custom_call" | custom-call | flops 53150220288 | bytes 48533548 | tf_op jit(solution)/shard_map/sglu_and_gradients/pallas_call | solution.py:350
  149.9 0.0 copy-start.2
  149.9 70.6 %attention_backward_and_gradients.1 = (bf16[1024,1024]{1,0:T(8,128)(2,1)}, f32[2,64,512]{2,1,0:T(8,128)}, f32[3,64,512]{2,1,0:T(8,128)}) custom-call(s32[1,3]{1,0:T(1,128)} %refs_0_.5, f32[8]{0:T(128)} %refs_1_.5, bf16[1024,1024]{1,0:T(8,128)(2,1)} %get-tuple-element.54.refs_15_.refs_2_, bf16[1024,1024]{1,0:T(8,128)(2,1)} %get-tuple-element.71.refs_3_, ...), custom_call_target="tpu_custom_call" | custom-call | flops 32212254720 | bytes 35524652 | tf_op jit(solution)/shard_map/attention_backward_and_gradients/pallas_call | solution.py:350
  220.5 0.0 copy-start
  220.5 2.1 slice_bitcast_fusion.3
  222.7 0.0 copy-done.2
  222.7 1.0 slice_bitcast_fusion
  223.7 0.0 copy-done
  223.7 0.0 copy-start.1
  223.7 1.3 copy.26
  225.0 1.0 copy-done.1
  226.0 1.3 copy.27
Async XLA Ops:
  149.9 72.8 %copy-start.2 = (f32[3,64,1408]{2,1,0:T(8,128)S(1)}, f32[3,64,1408]{2,1,0:T(8,128)}, u32[]{:S(2)}) copy-start(f32[3,64,1408]{2,1,0:T(8,128)} %get-tuple-element.85) | copy-start | bytes 3244036
  220.5 3.2 %copy-start = (bf16[1024,1024]{1,0:T(8,128)(2,1)S(1)}, bf16[1024,1024]{1,0:T(8,128)(2,1)}, u32[]{:S(2)}) copy-start(bf16[1024,1024]{1,0:T(8,128)(2,1)} %get-tuple-element.107) | copy-start | bytes 6291460
  223.7 2.3 %copy-start.1 = (bf16[1024,1024]{1,0:T(8,128)(2,1)S(1)}, bf16[1024,1024]{1,0:T(8,128)(2,1)}, u32[]{:S(2)}) copy-start(bf16[1024,1024]{1,0:T(8,128)(2,1)} %get-tuple-element.108) | copy-start | bytes 6291460

commit v5 on v4

--- a/solution.py
+++ b/solution.py
@@ -648,11 +648,13 @@
 
     @pl.when(step == 0)
     def _():
-        for copy in rows_in[:1] + loads + rows_in[1:]:
+        for copy in rows_in[:1] + loads[:2]:
             copy.start()
         state[...] = jnp.zeros_like(state)
         for copy in rows_in[:1] + loads[:2]:
             copy.wait()
+        for copy in loads[2:] + rows_in[1:]:
+            copy.start()
 
     @pl.when(step < chunks)
     def _():
@@ -943,7 +945,7 @@
 
     @pl.when(step == 0)
     def _():
-        for copy in own_block(0) + fetch(0) + own:
+        for copy in own_block(0) + fetch(0) + own[:2]:
             copy.start()
         term[...] = jnp.zeros_like(term)
         part[...] = jnp.zeros_like(part)
@@ -983,6 +985,8 @@
     def _():
         for copy in own[:2]:
             copy.wait()
+        for copy in own[2:]:
+            copy.start()
 
     @pl.when(step < blocks)
     def _():
@@ -1339,7 +1343,7 @@
 
     @pl.when(step == 0)
     def _():
-        for copy in loads + more:
+        for copy in loads:
             copy.start()
         for copy in loads[:3]:
             copy.wait()
@@ -1356,6 +1360,8 @@
         def _():
             for copy in loads[3:]:
                 copy.wait()
+            for copy in more:
+                copy.start()
 
         gs = jnp.concatenate([gsel[:, mine], gsel[:, theirs]], axis=1)
         made = [first, nn(normt[...], gs).astype(BF16)]

time: 230 us -> 230 us (level)
  no operation moved by 1% of the time
where the time goes in v5:
time: 230 us; the launch traced here: 227 us
  Pallas kernels  219 us (95%)
  local copies, waits for them, and re-layouts  6.81 us (3%)
    pallas_call x3, Pallas kernels, launch(): pl.pallas_call(body, grid=(steps,), in_specs=all_specs, out_specs=all_out...  219 us

profile of v5, /device:TPU:12, one launch (start us, length us, event | category | flops | bytes accessed | tf_op | source)
XLA Modules:
  0.0 226.8 jit_solution(8144857754699833427)
XLA Ops:
  0.6 39.3 %forward_to_sglu.1 = (bf16[1024,1024]{1,0:T(8,128)(2,1)}, bf16[1024,1024]{1,0:T(8,128)(2,1)}, bf16[4,8,128,256]{3,2,1,0:T(8,128)(2,1)}, bf16[1024,1024]{1,0:T(8,...) custom-call(s32[1,3]{1,0:T(1,128)} %refs_0_.5, ...), custom_call_target="tpu_custom_call" | custom-call | flops 12884901888 | bytes 62459948 | tf_op jit(solution)/shard_map/forward_to_sglu/pallas_call | solution.py:350
  39.9 109.5 %sglu_and_gradients.1 = (bf16[1024,1024]{1,0:T(8,128)(2,1)}, bf16[1024,1024]{1,0:T(8,128)(2,1)}, bf16[1024,1024]{1,0:T(8,128)(2,1)}, bf16[1024,1024]{1,0:T(8,128...) custom-call(s32[1,3]{1,0:T(1,128)} %refs_0_.5, ...), custom_call_target="tpu_custom_call" | custom-call | flops 53150220288 | bytes 48533548 | tf_op jit(solution)/shard_map/sglu_and_gradients/pallas_call | solution.py:350
  149.5 0.0 copy-start.2
  149.5 70.5 %attention_backward_and_gradients.1 = (bf16[1024,1024]{1,0:T(8,128)(2,1)}, f32[2,64,512]{2,1,0:T(8,128)}, f32[3,64,512]{2,1,0:T(8,128)}) custom-call(s32[1,3]{1,0:T(1,128)} %refs_0_.5, f32[8]{0:T(128)} %refs_1_.5, bf16[1024,1024]{1,0:T(8,128)(2,1)} %get-tuple-element.54.refs_15_.refs_2_, bf16[1024,1024]{1,0:T(8,128)(2,1)} %get-tuple-element.71.refs_3_, ...), custom_call_target="tpu_custom_call" | custom-call | flops 32212254720 | bytes 35524652 | tf_op jit(solution)/shard_map/attention_backward_and_gradients/pallas_call | solution.py:350
  220.0 0.0 copy-start
  220.0 2.1 slice_bitcast_fusion.3
  222.1 0.0 copy-done.2
  222.1 1.0 slice_bitcast_fusion
  223.1 0.0 copy-done
  223.1 0.0 copy-start.1
  223.1 1.3 copy.26
  224.4 1.0 copy-done.1
  225.5 1.3 copy.27
Async XLA Ops:
  149.5 72.6 %copy-start.2 = (f32[3,64,1408]{2,1,0:T(8,128)S(1)}, f32[3,64,1408]{2,1,0:T(8,128)}, u32[]{:S(2)}) copy-start(f32[3,64,1408]{2,1,0:T(8,128)} %get-tuple-element.85) | copy-start | bytes 3244036
  220.0 3.2 %copy-start = (bf16[1024,1024]{1,0:T(8,128)(2,1)S(1)}, bf16[1024,1024]{1,0:T(8,128)(2,1)}, u32[]{:S(2)}) copy-start(bf16[1024,1024]{1,0:T(8,128)(2,1)} %get-tuple-element.107) | copy-start | bytes 6291460
  223.1 2.3 %copy-start.1 = (bf16[1024,1024]{1,0:T(8,128)(2,1)S(1)}, bf16[1024,1024]{1,0:T(8,128)(2,1)}, u32[]{:S(2)}) copy-start(bf16[1024,1024]{1,0:T(8,128)(2,1)} %get-tuple-element.108) | copy-start | bytes 6291460
